TPU v7x, 128 devices: a whole 4x4x4 slice. The times are simulated.
128 devices in a mesh: dp: 2 (over y_hi), fsdp: 16 (over z, x), tensor: 4 (over y_lo, core).
Axes of the slice: x: 4, y: 4 (y_hi: 2, y_lo: 2; y = y_hi * 2 + y_lo), z: 4, core: 2. Of those that a mesh axis runs over, the one named last changes fastest.
Arguments:
- activations: bfloat16 [512, 8192], P('dp', 'fsdp'), may hold values from -6 to 6
- frozen_weight: bfloat16 [8192, 28672], P('fsdp', 'tensor'), may hold values from -0.0625 to 0.0625
- cayley_params: float32 [4, 256, 1024], replicated, may hold values from -0.9 to 0.9
- permutations: int32 [4, 8192], replicated, may hold values from 0 to 8191, as said below
- cotangent: bfloat16 [512, 28672], P('dp', 'tensor'), may hold values from -6 to 6
Outputs:
- projected: bfloat16 [512, 28672], P(('dp', 'fsdp'), 'tensor')
- param_grads: float32 [4, 256, 1024], P(None, ('dp', 'fsdp'))
Inputs may be any that keep to these rules, and one draw needn't show every extreme that they name: Row k is a butterfly permutation with span S = 8192 / 2^(3 - k): for position p = q * 32 + i, with q the block and i < 32, permutations[k, p] = (p - p mod S) + h * S / 2 + (q mod (S / 32)) * 16 + r, where h = sigma(i) // 16 and r = sigma(i) mod (16), and sigma is a permutation of 0 to 31 chosen for each factor and block.
All inputs are finite; a program needn't handle non-finite values.
Results may differ from a plain program's by a relative error of at most 0.012.
Values may be sent and summed in bfloat16 or wider, within the bound.
No kernel may reach another device: no remote copies, remote signals or barrier semaphores. Data moves between devices by JAX's collectives and lax.ppermute only.
A program may use at most 192 MiB of HBM per device.

v0:
```python
import jax
import jax.numpy as jnp
from jax import lax
from jax.sharding import PartitionSpec as P

BLOCK = 32
FACTORS = 4


HI = lax.Precision.HIGHEST


def cayley(params):
    shaped = params.reshape(params.shape[0], params.shape[1], BLOCK, BLOCK)
    skew = shaped - jnp.swapaxes(shaped, 2, 3)
    ident = jnp.eye(BLOCK, dtype=jnp.float32)
    plus = ident + skew
    metric = ident - jnp.matmul(skew, skew, precision=HI)
    right = jnp.matmul(plus, plus, precision=HI)
    lower = jnp.linalg.cholesky(metric)
    half = jax.scipy.linalg.solve_triangular(lower, right, lower=True)
    return jax.scipy.linalg.solve_triangular(lower, half, lower=True, trans=1)


def widen(blocks):
    group = 128 // BLOCK
    count = blocks.shape[0] // group
    shaped = blocks.reshape(count, group, BLOCK, BLOCK)
    bands = []
    for place in range(group):
        pieces = []
        if place > 0:
            pieces.append(jnp.zeros((count, BLOCK, place * BLOCK), jnp.bfloat16))
        pieces.append(shaped[:, place])
        if place < group - 1:
            pieces.append(jnp.zeros((count, BLOCK, (group - 1 - place) * BLOCK), jnp.bfloat16))
        bands.append(jnp.concatenate(pieces, axis=2))
    return jnp.concatenate(bands, axis=1)


def narrow(outer):
    group = 128 // BLOCK
    count = outer.shape[0]
    pieces = [
        outer[:, place * BLOCK : (place + 1) * BLOCK, place * BLOCK : (place + 1) * BLOCK]
        for place in range(group)
    ]
    return jnp.stack(pieces, axis=1).reshape(count * group, BLOCK * BLOCK)


def rotate(state, wides, permutations):
    saved = []
    for level in range(FACTORS):
        moved = jnp.take(state, permutations[level], axis=1)
        saved.append(moved)
        shaped = moved.reshape(moved.shape[0], -1, 128)
        state = (
            jnp.einsum("tgi,gij->tgj", shaped, wides[level], preferred_element_type=jnp.float32)
            .reshape(moved.shape)
            .astype(jnp.bfloat16)
        )
    return (state, saved)


def block_terms(saved, upstream, wides, permutations):
    terms = [None] * FACTORS
    for level in reversed(range(FACTORS)):
        rows_here, width = upstream.shape
        up_wide = upstream.reshape(rows_here, -1, 128)
        outer = jnp.einsum(
            "tgi,tgj->gij",
            saved[level].reshape(rows_here, -1, 128),
            up_wide,
            preferred_element_type=jnp.float32,
        )
        terms[level] = narrow(outer)
        if level > 0:
            spread = (
                jnp.einsum(
                    "tgj,gij->tgi", up_wide, wides[level], preferred_element_type=jnp.float32
                )
                .reshape(rows_here, width)
                .astype(jnp.bfloat16)
            )
            inverse = (
                jnp.zeros_like(permutations[level])
                .at[permutations[level]]
                .set(jnp.arange(width, dtype=jnp.int32))
            )
            upstream = jnp.take(spread, inverse, axis=1)
    return jnp.stack(terms)


def local(activations, frozen_weight, cayley_params, permutations, cotangent):
    group_size = lax.axis_size("fsdp")
    group_index = lax.axis_index("fsdp")
    tok_rows = activations.shape[0]
    own_tokens = tok_rows // group_size
    own_width = activations.shape[1]
    local_blocks = cayley_params.shape[1] // (lax.axis_size("dp") * group_size)
    offset = (lax.axis_index("dp") * group_size + group_index) * local_blocks
    local_params = lax.dynamic_slice_in_dim(cayley_params, offset, local_blocks, 1)
    rotation_local, pull = jax.vjp(cayley, local_params)
    local_half = rotation_local.reshape(
        rotation_local.shape[0], local_blocks, BLOCK * BLOCK
    ).astype(jnp.bfloat16)
    rotation_all = lax.all_gather(local_half, ("dp", "fsdp"), axis=1, tiled=True)
    wides = [widen(rotation_all[level]) for level in range(FACTORS)]
    full_rows = lax.all_gather(activations, "fsdp", axis=1, tiled=True)
    rotated_full, saved_full = rotate(full_rows, wides, permutations)
    rotated = lax.dynamic_slice_in_dim(rotated_full, group_index * own_width, own_width, 1)
    saved = [
        lax.dynamic_slice_in_dim(piece, group_index * own_tokens, own_tokens, 0)
        for piece in saved_full
    ]
    projected = lax.psum_scatter(
        jnp.dot(rotated, frozen_weight, preferred_element_type=jnp.float32),
        "fsdp",
        scatter_dimension=0,
        tiled=True,
    ).astype(jnp.bfloat16)
    partial_up = lax.dot_general(
        cotangent, frozen_weight, (((1,), (1,)), ((), ())), preferred_element_type=jnp.float32
    )
    upstream = lax.psum(partial_up, "tensor").astype(jnp.bfloat16)
    upstream_full = lax.all_gather(upstream, "fsdp", axis=1, tiled=True)
    upstream_own = lax.dynamic_slice_in_dim(upstream_full, group_index * own_tokens, own_tokens, 0)
    terms = block_terms(saved, upstream_own, wides, permutations)
    block_grad = lax.psum_scatter(terms, ("dp", "fsdp"), scatter_dimension=1, tiled=True)
    cotan_blocks = block_grad.reshape(block_grad.shape[0], local_blocks, BLOCK, BLOCK)
    param_grads = pull(cotan_blocks)[0]
    return (projected, param_grads)


def solution(mesh):
    return jax.shard_map(
        local,
        mesh=mesh,
        in_specs=(P("dp", "fsdp"), P("fsdp", "tensor"), P(), P(), P("dp", "tensor")),
        out_specs=(P(("dp", "fsdp"), "tensor"), P(None, ("dp", "fsdp"), None)),
        check_vma=False,
    )
```

profile of v0, /device:TPU:6, one launch (start us, length us, event | category | flops | bytes accessed | tf_op | source)
XLA Modules:
  0.0 1015.9 jit_solution(5586696151075053320)
XLA Ops:
  10.9 93.8 %custom-call.14 = f32[4,8,32,32]{3,2,1,0:T(8,128)S(1)} custom-call(f32[4,8,32,32]{3,2,1,0:T(8,128)S(1)} %fusion.58), custom_call_target="Cholesky" | custom-call | tf_op jit(solution)/shard_map/jvp(jit(cholesky))/cholesky | solution.py:20
  105.9 78.8 %custom-call.22 = f32[4,8,1,32,32]{3,4,2,1,0:T(8,128)S(1)} custom-call(f32[4,8,1,32,32]{4,3,2,1,0:T(8,128)S(1)} %get-tuple-element.51), custom_call_target="InvertDiagBlocksLowerTriangular" | custom-call | tf_op jit(solution)/shard_map/jvp(jit(_solve_triangular))/vmap(vmap())/triangular_solve/custom-call.2 | solution.py:22
  189.1 6.3 fusion.110
  195.4 18.3 %all-reduce.9 = bf16[256,512]{1,0:T(8,128)(2,1)} all-reduce(f32[256,512]{1,0:T(8,128)S(1)} %fusion.110), channel_id=1, replica_groups=mesh['dp'=2,'fsdp'=16,'tensor'=4] {'tensor'}, use_global_device_ids=true, to_apply=%region_3.7 | all-reduce | flops 131072 | bytes 786432 | tf_op jit(solution)/shard_map/psum | solution.py:125
  214.0 30.5 %scatter_custom_fusion = s32[8192]{0:T(1024)S(1)} fusion(s32[8192]{0:T(1024)S(1)} %bitcast.299, s32[8192]{0:T(1024)S(1)} %iota.183, s32[]{:T(128)} %constant.102.clone.1), kind=kCustom, calls=%fused_computation.191 | custom fusion | bytes 32772 | tf_op jit(solution)/shard_map/scatter | solution.py:88
  245.1 30.5 %scatter_custom_fusion.1 = s32[8192]{0:T(1024)S(1)} fusion(s32[8192]{0:T(1024)S(1)} %bitcast.298, s32[8192]{0:T(1024)S(1)} %iota.184, s32[]{:T(128)} %constant.102.clone.1), kind=kCustom, calls=%fused_computation.189 | custom fusion | bytes 32772 | tf_op jit(solution)/shard_map/scatter | solution.py:88
  276.2 30.5 %scatter_custom_fusion.2 = s32[8192]{0:T(1024)S(1)} fusion(s32[8192]{0:T(1024)S(1)} %bitcast.297, s32[8192]{0:T(1024)S(1)} %iota.185, s32[]{:T(128)} %constant.102.clone.1), kind=kCustom, calls=%fused_computation.187 | custom fusion | bytes 32772 | tf_op jit(solution)/shard_map/scatter | solution.py:88
  307.0 2.8 fusion.106
  309.8 3.0 reshape_squeeze.13
  320.6 4.5 pad_maximum_fusion.7
  328.6 2.8 reshape_squeeze.12
  355.5 4.0 fusion.10
  359.5 33.8 %gather_fusion = bf16[8192,256]{1,0:T(8,128)(2,1)} fusion(bf16[256,8192]{0,1:T(8,128)(2,1)} %all-gather.6.cloned.1.call-done, s32[8192]{0:T(1024)S(1)} %fusion.78), kind=kCustom, calls=%fused_computation.clone | custom fusion | bytes 8421376 | tf_op jit(solution)/shard_map/jit(_take)/gather | solution.py:54
  393.3 6.1 broadcast_select_fusion.3
  399.5 4.1 convolution_convert_fusion.3
  403.6 33.9 %gather_fusion.1 = bf16[8192,256]{1,0:T(8,128)(2,1)} fusion(bf16[256,8192]{0,1:T(8,128)(2,1)} %bitcast.255, s32[8192]{0:T(1024)S(1)} %fusion.79), kind=kCustom, calls=%fused_computation.2.clone | custom fusion | bytes 8421376 | tf_op jit(solution)/shard_map/jit(_take)/gather | solution.py:54
  437.5 6.1 broadcast_select_fusion.2
  443.6 4.0 convolution_convert_fusion.2
  447.6 33.8 %gather_fusion.2 = bf16[8192,256]{1,0:T(8,128)(2,1)} fusion(bf16[256,8192]{0,1:T(8,128)(2,1)} %bitcast.257, s32[8192]{0:T(1024)S(1)} %fusion.80), kind=kCustom, calls=%fused_computation.3.clone | custom fusion | bytes 8421376 | tf_op jit(solution)/shard_map/jit(_take)/gather | solution.py:54
  481.4 5.6 fusion.153
  487.0 5.2 fusion.154
  492.2 5.2 fusion.155
  497.4 5.6 broadcast_select_fusion.1
  506.4 30.1 %gather_fusion.4 = bf16[8192,16]{1,0:T(8,128)(2,1)} fusion(bf16[16,8192]{0,1:T(8,128)(2,1)} %bitcast.260, s32[8192]{0:T(1024)S(1)} %fusion.82), kind=kCustom, calls=%fused_computation.1.clone | custom fusion | bytes 557056 | tf_op jit(solution)/shard_map/jit(_take)/gather | solution.py:90
  536.5 5.7 broadcast_select_fusion.6
  543.5 3.6 fusion.35
  547.1 2.7 copy.260
  549.8 30.1 %gather_fusion.5 = bf16[8192,16]{1,0:T(8,128)(2,1)} fusion(bf16[16,8192]{0,1:T(8,128)(2,1)} %bitcast.261, s32[8192]{0:T(1024)S(1)} %fusion.83), kind=kCustom, calls=%fused_computation.5.clone | custom fusion | bytes 557056 | tf_op jit(solution)/shard_map/jit(_take)/gather | solution.py:90
  579.8 6.0 broadcast_select_fusion.5
  587.1 2.9 fusion.36
  591.8 3.5 constant_dynamic-slice_fusion.3
  595.4 30.0 %gather_fusion.6 = bf16[8192,16]{1,0:T(8,128)(2,1)} fusion(bf16[16,8192]{0,1:T(8,128)(2,1)} %bitcast.259, s32[8192]{0:T(1024)S(1)} %fusion.84), kind=kCustom, calls=%fused_computation.6.clone | custom fusion | bytes 557056 | tf_op jit(solution)/shard_map/jit(_take)/gather | solution.py:90
  625.4 6.0 broadcast_select_fusion.4
  634.7 2.6 copy.212
  637.3 3.9 stack_reshape.12
  649.5 4.6 stack_reshape.13
  659.7 2.7 copy.220
  662.4 5.0 stack_reshape.14
  667.4 8.1 convolution_convert_fusion.1
  675.5 33.9 %gather_fusion.3 = bf16[8192,256]{1,0:T(8,128)(2,1)} fusion(bf16[256,8192]{0,1:T(8,128)(2,1)} %bitcast.256, s32[8192]{0:T(1024)S(1)} %fusion.81), kind=kCustom, calls=%fused_computation.4.clone | custom fusion | bytes 8421376 | tf_op jit(solution)/shard_map/jit(_take)/gather | solution.py:54
  709.4 6.0 fusion.156
  721.7 4.6 stack_reshape.15
  726.2 4.4 pad_maximum_fusion.4
  730.8 6.1 broadcast_select_fusion
  738.8 5.1 fusion.67
  743.9 79.8 %custom-call.27 = f32[4,8,1,32,32]{3,4,2,1,0:T(8,128)S(1)} custom-call(f32[4,8,1,32,32]{4,3,2,1,0:T(8,128)} %get-tuple-element.50), custom_call_target="InvertDiagBlocksLowerTriangular" | custom-call | tf_op jit(solution)/shard_map/transpose(jvp(jit(cholesky)))/triangular_solve/custom-call.2 | solution.py:20
  823.8 89.6 %reduce-scatter.5.cloned.1.call-done = f32[4,8,1024]{2,1,0:T(8,128)} async-done(((f32[4,256,1024]{2,1,0:T(8,128)}), f32[4,8,1024]{2,1,0:T(8,128)}) %reduce-scatter.5.cloned.1.call-update) | async-done | bytes 131088 | tf_op jit(solution)/shard_map/reduce_scatter | solution.py:129
  928.1 79.3 %reduce-scatter.3.cloned.1.call-done = f32[16,7168]{1,0:T(8,128)} async-done(((f32[256,7168]{1,0:T(8,128)}), f32[16,7168]{1,0:T(8,128)}) %reduce-scatter.3.cloned.1.call-update) | async-done | bytes 458768 | tf_op jit(solution)/shard_map/reduce_scatter | solution.py:116
  (227 shorter events, 95.7 us)
Async XLA Ops:
  7.2 299.8 %all-gather.4.cloned.1.call-start = ((), (), s32[]{:S(2)}) async-start(), calls=%async_computation.2 | async-start | bytes 2162688 | tf_op jit(solution)/shard_map/all_gather | solution.py:107
  7.2 3.7 copy-start.42
  7.9 97.1 %copy-start.46 = (pred[32,32]{1,0:T(8,128)(4,1)}, pred[32,32]{1,0:T(8,128)(4,1)S(1)}, u32[]{:S(2)}) copy-start(pred[32,32]{1,0:T(8,128)(4,1)S(1)} %get-tuple-element.65) | copy-start | bytes 3076
  9.2 176.5 %copy-start.2 = (f32[4,8,32,32]{3,2,1,0:T(8,128)}, f32[4,8,32,32]{3,2,1,0:T(8,128)S(1)}, u32[]{:S(2)}) copy-start(f32[4,8,32,32]{3,2,1,0:T(8,128)S(1)} %bitcast_subtract_fusion.1) | copy-start | bytes 393220
  10.1 178.1 %copy-start.45 = (bf16[256,512]{1,0:T(8,128)(2,1)S(1)}, bf16[256,512]{1,0:T(8,128)(2,1)}, u32[]{:S(2)}) copy-start(bf16[256,512]{1,0:T(8,128)(2,1)} %param.13) | copy-start | bytes 786436
  104.9 90.5 %copy-start.50 = (pred[4,8]{1,0:T(4,128)(4,1)}, pred[4,8]{1,0:T(4,128)(4,1)S(1)}, u32[]{:S(2)}) copy-start(pred[4,8]{1,0:T(4,128)(4,1)S(1)} %compare_reduce_fusion) | copy-start | bytes 100
  184.7 10.7 %copy-start.4 = (f32[4,8,1,32,32]{3,4,2,1,0:T(8,128)}, f32[4,8,1,32,32]{3,4,2,1,0:T(8,128)S(1)}, u32[]{:S(2)}) copy-start(f32[4,8,1,32,32]{3,4,2,1,0:T(8,128)S(1)} %custom-call.22) | copy-start | bytes 393220
  188.1 171.4 %all-gather.6.cloned.1.call-start = ((), (), s32[]{:S(2)}) async-start(), calls=%async_computation.3 | async-start | bytes 4456448 | tf_op jit(solution)/shard_map/all_gather | solution.py:109
  189.0 24.8 %copy-start.44 = (s32[4,8192]{1,0:T(4,128)S(1)}, s32[4,8192]{1,0:T(4,128)}, u32[]{:S(2)}) copy-start(s32[4,8192]{1,0:T(4,128)} %param.16) | copy-start | bytes 393220
  189.0 314.0 %all-gather.8.cloned.1.call-start = ((), (), s32[]{:S(2)}) async-start(), calls=%async_computation.5 | async-start | bytes 4456448 | tf_op jit(solution)/shard_map/all_gather | solution.py:126
  213.7 699.7 %reduce-scatter.5.cloned.1.call-start = ((), (), s32[]{:S(2)}) async-start(), calls=%async_computation.6 | async-start | bytes 4325376 | tf_op jit(solution)/shard_map/reduce_scatter | solution.py:129
  333.8 3.6 copy-start.33
  333.8 7.2 copy-start.32
  333.8 8.2 copy-start.16
  335.6 8.1 copy-start.15
  341.0 8.8 copy-start.14
  343.8 7.8 copy-start.13
  345.6 7.9 copy-start.31
  345.6 8.9 copy-start.30
  393.3 6.1 copy-start.26
  393.3 6.1 copy-start.27
  393.3 6.2 copy-start.40
  393.3 6.2 copy-start.41
  437.5 6.1 copy-start.22
  437.5 6.1 copy-start.24
  437.5 6.2 copy-start.36
  437.5 6.2 copy-start.38
  481.4 5.6 copy-start
  487.0 5.2 copy-start.1
  504.7 38.8 %copy-start.34 = (bf16[64,1,32,32]{2,3,0,1:T(8,128)(2,1)S(1)}, bf16[64,1,32,32]{2,3,0,1:T(8,128)(2,1)}, u32[]{:S(2)}) copy-start(bf16[64,1,32,32]{2,3,0,1:T(8,128)(2,1)} %copy.273) | copy-start | bytes 393220
  504.7 38.8 %copy-start.35 = (bf16[64,1,32,32]{2,3,0,1:T(8,128)(2,1)S(1)}, bf16[64,1,32,32]{2,3,0,1:T(8,128)(2,1)}, u32[]{:S(2)}) copy-start(bf16[64,1,32,32]{2,3,0,1:T(8,128)(2,1)} %copy.274) | copy-start | bytes 393220
  536.5 7.0 copy-start.20
  536.5 7.0 copy-start.21
  547.1 32.8 %copy-start.49 = (pred[8192]{0:T(1024)(128)(4,1)S(1)}, pred[8192]{0:T(1024)(128)(4,1)}, u32[]{:S(2)}) copy-start(pred[8192]{0:T(1024)(128)(4,1)} %compare_and_fusion.1) | copy-start | bytes 24580
  547.1 40.0 %copy-start.37 = (bf16[64,1,32,32]{2,3,0,1:T(8,128)(2,1)S(1)}, bf16[64,1,32,32]{2,3,0,1:T(8,128)(2,1)}, u32[]{:S(2)}) copy-start(bf16[64,1,32,32]{2,3,0,1:T(8,128)(2,1)} %copy.275) | copy-start | bytes 393220
  547.1 40.0 %copy-start.39 = (bf16[64,1,32,32]{2,3,0,1:T(8,128)(2,1)S(1)}, bf16[64,1,32,32]{2,3,0,1:T(8,128)(2,1)}, u32[]{:S(2)}) copy-start(bf16[64,1,32,32]{2,3,0,1:T(8,128)(2,1)} %copy.276) | copy-start | bytes 393220
  579.8 7.3 copy-start.23
  579.8 7.3 copy-start.25
  625.4 6.0 copy-start.10
  730.7 276.7 %reduce-scatter.3.cloned.1.call-start = ((), (), s32[]{:S(2)}) async-start(), calls=%async_computation.4 | async-start | bytes 7798784 | tf_op jit(solution)/shard_map/reduce_scatter | solution.py:116
  730.7 7.5 slice-start
  743.9 170.6 %copy-start.5 = (f32[4,8,1,32,32]{3,4,2,1,0:T(8,128)S(1)}, f32[4,8,1,32,32]{3,4,2,1,0:T(8,128)}, u32[]{:S(2)}) copy-start(f32[4,8,1,32,32]{3,4,2,1,0:T(8,128)} %copy-done.4) | copy-start | bytes 393220
  743.9 171.6 %copy-start.12 = (f32[4,8,32,32]{3,2,1,0:T(8,128)S(1)}, f32[4,8,32,32]{3,2,1,0:T(8,128)}, u32[]{:S(2)}) copy-start(f32[4,8,32,32]{3,2,1,0:T(8,128)} %copy-done.11) | copy-start | bytes 393220
  743.9 172.6 %copy-start.17 = (f32[4,8,32,32]{3,2,1,0:T(8,128)S(1)}, f32[4,8,32,32]{3,2,1,0:T(8,128)}, u32[]{:S(2)}) copy-start(f32[4,8,32,32]{3,2,1,0:T(8,128)} %get-tuple-element.62) | copy-start | bytes 393220
  743.9 173.5 %copy-start.47 = (pred[32,32]{1,0:T(8,128)(4,1)S(1)}, pred[32,32]{1,0:T(8,128)(4,1)}, u32[]{:S(2)}) copy-start(pred[32,32]{1,0:T(8,128)(4,1)} %copy-done.46) | copy-start | bytes 3076
  914.5 4.7 copy-start.29
  914.5 4.7 copy-start.51
  921.0 3.8 copy-start.48
  (11 other events, 22.3 us)
Sparse Core Ops, SparseCore 0:
  188.2 71.2 all-gather.3
  261.7 50.2 all-gather.5
  314.2 56.9 all-gather.7
  730.8 182.5 reduce-scatter.4
  916.7 90.6 reduce-scatter.2
where the time goes:
time: 1030 us; the launch traced here: 1020 us
  local copies, waits for them, and re-layouts  416 us (40%)
  other arithmetic  338 us (33%)
  waiting for transfers between devices  169 us (16%)
  matrix products  59.1 us (6%)
  blocking collectives  18.3 us (2%)
  between operations  15.1 us (1%)
    another operation x6, other arithmetic, cayley(): lower = jnp.linalg.cholesky(metric)  175 us
    gather x4, local copies, waits for them, and re-layouts, rotate(): moved = jnp.take(state, permutations[level], axis=1)  135 us
    scatter x3, local copies, waits for them, and re-layouts, block_terms(): inverse = jnp.zeros_like(permutations[level]).at[permutations[level]].set...  91.4 us
    gather x3, local copies, waits for them, and re-layouts, block_terms(): upstream = jnp.take(spread, inverse, axis=1)  90.2 us
    reduce_scatter x1, waiting for transfers between devices, local(): lax.psum_scatter(terms, ('dp', 'fsdp'), scatter_dimension=1, tiled=True)  89.6 us
    another operation x2, other arithmetic, cayley(): return jax.scipy.linalg.solve_triangular(lower, half, lower=True, trans=1)  79.4 us
    reduce_scatter x1, waiting for transfers between devices, local(): lax.psum_scatter(jnp.dot(rotated, frozen_weight, preferred_element_type=j...  79.3 us
    select_n x8, other arithmetic, rotate(): moved = jnp.take(state, permutations[level], axis=1)  45.9 us
  transfers between devices with their start and end apart: 5, of which 2 were waited for; matrix products, arithmetic and copies ran while one was open for 40% of the time, Pallas kernels for 0%

commit v1 on v0

v1 whole, which is shorter than its diff:
```python
import functools

import jax
import jax.numpy as jnp
from jax import lax
from jax.experimental import pallas as pl
from jax.experimental.pallas import tpu as pltpu
from jax.sharding import PartitionSpec as P

BLOCK = 32
FACTORS = 4
RUN = 16
LANES = 128
BF = jnp.bfloat16
F32 = jnp.float32
HI = lax.Precision.HIGHEST


def iota(shape, dim):
    return lax.broadcasted_iota(jnp.int32, shape, dim)


def dot(a, b, ca, cb, precision=None):
    return lax.dot_general(
        a, b, (((ca,), (cb,)), ((), ())), precision=precision, preferred_element_type=F32
    )


def call(body, out_shape, args, scratch=(), limit=48 << 20):
    return pl.pallas_call(
        body,
        out_shape=out_shape,
        in_specs=[pl.BlockSpec(memory_space=pltpu.VMEM)] * len(args),
        out_specs=jax.tree.map(lambda _: pl.BlockSpec(memory_space=pltpu.VMEM), out_shape),
        scratch_shapes=list(scratch),
        compiler_params=pltpu.CompilerParams(vmem_limit_bytes=limit),
    )(*args)


def shape(dims, dtype):
    return jax.ShapeDtypeStruct(dims, dtype)


def inverse_body(p_ref, rd_ref, ad_ref, turned, mat, rows):
    turned[...] = p_ref[...].T
    sub = iota((BLOCK, LANES), 0)
    for i in range(BLOCK):
        skew = turned[i * BLOCK : (i + 1) * BLOCK, :] - turned[pl.ds(i, BLOCK, stride=BLOCK), :]
        mat[i] = jnp.where(sub == i, 1.0, 0.0) - skew

    def step(k, carry):
        here = sub == k
        pivot = 1.0 / mat[k, pl.ds(k, 1), :]
        line = jnp.where(here, pivot, mat[k] * pivot)
        for i in range(BLOCK):
            factor = mat[i, pl.ds(k, 1), :]
            mat[i] = jnp.where(here, 0.0, mat[i]) - factor * line
        mat[k] = line
        return carry

    lax.fori_loop(0, BLOCK, step, 0)
    for i in range(BLOCK):
        rows[pl.ds(i, LANES, stride=BLOCK), :] = mat[i].T
    same = iota((LANES, LANES), 0) // BLOCK == iota((LANES, LANES), 1) // BLOCK
    unit = jnp.where(iota((LANES, LANES), 0) == iota((LANES, LANES), 1), 1.0, 0.0)
    for g in range(24):
        piece = rows[g * LANES : (g + 1) * LANES, :]
        wide = jnp.where(same, jnp.concatenate([piece] * 4, axis=1), 0.0)
        if g < 16:
            rd_ref[g * LANES : (g + 1) * LANES, :] = (2.0 * wide - unit).astype(BF)
        else:
            ad_ref[(g - 16) * LANES : (g - 15) * LANES, :] = wide


def onehot(idx_ref, level, g):
    return jnp.where(
        iota((LANES, LANES), 0) == idx_ref[level : level + 1, g * LANES : (g + 1) * LANES], 1.0, 0.0
    ).astype(BF)


def shuffle(x, level):
    groups = 16 >> level
    width = 512 // groups
    pieces = []
    for h in range(groups // 2):
        for i in range(width // RUN):
            for half in range(2):
                start = (2 * h + half) * width + i * RUN
                pieces.append(x[start : start + RUN])
    return jnp.concatenate(pieces, axis=0)


def unshuffle(x, level):
    groups = 16 >> level
    width = 512 // groups
    count = width // RUN
    pieces = []
    for a in range(groups):
        for i in range(count):
            start = ((a // 2) * count + i) * BLOCK + (a % 2) * RUN
            pieces.append(x[start : start + RUN])
    return jnp.concatenate(pieces, axis=0)


def forward_body(x_ref, rd_ref, idx_ref, out_ref, moved_ref):
    x = x_ref[...]
    for level in range(FACTORS):
        x = shuffle(x, level)
        outs = []
        for g in range(4):
            moved = dot(onehot(idx_ref, level, g), x[g * LANES : (g + 1) * LANES], 0, 0).astype(BF)
            base = (level * 4 + g) * LANES
            moved_ref[base : base + LANES, :] = moved
            rot = rd_ref[base : base + LANES, :]
            if level < FACTORS - 1:
                outs.append(dot(rot, moved, 0, 0).astype(BF))
            else:
                out_ref[:, g * LANES : (g + 1) * LANES] = dot(moved, rot, 0, 0).astype(BF)
        if level < FACTORS - 1:
            x = jnp.concatenate(outs, axis=0)


def backward_body(up_ref, moved_ref, rd_ref, idx_ref, grad_ref):
    up = up_ref[...]
    same = iota((LANES, LANES), 0) // BLOCK == iota((LANES, LANES), 1) // BLOCK
    for level in reversed(range(FACTORS)):
        outs = []
        for g in range(4):
            base = (level * 4 + g) * LANES
            mine = up[g * LANES : (g + 1) * LANES]
            outer = jnp.where(same, dot(moved_ref[base : base + LANES, :], mine, 1, 1), 0.0)
            packed = outer[:BLOCK] + outer[BLOCK : 2 * BLOCK]
            packed = packed + outer[2 * BLOCK : 3 * BLOCK] + outer[3 * BLOCK :]
            grad_ref[level, g] = packed
            if level > 0:
                spread = dot(rd_ref[base : base + LANES, :], mine, 1, 0).astype(BF)
                outs.append(dot(onehot(idx_ref, level, g), spread, 1, 0).astype(BF))
        if level > 0:
            up = unshuffle(jnp.concatenate(outs, axis=0), level)


def pull_body(g_ref, ad_ref, out_ref):
    same = iota((LANES, LANES), 0) // BLOCK == iota((LANES, LANES), 1) // BLOCK
    for g in range(8):
        grad = jnp.where(same, jnp.concatenate([g_ref[g]] * 4, axis=0), 0.0)
        inv = ad_ref[g * LANES : (g + 1) * LANES, :]
        both = 2.0 * dot(dot(inv, grad, 0, 0, HI), inv, 1, 1, HI)
        both = both - both.T
        packed = both[:BLOCK] + both[BLOCK : 2 * BLOCK]
        out_ref[g] = packed + both[2 * BLOCK : 3 * BLOCK] + both[3 * BLOCK :]


def fetch(array, start, count, axis):
    return lax.dynamic_slice_in_dim(array, start, count, axis)


def own_blocks(table, f):
    tail = table.shape[2:]
    parts = []
    for level in range(FACTORS):
        groups = 8 >> level
        shaped = table[level].reshape(groups, 256 // groups, *tail)
        parts.append(fetch(shaped, f * (16 // groups), 16 // groups, 1).reshape(16, *tail))
    return jnp.concatenate(parts, axis=0)


def shift_z(s):
    return [(z * 4 + x, ((z + s) % 4) * 4 + x) for z in range(4) for x in range(4)]


def shift_x(s):
    return [(z * 4 + x, z * 4 + (x + s) % 4) for z in range(4) for x in range(4)]


def send(x, pairs, axis="fsdp"):
    return lax.ppermute(x, axis, pairs)


def roll(x, by, axis):
    return fetch(jnp.concatenate([x, x], axis=axis), by, x.shape[axis], axis)


def reduce_stage(part, shift):
    half = part.shape[1] // 2
    from_low = send(part[2, :half], shift(1))
    from_high = send(part[2, half:], shift(3))
    up = jnp.concatenate([(part[1, :half].astype(F32) + from_low).astype(BF), part[1, half:]], 0)
    down = jnp.concatenate([part[3, :half], (part[3, half:].astype(F32) + from_high).astype(BF)], 0)
    return (part[0].astype(F32) + send(up, shift(1)) + send(down, shift(3))).astype(BF)


def direct_stage(part, shift):
    total = part[0].astype(F32)
    for s in (1, 3, 2):
        total = total + send(part[s], shift(s))
    return total.astype(BF)


def local(activations, frozen_weight, cayley_params, permutations, cotangent):
    f = lax.axis_index("fsdp")
    d = lax.axis_index("dp")
    z, x = f // 4, f % 4
    tokens = activations.shape[0]

    mixed = lax.all_to_all(
        activations.T.reshape(16, BLOCK, tokens), "fsdp", 0, 0, tiled=True
    ).reshape(512, tokens)

    dest = fetch(cayley_params, (d * 16 + f) * 8, 8, 1).reshape(32, BLOCK * BLOCK)
    blocks = jnp.concatenate(
        [own_blocks(cayley_params, f), dest, jnp.zeros((32, BLOCK * BLOCK), F32)], axis=0
    )
    rd, ad = call(
        inverse_body,
        (shape((2048, LANES), BF), shape((1024, LANES), F32)),
        (blocks,),
        (
            pltpu.VMEM((BLOCK * BLOCK, LANES), F32),
            pltpu.VMEM((BLOCK, BLOCK, LANES), F32),
            pltpu.VMEM((BLOCK * LANES, BLOCK), F32),
        ),
    )

    sizes = jnp.array([1024, 2048, 4096, 8192], jnp.int32).reshape(FACTORS, 1)
    sigma = (permutations % sizes) // (sizes // 2) * RUN + permutations % RUN
    idx = own_blocks(sigma.reshape(FACTORS, 256, BLOCK), f).reshape(FACTORS, 512)
    idx = idx + (jnp.arange(512, dtype=jnp.int32) // BLOCK % 4 * BLOCK)[None]

    state, moved = call(
        forward_body, (shape((tokens, 512), BF), shape((2048, tokens), BF)), (mixed, rd, idx)
    )

    state = roll(roll(state.reshape(4, 4, RUN, 512), z, 0), x, 1)
    half = frozen_weight.shape[1] // 2
    first = jnp.dot(
        state.reshape(tokens, 512), frozen_weight[:, :half], preferred_element_type=F32
    ).astype(BF)
    second = jnp.dot(
        state.transpose(1, 0, 2, 3).reshape(tokens, 512),
        frozen_weight[:, half:],
        preferred_element_type=F32,
    ).astype(BF)
    first = reduce_stage(first.reshape(4, 64, half), shift_z)
    second = reduce_stage(second.reshape(4, 64, half), shift_x)
    first = direct_stage(first.reshape(4, RUN, half), shift_x)
    second = direct_stage(second.reshape(4, RUN, half), shift_z)
    projected = jnp.concatenate([first, second], axis=1)

    up = dot(frozen_weight, cotangent, 1, 1).astype(BF)
    up = (up.astype(F32) + send(up, [(t, t ^ 1) for t in range(4)], "tensor")).astype(BF)
    up = (up.astype(F32) + send(up, [(t, t ^ 2) for t in range(4)], "tensor")).astype(BF)

    grads = call(
        backward_body, shape((FACTORS, 4, BLOCK, LANES), F32), (up, moved, rd, idx)
    )
    grads = fetch(grads, 2 * d, 2, 1) + send(
        fetch(grads, 2 - 2 * d, 2, 1), [(0, 1), (1, 0)], "dp"
    )

    low, high = f // 4, f % 4
    spots = grads[0].reshape(2, BLOCK, 2, 64).transpose(0, 2, 1, 3).reshape(4, BLOCK, 64)
    blank = jnp.zeros_like(spots)
    odd = f % 2 == 1
    spots = jnp.concatenate([jnp.where(odd, blank, spots), jnp.where(odd, spots, blank)], axis=2)
    level0 = [0.0, 0.0]
    for r in range(4):
        pairs = [(s, ((s % 4 + r) % 4) * 4 + s // 4) for s in range(16)]
        got = send(lax.dynamic_index_in_dim(spots, (high + r) % 4, 0, False), pairs)
        second_pair = (low - r) % 4 // 2 == 1
        level0[0] = level0[0] + jnp.where(second_pair, 0.0, got)
        level0[1] = level0[1] + jnp.where(second_pair, got, 0.0)
    got = []
    for r in range(2):
        pairs = [(s, ((s % 2 + r) % 2) * 8 + s // 2) for s in range(16)]
        got.append(send(lax.dynamic_index_in_dim(grads[1], (f + r) % 2, 0, False), pairs))
    swap = f // 8 == 1
    level1 = [jnp.where(swap, got[1], got[0]), jnp.where(swap, got[0], got[1])]
    pairs = [
        (e * 16 + s, (s // 8) * 16 + 2 * (s % 8) + e) for e in range(2) for s in range(16)
    ]
    level3 = send(grads[3], pairs, ("dp", "fsdp"))
    owned = jnp.concatenate([jnp.stack(level0), jnp.stack(level1), grads[2], level3], axis=0)
    pulled = call(pull_body, shape((8, BLOCK, LANES), F32), (owned, ad))
    param_grads = (
        pulled.reshape(FACTORS, 2, BLOCK, 4, BLOCK)
        .transpose(0, 1, 3, 2, 4)
        .reshape(FACTORS, 8, BLOCK * BLOCK)
    )
    return (projected, param_grads)


def solution(mesh):
    return jax.shard_map(
        local,
        mesh=mesh,
        in_specs=(P("dp", "fsdp"), P("fsdp", "tensor"), P(), P(), P("dp", "tensor")),
        out_specs=(P(("dp", "fsdp"), "tensor"), P(None, ("dp", "fsdp"), None)),
        check_vma=False,
    )
```

time: 1030 us -> 125 us (0.12); the launches traced: 1020 us -> 123 us
  local copies, waits for them, and re-layouts: 416 us -> 11.2 us
  other arithmetic: 338 us -> 13.5 us
  waiting for transfers between devices: 169 us -> 15.3 us
  starting transfers between devices: 0.21 us -> 55.7 us
  matrix products: 59.1 us -> 12.6 us
  blocking collectives: 18.3 us -> 0 us
  Pallas kernels: 0 us -> 13.7 us
  between operations: 15.1 us -> 1.52 us
    another operation x13 -> x0, other arithmetic: 261 us -> none  [the longest x6 175 us: cayley(): lower = jnp.linalg.cholesky(metric)]
    gather x7 -> x0, local copies, waits for them, and re-layouts: 226 us -> none  [the longest x4 135 us: rotate(): moved = jnp.take(state, permutations[level], axis=1)]
    reduce_scatter x2 -> x0, waiting for transfers between devices: 169 us -> none  [the longest x1 89.6 us: local(): lax.psum_scatter(terms, ('dp', 'fsdp'), scatter_dimension=1, tiled=True)]
    scatter x3 -> x0, local copies, waits for them, and re-layouts: 91.4 us -> none  [block_terms(): inverse = jnp.zeros_like(permutations[level]).at[permutations[level]].set...]
    select_n x12 -> x0, other arithmetic: 63.7 us -> none  [the longest x8 45.9 us: rotate(): moved = jnp.take(state, permutations[level], axis=1)]
    ppermute x0 -> x24, starting transfers between devices: none -> 47.4 us  [send(): return lax.ppermute(x, axis, pairs)]
    another operation x19 -> x3, local copies, waits for them, and re-layouts: 41.5 us -> 0.24 us  [own_blocks(): shaped = table[level].reshape(groups, 256 // groups, *tail)]
    dot_general x22 -> x3, matrix products: 51.7 us -> 12.6 us  [the longest x1 6.27 us: dot(): lax.dot_general(a, b, (((ca,), (cb,)), ((), ())), precision=precision, pr...]
  transfers between devices with their start and end apart: 5 -> 25, of which waited for: 2 -> 9; matrix products, arithmetic and copies ran while one was open for 40% -> 28% of each run, Pallas kernels for 0% -> 11%
where the time goes in v1:
time: 125 us; the launch traced here: 123 us
  starting transfers between devices  55.7 us (45%)
  waiting for transfers between devices  15.3 us (12%)
  Pallas kernels  13.7 us (11%)
  other arithmetic  13.5 us (11%)
  matrix products  12.6 us (10%)
  local copies, waits for them, and re-layouts  11.2 us (9%)
  between operations  1.52 us (1%)
    ppermute x24, starting transfers between devices, send(): return lax.ppermute(x, axis, pairs)  47.4 us
    ppermute x24, waiting for transfers between devices, send(): return lax.ppermute(x, axis, pairs)  15.3 us
    pallas_call x4, Pallas kernels, call(): pl.pallas_call(body, out_shape=out_shape, in_specs=[pl.BlockSpec(memory_s...  13.7 us
    all_to_all x1, starting transfers between devices, local(): lax.all_to_all(activations.T.reshape(16, BLOCK, tokens), 'fsdp', 0, 0, ti...  8.26 us
    dot_general x1, matrix products, dot(): lax.dot_general(a, b, (((ca,), (cb,)), ((), ())), precision=precision, pr...  6.27 us
    add x1, other arithmetic, local(): sigma = permutations % sizes // (sizes // 2) * RUN + permutations % RUN  6.16 us
    slice x3, local copies, waits for them, and re-layouts, own_blocks(): shaped = table[level].reshape(groups, 256 // groups, *tail)  4.39 us
    dot_general x1, matrix products, local(): jnp.dot(state.transpose(1, 0, 2, 3).reshape(tokens, 512), frozen_weight[:...  3.16 us
  transfers between devices with their start and end apart: 25, of which 9 were waited for; matrix products, arithmetic and copies ran while one was open for 28% of the time, Pallas kernels for 11%

profile of v1, /device:TPU:6, one launch (start us, length us, event | category | flops | bytes accessed | tf_op | source)
XLA Modules:
  0.0 123.4 jit_solution(3888347929439758024)
XLA Ops:
  0.6 1.8 %copy.16 = bf16[256,512]{0,1:T(8,128)(2,1)} copy(bf16[256,512]{1,0:T(8,128)(2,1)} %param.6) | data formatting | bytes 524288 | tf_op args[0]
  2.4 8.3 %all-to-all-start = ((bf16[16,32,256]{2,1,0:T(8,128)(2,1)}), bf16[16,32,256]{2,1,0:T(8,128)(2,1)S(1)}, u32[]{:S(2)}, u32[]{:S(2)}) async-start(bf16[16,32,256]{2,1,0:T(8,128)(2,1)} %bitcast.1), calls=%async_computation | async-start | bytes 524288 | tf_op jit(solution)/shard_map/all_to_all | solution.py:205
  10.7 6.3 %convolution_convert_fusion.2 = bf16[512,256]{1,0:T(8,128)(2,1)S(1)} fusion(bf16[512,7168]{1,0:T(8,128)(2,1)} %param.7, bf16[256,7168]{1,0:T(8,128)(2,1)} %param.10), kind=kOutput, calls=%fused_computation.4 | convolution fusion | flops 1879179264 | bytes 11272192 | tf_op jit(solution)/shard_map/dot_general | solution.py:24
  17.3 4.0 %fusion.25 = (f32[1,256,1024]{2,1,0:T(8,128)S(1)}, f32[1,256,1024]{2,1,0:T(8,128)S(1)}, f32[1,256,1024]{2,1,0:T(8,128)}, f32[1,256,1024]{2,1,0:T(8,128)}) fusion(f32[4,256,1024]{2,1,0:T(8,128)} %param.8), kind=kLoop, calls=%fused_computation.113 | loop fusion | bytes 8388608 | tf_op jit(solution)/shard_map/slice | solution.py:162
  21.2 1.0 constant_dynamic-slice_fusion.4
  22.3 0.9 constant_dynamic-slice_fusion.3
  23.3 0.9 bitcast_dynamic-update-slice_fusion
  24.3 6.2 %fusion.9 = s32[4,8192]{1,0:T(4,128)S(1)} fusion(s32[4,8192]{1,0:T(4,128)} %param.9, s32[4]{0:T(128)S(1)} %copy-done.3, s32[4]{0:T(128)S(1)} %copy-done.2), kind=kLoop, calls=%fused_computation.48 | loop fusion | flops 884736 | bytes 262176 | tf_op jit(solution)/shard_map/add | solution.py:225
  30.4 0.3 slice_reduce_fusion.3
  31.5 7.5 %shard_map.77 = (bf16[2048,128]{1,0:T(8,128)(2,1)S(1)}, f32[1024,128]{1,0:T(8,128)S(1)}) custom-call(f32[128,1024]{1,0:T(8,128)S(1)} %broadcast_dynamic-update-slice_fusion.p_ref), custom_call_target="tpu_custom_call" | custom-call | tf_op jit(solution)/shard_map/pallas_call | solution.py:30
  39.2 1.5 %shard_map.78 = (bf16[256,512]{1,0:T(8,128)(2,1)S(1)}, bf16[2048,256]{1,0:T(8,128)(2,1)S(1)}) custom-call(bf16[512,256]{1,0:T(8,128)(2,1)S(1)} %bitcast.105, bf16[2048,128]{1,0:T(8,128)(2,1)S(1)} %get-tuple-element.6.rd_ref, s32[4,512]{1,0:T(4,128)S(1)} %broadcast_add_fusion.idx_ref), custom_call_target="tpu_custom_call" | custom-call | tf_op jit(solution)/shard_map/pallas_call | solution.py:30
  41.0 3.2 %convolution_convert_fusion.1 = bf16[256,3584]{1,0:T(8,128)(2,1)S(1)} fusion(bf16[256,512]{1,0:T(8,128)(2,1)S(1)} %bitcast.115, bf16[512,7168]{1,0:T(8,128)(2,1)} %param.7), kind=kOutput, calls=%fused_computation.1 | convolution fusion | flops 940441600 | bytes 5767168 | tf_op jit(solution)/shard_map/dot_general | solution.py:235
  44.3 1.8 %collective-permute-start = (bf16[32,3584]{1,0:T(8,128)(2,1)S(1)}, bf16[32,3584]{1,0:T(8,128)(2,1)S(1)}, u32[]{:S(2)}, u32[]{:S(2)}) collective-permute-start(bf16[32,3584]{1,0:T(8,128)(2,1)S(1)} %get-tuple-element.20), channel_id=1, source_target_pairs={{0,16},{4,20},{8,24},{12,28},{16,32},{20,36},{24,40},{28,44},{32,4... | collective-permute-start | bytes 688136 | tf_op jit(solution)/shard_map/ppermute | solution.py:176
  46.1 1.8 %collective-permute-start.2 = (bf16[32,3584]{1,0:T(8,128)(2,1)S(1)}, bf16[32,3584]{1,0:T(8,128)(2,1)S(1)}, u32[]{:S(2)}, u32[]{:S(2)}) collective-permute-start(bf16[32,3584]{1,0:T(8,128)(2,1)S(1)} %get-tuple-element.21), channel_id=1, source_target_pairs={{0,48},{4,52},{8,56},{12,60},{16,0},{20,4},{24,8},{28,12},{32,16},... | collective-permute-start | bytes 688136 | tf_op jit(solution)/shard_map/ppermute | solution.py:176
  47.8 3.2 %convolution_convert_fusion = bf16[256,3584]{1,0:T(8,128)(2,1)S(1)} fusion(bf16[256,512]{1,0:T(8,128)(2,1)S(1)} %bitcast.118, bf16[512,7168]{1,0:T(8,128)(2,1)} %param.7), kind=kOutput, calls=%fused_computation | convolution fusion | flops 940441600 | bytes 5767168 | tf_op jit(solution)/shard_map/dot_general | solution.py:238
  51.3 1.9 %collective-permute-start.9 = (bf16[32,3584]{1,0:T(8,128)(2,1)S(1)}, bf16[32,3584]{1,0:T(8,128)(2,1)S(1)}, u32[]{:S(2)}, u32[]{:S(2)}) collective-permute-start(bf16[32,3584]{1,0:T(8,128)(2,1)S(1)} %get-tuple-element.27), channel_id=1, source_target_pairs={{0,12},{4,0},{8,4},{12,8},{16,28},{20,16},{24,20},{28,24},{32,44},... | collective-permute-start | bytes 688136 | tf_op jit(solution)/shard_map/ppermute | solution.py:176
  53.2 1.7 %collective-permute-start.15 = (bf16[512,256]{1,0:T(8,128)(2,1)S(1)}, bf16[512,256]{1,0:T(8,128)(2,1)S(1)}, u32[]{:S(2)}, u32[]{:S(2)}) collective-permute-start(bf16[512,256]{1,0:T(8,128)(2,1)S(1)} %add_convert_fusion.3), channel_id=1, source_target_pairs={{0,2},{1,3},{2,0},{3,1},{4,6},{5,7},{6,4},{7,5},{8,10},{9,11},{10,... | collective-permute-start | bytes 786440 | tf_op jit(solution)/shard_map/ppermute | solution.py:176
  55.0 0.8 pad_maximum_fusion
  56.2 0.8 pad_maximum_fusion.1
  57.0 1.6 %collective-permute-done.7 = bf16[32,3584]{1,0:T(8,128)(2,1)S(1)} collective-permute-done((bf16[32,3584]{1,0:T(8,128)(2,1)S(1)}, bf16[32,3584]{1,0:T(8,128)(2,1)S(1)}, u32[]{:S(2)}, u32[]{:S(2)}) %collective-permute-start.7) | collective-permute-done | bytes 229408 | tf_op jit(solution)/shard_map/ppermute | solution.py:176
  58.6 1.3 %collective-permute-done.9 = bf16[32,3584]{1,0:T(8,128)(2,1)S(1)} collective-permute-done((bf16[32,3584]{1,0:T(8,128)(2,1)S(1)}, bf16[32,3584]{1,0:T(8,128)(2,1)S(1)}, u32[]{:S(2)}, u32[]{:S(2)}) %collective-permute-start.9) | collective-permute-done | bytes 229408 | tf_op jit(solution)/shard_map/ppermute | solution.py:176
  60.0 0.8 pad_maximum_fusion.2
  61.0 2.6 %shard_map.79 = f32[4,4,32,128]{3,2,1,0:T(8,128)S(1)} custom-call(bf16[512,256]{1,0:T(8,128)(2,1)S(1)} %add_convert_fusion.2.up_ref, bf16[2048,256]{1,0:T(8,128)(2,1)S(1)} %get-tuple-element.8.moved_ref, bf16[2048,128]{1,0:T(8,128)(2,1)S(1)} %get-tuple-element.6.rd_ref, s32[4,512]{1,0:T(4,128)S(1)} %broadcast_add_fusion.idx_ref), custom_call_target="tpu_custom_call" | custom-call | tf_op jit(solution)/shard_map/pallas_call | solution.py:30
  63.6 3.3 %collective-permute-start.16 = (f32[4,2,32,128]{3,2,1,0:T(8,128)S(1)}, f32[4,2,32,128]{3,2,1,0:T(8,128)S(1)}, u32[]{:S(2)}, u32[]{:S(2)}) collective-permute-start(f32[4,2,32,128]{3,2,1,0:T(8,128)S(1)} %constant_dynamic-slice_fusion), channel_id=1, source_target_pairs={{0,64},{64,0},{1,65},{65,1},{2,66},{66,2},{3,67},{67,3},{4,68},{68... | collective-permute-start | bytes 393224 | tf_op jit(solution)/shard_map/ppermute | solution.py:176
  66.9 0.8 pad_maximum_fusion.3
  67.7 2.5 %collective-permute-done.16 = f32[4,2,32,128]{3,2,1,0:T(8,128)S(1)} collective-permute-done((f32[4,2,32,128]{3,2,1,0:T(8,128)S(1)}, f32[4,2,32,128]{3,2,1,0:T(8,128)S(1)}, u32[]{:S(2)}, u32[]{:S(2)}) %collective-permute-start.16) | collective-permute-done | bytes 131104 | tf_op jit(solution)/shard_map/ppermute | solution.py:176
  70.5 4.6 %collective-permute-start.17 = (f32[32,128]{1,0:T(8,128)S(1)}, f32[32,128]{1,0:T(8,128)S(1)}, u32[]{:S(2)}, u32[]{:S(2)}) collective-permute-start(f32[32,128]{1,0:T(8,128)S(1)} %get-tuple-element.40), channel_id=1, source_target_pairs={{0,0},{4,16},{8,32},{12,48},{16,4},{20,20},{24,36},{28,52},{32,8},... | collective-permute-start | bytes 49160 | tf_op jit(solution)/shard_map/ppermute | solution.py:176
  75.2 0.3 collective-permute-start.19
  75.5 4.5 %collective-permute-start.20 = (f32[32,128]{1,0:T(8,128)S(1)}, f32[32,128]{1,0:T(8,128)S(1)}, u32[]{:S(2)}, u32[]{:S(2)}) collective-permute-start(f32[32,128]{1,0:T(8,128)S(1)} %get-tuple-element.43), channel_id=1, source_target_pairs={{0,48},{4,0},{8,16},{12,32},{16,52},{20,4},{24,20},{28,36},{32,56}... | collective-permute-start | bytes 49160 | tf_op jit(solution)/shard_map/ppermute | solution.py:176
  80.0 0.9 collective-permute-start.3
  80.8 2.1 %collective-permute-start.8 = (bf16[64,3584]{1,0:T(8,128)(2,1)}, bf16[64,3584]{1,0:T(8,128)(2,1)S(1)}, u32[]{:S(2)}, u32[]{:S(2)}) collective-permute-start(bf16[64,3584]{1,0:T(8,128)(2,1)} %pad_maximum_fusion.2), channel_id=1, source_target_pairs={{0,4},{4,8},{8,12},{12,0},{16,20},{20,24},{24,28},{28,16},{32,36},... | collective-permute-start | bytes 1376264 | tf_op jit(solution)/shard_map/ppermute | solution.py:176
  83.0 1.7 %collective-permute-start.21 = (f32[32,128]{1,0:T(8,128)S(1)}, f32[32,128]{1,0:T(8,128)S(1)}, u32[]{:S(2)}, u32[]{:S(2)}) collective-permute-start(f32[32,128]{1,0:T(8,128)S(1)} %get-tuple-element.45), channel_id=1, source_target_pairs={{0,32},{4,0},{8,36},{12,4},{16,40},{20,8},{24,44},{28,12},{32,48},... | collective-permute-start | bytes 49160 | tf_op jit(solution)/shard_map/ppermute | solution.py:176
  84.6 4.3 %collective-permute-start.22 = (f32[32,128]{1,0:T(8,128)S(1)}, f32[32,128]{1,0:T(8,128)S(1)}, u32[]{:S(2)}, u32[]{:S(2)}) collective-permute-start(f32[32,128]{1,0:T(8,128)S(1)} %get-tuple-element.44), channel_id=1, source_target_pairs={{0,0},{4,32},{8,4},{12,36},{16,8},{20,40},{24,12},{28,44},{32,16},... | collective-permute-start | bytes 49160 | tf_op jit(solution)/shard_map/ppermute | solution.py:176
  89.0 0.6 collective-permute-done.21
  89.6 2.1 %collective-permute-start.10 = (bf16[64,3584]{1,0:T(8,128)(2,1)}, bf16[64,3584]{1,0:T(8,128)(2,1)S(1)}, u32[]{:S(2)}, u32[]{:S(2)}) collective-permute-start(bf16[64,3584]{1,0:T(8,128)(2,1)} %pad_maximum_fusion.3), channel_id=1, source_target_pairs={{0,12},{4,0},{8,4},{12,8},{16,28},{20,16},{24,20},{28,24},{32,44},... | collective-permute-start | bytes 1376264 | tf_op jit(solution)/shard_map/ppermute | solution.py:176
  91.9 5.6 %collective-permute-start.23 = (f32[2,32,128]{2,1,0:T(8,128)S(1)}, f32[2,32,128]{2,1,0:T(8,128)S(1)}, u32[]{:S(2)}, u32[]{:S(2)}) collective-permute-start(f32[2,32,128]{2,1,0:T(8,128)S(1)} %get-tuple-element.36), channel_id=1, source_target_pairs={{0,0},{4,8},{8,16},{12,24},{16,32},{20,40},{24,48},{28,56},{32,64}... | collective-permute-start | bytes 98312 | tf_op jit(solution)/shard_map/ppermute | solution.py:176
  97.6 4.1 %collective-permute-done.23 = f32[2,32,128]{2,1,0:T(8,128)S(1)} collective-permute-done((f32[2,32,128]{2,1,0:T(8,128)S(1)}, f32[2,32,128]{2,1,0:T(8,128)S(1)}, u32[]{:S(2)}, u32[]{:S(2)}) %collective-permute-start.23) | collective-permute-done | bytes 32800 | tf_op jit(solution)/shard_map/ppermute | solution.py:176
  101.7 2.1 %shard_map.80 = f32[8,32,128]{2,1,0:T(8,128)S(1)} custom-call(f32[8,32,128]{2,1,0:T(8,128)S(1)} %constant_dynamic-update-slice_fusion.2.g_ref, f32[1024,128]{1,0:T(8,128)S(1)} %get-tuple-element.9.ad_ref), custom_call_target="tpu_custom_call" | custom-call | tf_op jit(solution)/shard_map/pallas_call | solution.py:30
  104.2 0.9 reshape.186
  105.1 1.2 add_convert_fusion.1
  106.4 2.0 %collective-permute-start.5 = (bf16[16,3584]{1,0:T(8,128)(2,1)S(1)}, bf16[16,3584]{1,0:T(8,128)(2,1)S(1)}, u32[]{:S(2)}, u32[]{:S(2)}) collective-permute-start(bf16[16,3584]{1,0:T(8,128)(2,1)S(1)} %get-tuple-element.32), channel_id=1, source_target_pairs={{0,12},{4,0},{8,4},{12,8},{16,28},{20,16},{24,20},{28,24},{32,44},... | collective-permute-start | bytes 344072 | tf_op jit(solution)/shard_map/ppermute | solution.py:176
  108.4 1.2 add_convert_fusion
  109.6 3.6 %collective-permute-start.11 = (bf16[16,3584]{1,0:T(8,128)(2,1)S(1)}, bf16[16,3584]{1,0:T(8,128)(2,1)S(1)}, u32[]{:S(2)}, u32[]{:S(2)}) collective-permute-start(bf16[16,3584]{1,0:T(8,128)(2,1)S(1)} %get-tuple-element.33), channel_id=1, source_target_pairs={{0,16},{4,20},{8,24},{12,28},{16,32},{20,36},{24,40},{28,44},{32,4... | collective-permute-start | bytes 344072 | tf_op jit(solution)/shard_map/ppermute | solution.py:176
  113.2 3.1 %collective-permute-start.12 = (bf16[16,3584]{1,0:T(8,128)(2,1)S(1)}, bf16[16,3584]{1,0:T(8,128)(2,1)S(1)}, u32[]{:S(2)}, u32[]{:S(2)}) collective-permute-start(bf16[16,3584]{1,0:T(8,128)(2,1)S(1)} %get-tuple-element.35), channel_id=1, source_target_pairs={{0,48},{4,52},{8,56},{12,60},{16,0},{20,4},{24,8},{28,12},{32,16},... | collective-permute-start | bytes 344072 | tf_op jit(solution)/shard_map/ppermute | solution.py:176
  116.3 1.4 %collective-permute-start.13 = (bf16[16,3584]{1,0:T(8,128)(2,1)S(1)}, bf16[16,3584]{1,0:T(8,128)(2,1)S(1)}, u32[]{:S(2)}, u32[]{:S(2)}) collective-permute-start(bf16[16,3584]{1,0:T(8,128)(2,1)S(1)} %get-tuple-element.34), channel_id=1, source_target_pairs={{0,32},{4,36},{8,40},{12,44},{16,48},{20,52},{24,56},{28,60},{32,0... | collective-permute-start | bytes 344072 | tf_op jit(solution)/shard_map/ppermute | solution.py:176
  117.8 1.2 collective-permute-done.11
  119.0 3.6 %collective-permute-done.13 = bf16[16,3584]{1,0:T(8,128)(2,1)S(1)} collective-permute-done((bf16[16,3584]{1,0:T(8,128)(2,1)S(1)}, bf16[16,3584]{1,0:T(8,128)(2,1)S(1)}, u32[]{:S(2)}, u32[]{:S(2)}) %collective-permute-start.13) | collective-permute-done | bytes 114720 | tf_op jit(solution)/shard_map/ppermute | solution.py:176
  122.7 0.7 pad_maximum_fusion.4
  (82 shorter events, 3.5 us)
Async XLA Ops:
  2.4 36.8 %all-to-all-start = ((bf16[16,32,256]{2,1,0:T(8,128)(2,1)}), bf16[16,32,256]{2,1,0:T(8,128)(2,1)S(1)}, u32[]{:S(2)}, u32[]{:S(2)}) async-start(bf16[16,32,256]{2,1,0:T(8,128)(2,1)} %bitcast.1), calls=%async_computation | async-start | bytes 524288 | tf_op jit(solution)/shard_map/all_to_all | solution.py:205
  17.0 36.2 %collective-permute-start.14 = (bf16[512,256]{1,0:T(8,128)(2,1)S(1)}, bf16[512,256]{1,0:T(8,128)(2,1)S(1)}, u32[]{:S(2)}, u32[]{:S(2)}) collective-permute-start(bf16[512,256]{1,0:T(8,128)(2,1)S(1)} %convolution_convert_fusion.2), channel_id=1, source_target_pairs={{0,1},{1,0},{2,3},{3,2},{4,5},{5,4},{6,7},{7,6},{8,9},{9,8},{10,11... | collective-permute-start | bytes 786440 | tf_op jit(solution)/shard_map/ppermute | solution.py:176
  17.2 7.0 %copy-start.2 = (s32[4]{0:T(128)S(1)}, s32[4]{0:T(128)}, u32[]{:S(2)}) copy-start(s32[4]{0:T(128)} %constant.230) | copy-start | bytes 52
  17.3 7.0 %copy-start.3 = (s32[4]{0:T(128)S(1)}, s32[4]{0:T(128)}, u32[]{:S(2)}) copy-start(s32[4]{0:T(128)} %constant.246) | copy-start | bytes 52
  44.2 10.7 %copy-start.1 = (bf16[256,3584]{1,0:T(8,128)(2,1)}, bf16[256,3584]{1,0:T(8,128)(2,1)S(1)}, u32[]{:S(2)}) copy-start(bf16[256,3584]{1,0:T(8,128)(2,1)S(1)} %convolution_convert_fusion.1) | copy-start | bytes 5505028
  44.3 10.6 %collective-permute-start = (bf16[32,3584]{1,0:T(8,128)(2,1)S(1)}, bf16[32,3584]{1,0:T(8,128)(2,1)S(1)}, u32[]{:S(2)}, u32[]{:S(2)}) collective-permute-start(bf16[32,3584]{1,0:T(8,128)(2,1)S(1)} %get-tuple-element.20), channel_id=1, source_target_pairs={{0,16},{4,20},{8,24},{12,28},{16,32},{20,36},{24,40},{28,44},{32,4... | collective-permute-start | bytes 688136 | tf_op jit(solution)/shard_map/ppermute | solution.py:176
  46.1 8.9 %collective-permute-start.2 = (bf16[32,3584]{1,0:T(8,128)(2,1)S(1)}, bf16[32,3584]{1,0:T(8,128)(2,1)S(1)}, u32[]{:S(2)}, u32[]{:S(2)}) collective-permute-start(bf16[32,3584]{1,0:T(8,128)(2,1)S(1)} %get-tuple-element.21), channel_id=1, source_target_pairs={{0,48},{4,52},{8,56},{12,60},{16,0},{20,4},{24,8},{28,12},{32,16},... | collective-permute-start | bytes 688136 | tf_op jit(solution)/shard_map/ppermute | solution.py:176
  51.0 9.8 %copy-start = (bf16[256,3584]{1,0:T(8,128)(2,1)}, bf16[256,3584]{1,0:T(8,128)(2,1)S(1)}, u32[]{:S(2)}) copy-start(bf16[256,3584]{1,0:T(8,128)(2,1)S(1)} %convolution_convert_fusion) | copy-start | bytes 5505028
  51.1 7.5 %collective-permute-start.7 = (bf16[32,3584]{1,0:T(8,128)(2,1)S(1)}, bf16[32,3584]{1,0:T(8,128)(2,1)S(1)}, u32[]{:S(2)}, u32[]{:S(2)}) collective-permute-start(bf16[32,3584]{1,0:T(8,128)(2,1)S(1)} %get-tuple-element.26), channel_id=1, source_target_pairs={{0,4},{4,8},{8,12},{12,0},{16,20},{20,24},{24,28},{28,16},{32,36},... | collective-permute-start | bytes 688136 | tf_op jit(solution)/shard_map/ppermute | solution.py:176
  51.3 8.6 %collective-permute-start.9 = (bf16[32,3584]{1,0:T(8,128)(2,1)S(1)}, bf16[32,3584]{1,0:T(8,128)(2,1)S(1)}, u32[]{:S(2)}, u32[]{:S(2)}) collective-permute-start(bf16[32,3584]{1,0:T(8,128)(2,1)S(1)} %get-tuple-element.27), channel_id=1, source_target_pairs={{0,12},{4,0},{8,4},{12,8},{16,28},{20,16},{24,20},{28,24},{32,44},... | collective-permute-start | bytes 688136 | tf_op jit(solution)/shard_map/ppermute | solution.py:176
  53.2 7.7 %collective-permute-start.15 = (bf16[512,256]{1,0:T(8,128)(2,1)S(1)}, bf16[512,256]{1,0:T(8,128)(2,1)S(1)}, u32[]{:S(2)}, u32[]{:S(2)}) collective-permute-start(bf16[512,256]{1,0:T(8,128)(2,1)S(1)} %add_convert_fusion.3), channel_id=1, source_target_pairs={{0,2},{1,3},{2,0},{3,1},{4,6},{5,7},{6,4},{7,5},{8,10},{9,11},{10,... | collective-permute-start | bytes 786440 | tf_op jit(solution)/shard_map/ppermute | solution.py:176
  55.9 49.2 %collective-permute-start.1 = (bf16[64,3584]{1,0:T(8,128)(2,1)}, bf16[64,3584]{1,0:T(8,128)(2,1)S(1)}, u32[]{:S(2)}, u32[]{:S(2)}) collective-permute-start(bf16[64,3584]{1,0:T(8,128)(2,1)} %pad_maximum_fusion), channel_id=1, source_target_pairs={{0,16},{4,20},{8,24},{12,28},{16,32},{20,36},{24,40},{28,44},{32,4... | collective-permute-start | bytes 1376264 | tf_op jit(solution)/shard_map/ppermute | solution.py:176
  63.6 6.6 %collective-permute-start.16 = (f32[4,2,32,128]{3,2,1,0:T(8,128)S(1)}, f32[4,2,32,128]{3,2,1,0:T(8,128)S(1)}, u32[]{:S(2)}, u32[]{:S(2)}) collective-permute-start(f32[4,2,32,128]{3,2,1,0:T(8,128)S(1)} %constant_dynamic-slice_fusion), channel_id=1, source_target_pairs={{0,64},{64,0},{1,65},{65,1},{2,66},{66,2},{3,67},{67,3},{4,68},{68... | collective-permute-start | bytes 393224 | tf_op jit(solution)/shard_map/ppermute | solution.py:176
  70.5 9.5 %collective-permute-start.17 = (f32[32,128]{1,0:T(8,128)S(1)}, f32[32,128]{1,0:T(8,128)S(1)}, u32[]{:S(2)}, u32[]{:S(2)}) collective-permute-start(f32[32,128]{1,0:T(8,128)S(1)} %get-tuple-element.40), channel_id=1, source_target_pairs={{0,0},{4,16},{8,32},{12,48},{16,4},{20,20},{24,36},{28,52},{32,8},... | collective-permute-start | bytes 49160 | tf_op jit(solution)/shard_map/ppermute | solution.py:176
  75.1 5.7 %collective-permute-start.18 = (f32[32,128]{1,0:T(8,128)S(1)}, f32[32,128]{1,0:T(8,128)S(1)}, u32[]{:S(2)}, u32[]{:S(2)}) collective-permute-start(f32[32,128]{1,0:T(8,128)S(1)} %get-tuple-element.41), channel_id=1, source_target_pairs={{0,16},{4,32},{8,48},{12,0},{16,20},{20,36},{24,52},{28,4},{32,24}... | collective-permute-start | bytes 49160 | tf_op jit(solution)/shard_map/ppermute | solution.py:176
  75.2 7.8 %collective-permute-start.19 = (f32[32,128]{1,0:T(8,128)S(1)}, f32[32,128]{1,0:T(8,128)S(1)}, u32[]{:S(2)}, u32[]{:S(2)}) collective-permute-start(f32[32,128]{1,0:T(8,128)S(1)} %get-tuple-element.42), channel_id=1, source_target_pairs={{0,32},{4,48},{8,0},{12,16},{16,36},{20,52},{24,4},{28,20},{32,40}... | collective-permute-start | bytes 49160 | tf_op jit(solution)/shard_map/ppermute | solution.py:176
  75.5 9.1 %collective-permute-start.20 = (f32[32,128]{1,0:T(8,128)S(1)}, f32[32,128]{1,0:T(8,128)S(1)}, u32[]{:S(2)}, u32[]{:S(2)}) collective-permute-start(f32[32,128]{1,0:T(8,128)S(1)} %get-tuple-element.43), channel_id=1, source_target_pairs={{0,48},{4,0},{8,16},{12,32},{16,52},{20,4},{24,20},{28,36},{32,56}... | collective-permute-start | bytes 49160 | tf_op jit(solution)/shard_map/ppermute | solution.py:176
  80.0 25.1 %collective-permute-start.3 = (bf16[64,3584]{1,0:T(8,128)(2,1)}, bf16[64,3584]{1,0:T(8,128)(2,1)S(1)}, u32[]{:S(2)}, u32[]{:S(2)}) collective-permute-start(bf16[64,3584]{1,0:T(8,128)(2,1)} %pad_maximum_fusion.1), channel_id=1, source_target_pairs={{0,48},{4,52},{8,56},{12,60},{16,0},{20,4},{24,8},{28,12},{32,16},... | collective-permute-start | bytes 1376264 | tf_op jit(solution)/shard_map/ppermute | solution.py:176
  80.8 27.6 %collective-permute-start.8 = (bf16[64,3584]{1,0:T(8,128)(2,1)}, bf16[64,3584]{1,0:T(8,128)(2,1)S(1)}, u32[]{:S(2)}, u32[]{:S(2)}) collective-permute-start(bf16[64,3584]{1,0:T(8,128)(2,1)} %pad_maximum_fusion.2), channel_id=1, source_target_pairs={{0,4},{4,8},{8,12},{12,0},{16,20},{20,24},{24,28},{28,16},{32,36},... | collective-permute-start | bytes 1376264 | tf_op jit(solution)/shard_map/ppermute | solution.py:176
  83.0 6.6 %collective-permute-start.21 = (f32[32,128]{1,0:T(8,128)S(1)}, f32[32,128]{1,0:T(8,128)S(1)}, u32[]{:S(2)}, u32[]{:S(2)}) collective-permute-start(f32[32,128]{1,0:T(8,128)S(1)} %get-tuple-element.45), channel_id=1, source_target_pairs={{0,32},{4,0},{8,36},{12,4},{16,40},{20,8},{24,44},{28,12},{32,48},... | collective-permute-start | bytes 49160 | tf_op jit(solution)/shard_map/ppermute | solution.py:176
  84.6 7.3 %collective-permute-start.22 = (f32[32,128]{1,0:T(8,128)S(1)}, f32[32,128]{1,0:T(8,128)S(1)}, u32[]{:S(2)}, u32[]{:S(2)}) collective-permute-start(f32[32,128]{1,0:T(8,128)S(1)} %get-tuple-element.44), channel_id=1, source_target_pairs={{0,0},{4,32},{8,4},{12,36},{16,8},{20,40},{24,12},{28,44},{32,16},... | collective-permute-start | bytes 49160 | tf_op jit(solution)/shard_map/ppermute | solution.py:176
  89.6 18.8 %collective-permute-start.10 = (bf16[64,3584]{1,0:T(8,128)(2,1)}, bf16[64,3584]{1,0:T(8,128)(2,1)S(1)}, u32[]{:S(2)}, u32[]{:S(2)}) collective-permute-start(bf16[64,3584]{1,0:T(8,128)(2,1)} %pad_maximum_fusion.3), channel_id=1, source_target_pairs={{0,12},{4,0},{8,4},{12,8},{16,28},{20,16},{24,20},{28,24},{32,44},... | collective-permute-start | bytes 1376264 | tf_op jit(solution)/shard_map/ppermute | solution.py:176
  91.9 9.8 %collective-permute-start.23 = (f32[2,32,128]{2,1,0:T(8,128)S(1)}, f32[2,32,128]{2,1,0:T(8,128)S(1)}, u32[]{:S(2)}, u32[]{:S(2)}) collective-permute-start(f32[2,32,128]{2,1,0:T(8,128)S(1)} %get-tuple-element.36), channel_id=1, source_target_pairs={{0,0},{4,8},{8,16},{12,24},{16,32},{20,40},{24,48},{28,56},{32,64}... | collective-permute-start | bytes 98312 | tf_op jit(solution)/shard_map/ppermute | solution.py:176
  106.3 10.0 %collective-permute-start.4 = (bf16[16,3584]{1,0:T(8,128)(2,1)S(1)}, bf16[16,3584]{1,0:T(8,128)(2,1)S(1)}, u32[]{:S(2)}, u32[]{:S(2)}) collective-permute-start(bf16[16,3584]{1,0:T(8,128)(2,1)S(1)} %get-tuple-element.30), channel_id=1, source_target_pairs={{0,4},{4,8},{8,12},{12,0},{16,20},{20,24},{24,28},{28,16},{32,36},... | collective-permute-start | bytes 344072 | tf_op jit(solution)/shard_map/ppermute | solution.py:176
  106.4 11.3 %collective-permute-start.5 = (bf16[16,3584]{1,0:T(8,128)(2,1)S(1)}, bf16[16,3584]{1,0:T(8,128)(2,1)S(1)}, u32[]{:S(2)}, u32[]{:S(2)}) collective-permute-start(bf16[16,3584]{1,0:T(8,128)(2,1)S(1)} %get-tuple-element.32), channel_id=1, source_target_pairs={{0,12},{4,0},{8,4},{12,8},{16,28},{20,16},{24,20},{28,24},{32,44},... | collective-permute-start | bytes 344072 | tf_op jit(solution)/shard_map/ppermute | solution.py:176
  108.4 9.3 %collective-permute-start.6 = (bf16[16,3584]{1,0:T(8,128)(2,1)S(1)}, bf16[16,3584]{1,0:T(8,128)(2,1)S(1)}, u32[]{:S(2)}, u32[]{:S(2)}) collective-permute-start(bf16[16,3584]{1,0:T(8,128)(2,1)S(1)} %get-tuple-element.31), channel_id=1, source_target_pairs={{0,8},{4,12},{8,0},{12,4},{16,24},{20,28},{24,16},{28,20},{32,40},... | collective-permute-start | bytes 344072 | tf_op jit(solution)/shard_map/ppermute | solution.py:176
  109.6 9.4 %collective-permute-start.11 = (bf16[16,3584]{1,0:T(8,128)(2,1)S(1)}, bf16[16,3584]{1,0:T(8,128)(2,1)S(1)}, u32[]{:S(2)}, u32[]{:S(2)}) collective-permute-start(bf16[16,3584]{1,0:T(8,128)(2,1)S(1)} %get-tuple-element.33), channel_id=1, source_target_pairs={{0,16},{4,20},{8,24},{12,28},{16,32},{20,36},{24,40},{28,44},{32,4... | collective-permute-start | bytes 344072 | tf_op jit(solution)/shard_map/ppermute | solution.py:176
  113.2 5.8 %collective-permute-start.12 = (bf16[16,3584]{1,0:T(8,128)(2,1)S(1)}, bf16[16,3584]{1,0:T(8,128)(2,1)S(1)}, u32[]{:S(2)}, u32[]{:S(2)}) collective-permute-start(bf16[16,3584]{1,0:T(8,128)(2,1)S(1)} %get-tuple-element.35), channel_id=1, source_target_pairs={{0,48},{4,52},{8,56},{12,60},{16,0},{20,4},{24,8},{28,12},{32,16},... | collective-permute-start | bytes 344072 | tf_op jit(solution)/shard_map/ppermute | solution.py:176
  116.3 6.3 %collective-permute-start.13 = (bf16[16,3584]{1,0:T(8,128)(2,1)S(1)}, bf16[16,3584]{1,0:T(8,128)(2,1)S(1)}, u32[]{:S(2)}, u32[]{:S(2)}) collective-permute-start(bf16[16,3584]{1,0:T(8,128)(2,1)S(1)} %get-tuple-element.34), channel_id=1, source_target_pairs={{0,32},{4,36},{8,40},{12,44},{16,48},{20,52},{24,56},{28,60},{32,0... | collective-permute-start | bytes 344072 | tf_op jit(solution)/shard_map/ppermute | solution.py:176

commit v2 on v1

v2 whole, which is shorter than its diff:
```python
import functools

import jax
import jax.numpy as jnp
from jax import lax
from jax.experimental import pallas as pl
from jax.experimental.pallas import tpu as pltpu
from jax.sharding import PartitionSpec as P

BLOCK = 32
FACTORS = 4
RUN = 16
LANES = 128
BF = jnp.bfloat16
F32 = jnp.float32
HI = lax.Precision.HIGHEST


def iota(shape, dim):
    return lax.broadcasted_iota(jnp.int32, shape, dim)


def dot(a, b, ca, cb, precision=None):
    return lax.dot_general(
        a, b, (((ca,), (cb,)), ((), ())), precision=precision, preferred_element_type=F32
    )


def call(body, out_shape, args, scratch=(), limit=12 << 20):
    return pl.pallas_call(
        body,
        out_shape=out_shape,
        in_specs=[pl.BlockSpec(memory_space=pltpu.VMEM)] * len(args),
        out_specs=jax.tree.map(lambda _: pl.BlockSpec(memory_space=pltpu.VMEM), out_shape),
        scratch_shapes=list(scratch),
        compiler_params=pltpu.CompilerParams(vmem_limit_bytes=limit),
    )(*args)


def shape(dims, dtype):
    return jax.ShapeDtypeStruct(dims, dtype)


def far(x):
    return pltpu.with_memory_space_constraint(x, pltpu.HBM)


def prepare_body(
    params, perms, rot_ref, inv_ref, idx_ref, fetched, chosen, turned, mat, rows, perm_ref, sem, perm_sem
):
    f = lax.axis_index("fsdp")
    d = lax.axis_index("dp")
    copies = []

    def pull(level, start, count, to):
        source = params.at[level, pl.ds(pl.multiple_of(start, 8), count)]
        copies.append(pltpu.make_async_copy(source, fetched.at[pl.ds(to, count)], sem))

    for h in range(8):
        pull(0, h * 32 + f // 4 * 8, 8, h * 8)
    for g in range(4):
        pull(1, g * 64 + f // 2 * 8, 8, 64 + g * 8)
    for g in range(2):
        pull(2, g * 128 + f * 8, 8, 96 + g * 8)
    pull(3, f * 16, 16, 112)
    for level in range(FACTORS):
        pull(level, (d * 16 + f) * 8, 8, 128 + level * 8)
    for copy in copies:
        copy.start()
    perm_copy = pltpu.make_async_copy(perms, perm_ref, perm_sem)
    perm_copy.start()
    perm_copy.wait()

    lane = iota((1, LANES), 1)
    odd = f % 2 == 1
    half = f // 2 * LANES

    def window(level, start):
        return perm_ref[level : level + 1, pl.ds(pl.multiple_of(start, LANES), LANES)]

    for level in range(FACTORS):
        for g in range(4):
            if level == 0:
                left = window(0, 2 * g * 1024 + half)
                right = window(0, (2 * g + 1) * 1024 + half)
                left = jnp.where(odd, pltpu.roll(left, 64, 1), left)
                right = jnp.where(odd, right, pltpu.roll(right, 64, 1))
                value = jnp.where(lane < 64, left, right)
            elif level == 1:
                value = window(1, g * 2048 + f * 128)
            elif level == 2:
                value = window(2, g // 2 * 4096 + f * 256 + g % 2 * LANES)
            else:
                value = window(3, f * 512 + g * LANES)
            sigma = (value >> (9 + level) & 1) * RUN + (value & (RUN - 1))
            idx_ref[level * 4 + g : level * 4 + g + 1, :] = sigma + lane // BLOCK * BLOCK

    for copy in copies:
        copy.wait()
    for h in range(8):
        rows8 = fetched[h * 8 : h * 8 + 8, :]
        pair = rows8[:2]
        for s in range(1, 4):
            pair = jnp.where(f % 4 == s, rows8[2 * s : 2 * s + 2], pair)
        chosen[2 * h : 2 * h + 2, :] = pair
    for g in range(4):
        rows8 = fetched[64 + g * 8 : 72 + g * 8, :]
        chosen[16 + 4 * g : 20 + 4 * g, :] = jnp.where(odd, rows8[4:], rows8[:4])
    chosen[32:96, :] = fetched[96:160, :]
    chosen[96:, :] = fetched[:32, :]
    turned[...] = chosen[...].T
    sub = iota((BLOCK, LANES), 0)
    for i in range(BLOCK):
        skew = turned[i * BLOCK : (i + 1) * BLOCK, :] - turned[pl.ds(i, BLOCK, stride=BLOCK), :]
        mat[i] = jnp.where(sub == i, 1.0, 0.0) - skew

    def step(k, carry):
        here = sub == k
        pivot = 1.0 / mat[k, pl.ds(k, 1), :]
        line = jnp.where(here, pivot, mat[k] * pivot)
        for i in range(BLOCK):
            factor = mat[i, pl.ds(k, 1), :]
            mat[i] = jnp.where(here, 0.0, mat[i]) - factor * line
        mat[k] = line
        return carry

    lax.fori_loop(0, BLOCK, step, 0)
    for i in range(BLOCK):
        rows[pl.ds(i, LANES, stride=BLOCK), :] = mat[i].T
    same = iota((LANES, LANES), 0) // BLOCK == iota((LANES, LANES), 1) // BLOCK
    unit = jnp.where(iota((LANES, LANES), 0) == iota((LANES, LANES), 1), 1.0, 0.0)
    for g in range(24):
        piece = rows[g * LANES : (g + 1) * LANES, :]
        wide = jnp.where(same, jnp.concatenate([piece] * 4, axis=1), 0.0)
        if g < 16:
            rotation = (2.0 * wide - unit).astype(BF)
            rot_ref[g * LANES : (g + 1) * LANES, :] = dot(onehot(idx_ref, g), rotation, 1, 0).astype(BF)
        else:
            inv_ref[(g - 16) * LANES : (g - 15) * LANES, :] = wide


def onehot(idx_ref, g):
    return jnp.where(iota((LANES, LANES), 0) == idx_ref[g : g + 1, :], 1.0, 0.0).astype(BF)


def shuffle(x, level):
    groups = 16 >> level
    width = 512 // groups
    pieces = []
    for h in range(groups // 2):
        for i in range(width // RUN):
            for half in range(2):
                start = (2 * h + half) * width + i * RUN
                pieces.append(x[start : start + RUN])
    return jnp.concatenate(pieces, axis=0)


def unshuffle(x, level):
    groups = 16 >> level
    width = 512 // groups
    count = width // RUN
    pieces = []
    for a in range(groups):
        for i in range(count):
            start = ((a // 2) * count + i) * BLOCK + (a % 2) * RUN
            pieces.append(x[start : start + RUN])
    return jnp.concatenate(pieces, axis=0)


def forward_body(
    x_ref, rot_ref, weight, cotan, *rest, tiles
):
    parts, up_ref, saved_ref = rest[:4], rest[4], rest[5]
    w_ref, c_ref, out_ref, staged, w_sems, c_sem, p_sem = rest[6:]
    tile = weight.shape[1] // tiles
    fetches = []
    for i in range(tiles):
        span = pl.ds(i * tile, tile)
        fetches.append(pltpu.make_async_copy(weight.at[:, span], w_ref.at[:, span], w_sems.at[i]))
    fetches.append(pltpu.make_async_copy(cotan, c_ref, c_sem))
    for fetch in fetches:
        fetch.start()

    f = lax.axis_index("fsdp")
    z, x_own = f // 4, f % 4
    second = lax.axis_index("tensor") % 2 == 1
    x = x_ref[...]
    for level in range(FACTORS):
        x = shuffle(x, level)
        saved_ref[level] = x
        outs = []
        for g in range(4):
            rot = rot_ref[(level * 4 + g) * LANES : (level * 4 + g + 1) * LANES, :]
            mine = x[g * LANES : (g + 1) * LANES]
            if level < FACTORS - 1:
                outs.append(dot(rot, mine, 0, 0).astype(BF))
            else:
                outs.append(dot(mine, rot, 0, 0).astype(BF))
        x = jnp.concatenate(outs, axis=0 if level < FACTORS - 1 else 1)
    for block in range(16):
        dz, dx = (block // 4 - z + 4) % 4, (block % 4 - x_own + 4) % 4
        slot = jnp.where(second, dx * 4 + dz, dz * 4 + dx)
        out_ref[pl.ds(pl.multiple_of(slot * RUN, RUN), RUN), :] = x[block * RUN : (block + 1) * RUN]

    copies = []
    for i in range(tiles):
        span = pl.ds(i * tile, tile)
        fetches[i].wait()
        staged[i] = dot(out_ref[...], w_ref[:, span], 1, 0).astype(BF)
        for s in range(4):
            copy = pltpu.make_async_copy(staged.at[i, pl.ds(s * 64, 64)], parts[s].at[:, span], p_sem)
            copy.start()
            copies.append(copy)
    fetches[tiles].wait()
    up_ref[...] = dot(w_ref[...], c_ref[...], 1, 1).astype(BF)
    for copy in copies:
        copy.wait()


def forward(mixed, rot, weight, cotangent, tiles=7):
    depth, tokens = mixed.shape
    columns = weight.shape[1]
    vmem = pl.BlockSpec(memory_space=pltpu.VMEM)
    hbm = pl.BlockSpec(memory_space=pltpu.HBM)
    return pl.pallas_call(
        functools.partial(forward_body, tiles=tiles),
        out_shape=[pltpu.HBM((tokens // 4, columns), BF)] * 4
        + [shape((depth, tokens), BF), shape((FACTORS, depth, tokens), BF)],
        in_specs=[vmem, vmem, hbm, hbm],
        out_specs=[hbm] * 4 + [vmem] * 2,
        scratch_shapes=[
            pltpu.VMEM((depth, columns), BF),
            pltpu.VMEM((tokens, columns), BF),
            pltpu.VMEM((tokens, depth), BF),
            pltpu.VMEM((tiles, tokens, columns // tiles), BF),
            pltpu.SemaphoreType.DMA((tiles,)),
            pltpu.SemaphoreType.DMA,
            pltpu.SemaphoreType.DMA,
        ],
        compiler_params=pltpu.CompilerParams(vmem_limit_bytes=32 << 20),
    )(mixed, rot, far(weight), far(cotangent))


def backward_body(up_ref, saved_ref, rot_ref, idx_ref, grad_ref):
    d = lax.axis_index("dp")
    up = up_ref[...]
    same = iota((LANES, LANES), 0) // BLOCK == iota((LANES, LANES), 1) // BLOCK
    for level in reversed(range(FACTORS)):
        outs = []
        for g in range(4):
            base = (level * 4 + g) * LANES
            mine = up[g * LANES : (g + 1) * LANES]
            x = saved_ref[level, g * LANES : (g + 1) * LANES, :]
            moved = dot(onehot(idx_ref, level * 4 + g), x, 0, 0).astype(BF)
            outer = jnp.where(same, dot(moved, mine, 1, 1), 0.0)
            packed = outer[:BLOCK] + outer[BLOCK : 2 * BLOCK]
            packed = packed + outer[2 * BLOCK : 3 * BLOCK] + outer[3 * BLOCK :]
            grad_ref[(g // 2 + d) % 2, level, g % 2] = packed
            if level > 0:
                outs.append(dot(rot_ref[base : base + LANES, :], mine, 1, 0).astype(BF))
        if level > 0:
            up = unshuffle(jnp.concatenate(outs, axis=0), level)


def pull_body(g_ref, ad_ref, out_ref):
    same = iota((LANES, LANES), 0) // BLOCK == iota((LANES, LANES), 1) // BLOCK
    for g in range(8):
        grad = jnp.where(same, jnp.concatenate([g_ref[g]] * 4, axis=0), 0.0)
        inv = ad_ref[g * LANES : (g + 1) * LANES, :]
        both = 2.0 * dot(dot(inv, grad, 0, 0, HI), inv, 1, 1, HI)
        both = both - both.T
        packed = both[:BLOCK] + both[BLOCK : 2 * BLOCK]
        out_ref[g] = packed + both[2 * BLOCK : 3 * BLOCK] + both[3 * BLOCK :]


def ring_pairs(stage, s):
    pairs = []
    for f in range(16):
        for t in range(4):
            z, x = f // 4, f % 4
            if (t % 2) ^ stage:
                x = (x + s) % 4
            else:
                z = (z + s) % 4
            pairs.append((f * 4 + t, (z * 4 + x) * 4 + t))
    return pairs


def ring(x, stage, s):
    return lax.ppermute(x, ("fsdp", "tensor"), ring_pairs(stage, s))


def local(activations, frozen_weight, cayley_params, permutations, cotangent):
    tokens = activations.shape[0]
    mixed = lax.all_to_all(
        activations.T.reshape(16, BLOCK, tokens), "fsdp", 0, 0, tiled=True
    ).reshape(512, tokens)

    rot, inv, idx = pl.pallas_call(
        prepare_body,
        out_shape=(shape((2048, LANES), BF), shape((1024, LANES), F32), shape((16, LANES), jnp.int32)),
        in_specs=[pl.BlockSpec(memory_space=pl.ANY)] * 2,
        out_specs=(pl.BlockSpec(memory_space=pltpu.VMEM),) * 3,
        scratch_shapes=[
            pltpu.VMEM((160, BLOCK * BLOCK), F32),
            pltpu.VMEM((LANES, BLOCK * BLOCK), F32),
            pltpu.VMEM((BLOCK * BLOCK, LANES), F32),
            pltpu.VMEM((BLOCK, BLOCK, LANES), F32),
            pltpu.VMEM((BLOCK * LANES, BLOCK), F32),
            pltpu.VMEM((FACTORS, 8192), jnp.int32),
            pltpu.SemaphoreType.DMA,
            pltpu.SemaphoreType.DMA,
        ],
        compiler_params=pltpu.CompilerParams(vmem_limit_bytes=12 << 20),
    )(far(cayley_params), far(permutations))

    *parts, up, saved = forward(mixed, rot, frozen_weight, cotangent)
    near, back, across = [ring(parts[s], 0, s) for s in (1, 3, 2)]

    for bit in (1, 2):
        other = lax.ppermute(up, "tensor", [(t, t ^ bit) for t in range(4)])
        up = (up.astype(F32) + other).astype(BF)
    grads = call(
        backward_body, shape((2, FACTORS, 2, BLOCK, LANES), F32), (up, saved, rot, idx)
    )
    grads = grads[0] + lax.ppermute(grads[1], "dp", [(0, 1), (1, 0)])
    grads, near, back = lax.optimization_barrier((grads, near, back))

    f = lax.axis_index("fsdp")
    level3 = lax.ppermute(
        grads[3],
        ("dp", "fsdp"),
        [(e * 16 + s, s // 8 * 16 + s % 8 * 2 + e) for e in range(2) for s in range(16)],
    )
    spots = grads[0].reshape(2, BLOCK, 2, 64).transpose(0, 2, 1, 3).reshape(4, BLOCK, 64)
    odd = f % 2 == 1
    spots = jnp.concatenate([jnp.where(odd, 0.0, spots), jnp.where(odd, spots, 0.0)], axis=2)
    slots = jnp.stack([jnp.repeat(spots, 4, axis=0), jnp.repeat(grads[1], 8, axis=0)], axis=1)
    slots = lax.all_to_all(slots.astype(BF), "fsdp", 0, 0, tiled=True)

    across, level3 = lax.optimization_barrier((across, level3))
    parts = [parts[0], near, back, across]
    wide = [sum(p[k * RUN : (k + 1) * RUN].astype(F32) for p in parts).astype(BF) for k in range(4)]
    last = [ring(wide[s], 1, s) for s in (2, 1, 3)]

    level0 = lax.dynamic_slice_in_dim(slots[:, 0], f % 4 * 4, 4, 0).astype(F32)
    level0 = level0.reshape(2, 2, BLOCK, LANES).sum(1)
    level1 = lax.dynamic_slice_in_dim(slots[:, 1], f % 8 * 2, 2, 0).astype(F32)
    owned = jnp.concatenate([level0, level1, grads[2], level3], axis=0)
    pulled = call(pull_body, shape((8, BLOCK, LANES), F32), (owned, inv))
    param_grads = (
        pulled.reshape(FACTORS, 2, BLOCK, 4, BLOCK)
        .transpose(0, 1, 3, 2, 4)
        .reshape(FACTORS, 8, BLOCK * BLOCK)
    )
    param_grads, last = lax.optimization_barrier((param_grads, last))
    projected = sum(p.astype(F32) for p in [wide[0]] + last).astype(BF)
    return (projected, param_grads)


def solution(mesh):
    return jax.shard_map(
        local,
        mesh=mesh,
        in_specs=(P("dp", "fsdp"), P("fsdp", "tensor"), P(), P(), P("dp", "tensor")),
        out_specs=(P(("dp", "fsdp"), "tensor"), P(None, ("dp", "fsdp"), None)),
        check_vma=False,
    )
```

time: 125 us -> 85.6 us (0.68)
  matrix products: 12.6 us -> 0 us
  starting transfers between devices: 55.7 us -> 44.3 us
  local copies, waits for them, and re-layouts: 11.2 us -> 3.28 us
  Pallas kernels: 13.7 us -> 21.6 us
  other arithmetic: 13.5 us -> 5.7 us
  waiting for transfers between devices: 15.3 us -> 9.48 us
    ppermute x24 -> x10, starting transfers between devices: 47.4 us -> 18.4 us  [the longest x6 9.75 us: ring(): return lax.ppermute(x, ('fsdp', 'tensor'), ring_pairs(stage, s))]
    all_to_all x0 -> x1, starting transfers between devices: none -> 17.6 us  [local(): slots = lax.all_to_all(slots.astype(BF), 'fsdp', 0, 0, tiled=True)]
    pallas_call x0 -> x2, Pallas kernels: none -> 17.2 us  [the longest x1 8.92 us: local(): pl.pallas_call(prepare_body, out_shape=(shape((2048, LANES), BF), shape((...]
    dot_general x3 -> x0, matrix products: 12.6 us -> none  [the longest x1 6.27 us: dot(): lax.dot_general(a, b, (((ca,), (cb,)), ((), ())), precision=precision, pr...]
    pallas_call x4 -> x2, Pallas kernels: 13.7 us -> 4.41 us  [call(): pl.pallas_call(body, out_shape=out_shape, in_specs=[pl.BlockSpec(memory_s...]
    add x3 -> x1, other arithmetic: 6.19 us -> 0.02 us  [local(): grads = grads[0] + lax.ppermute(grads[1], 'dp', [(0, 1), (1, 0)])]
    ppermute x24 -> x10, waiting for transfers between devices: 15.3 us -> 9.14 us  [the longest x2 5.07 us: local(): other = lax.ppermute(up, 'tensor', [(t, t ^ bit) for t in range(4)])]
    slice x5 -> x1, local copies, waits for them, and re-layouts: 4.44 us -> 0.02 us  [local(): level0 = lax.dynamic_slice_in_dim(slots[:, 0], f % 4 * 4, 4, 0).astype(F32)]
  transfers between devices with their start and end apart: 25 -> 12, of which waited for: 9 -> 7; matrix products, arithmetic and copies ran while one was open for 28% -> 6% of each run, Pallas kernels for 11% -> 16%
where the time goes in v2:
time: 85.6 us; the launch traced here: 85.2 us
  starting transfers between devices  44.3 us (52%)
  Pallas kernels  21.6 us (25%)
  waiting for transfers between devices  9.48 us (11%)
  other arithmetic  5.7 us (7%)
  local copies, waits for them, and re-layouts  3.28 us (4%)
    all_to_all x1, starting transfers between devices, local(): slots = lax.all_to_all(slots.astype(BF), 'fsdp', 0, 0, tiled=True)  17.6 us
    ppermute x6, starting transfers between devices, ring(): return lax.ppermute(x, ('fsdp', 'tensor'), ring_pairs(stage, s))  9.75 us
    pallas_call x1, Pallas kernels, local(): pl.pallas_call(prepare_body, out_shape=(shape((2048, LANES), BF), shape((...  8.92 us
    pallas_call x1, Pallas kernels, forward(): pl.pallas_call(functools.partial(forward_body, tiles=tiles), out_shape=[p...  8.27 us
    all_to_all x1, starting transfers between devices, local(): lax.all_to_all(activations.T.reshape(16, BLOCK, tokens), 'fsdp', 0, 0, ti...  8.26 us
    ppermute x2, waiting for transfers between devices, local(): other = lax.ppermute(up, 'tensor', [(t, t ^ bit) for t in range(4)])  5.07 us
    pallas_call x2, Pallas kernels, call(): pl.pallas_call(body, out_shape=out_shape, in_specs=[pl.BlockSpec(memory_s...  4.41 us
    ppermute x6, waiting for transfers between devices, ring(): return lax.ppermute(x, ('fsdp', 'tensor'), ring_pairs(stage, s))  3.77 us
  transfers between devices with their start and end apart: 12, of which 7 were waited for; matrix products, arithmetic and copies ran while one was open for 6% of the time, Pallas kernels for 16%

profile of v2, /device:TPU:6, one launch (start us, length us, event | category | flops | bytes accessed | tf_op | source)
XLA Modules:
  0.0 85.2 jit_solution(5198653156481642844)
XLA Ops:
  0.6 1.8 %copy.13 = bf16[256,512]{0,1:T(8,128)(2,1)} copy(bf16[256,512]{1,0:T(8,128)(2,1)} %param.5) | data formatting | bytes 524288 | tf_op args[0]
  2.4 8.3 %all-to-all-start = ((bf16[16,32,256]{2,1,0:T(8,128)(2,1)}), bf16[16,32,256]{2,1,0:T(8,128)(2,1)S(1)}, u32[]{:S(2)}, u32[]{:S(2)}) async-start(bf16[16,32,256]{2,1,0:T(8,128)(2,1)} %bitcast.1), calls=%async_computation | async-start | bytes 524288 | tf_op jit(solution)/shard_map/all_to_all | solution.py:295
  10.7 8.9 %shard_map.68 = (bf16[2048,128]{1,0:T(8,128)(2,1)S(1)}, f32[1024,128]{1,0:T(8,128)S(1)}, s32[16,128]{1,0:T(8,128)S(1)}) custom-call(f32[4,256,1024]{2,1,0:T(8,128)} %params.1, s32[4,8192]{1,0:T(4,128)} %perms.1), custom_call_target="tpu_custom_call" | custom-call | tf_op jit(solution)/shard_map/pallas_call | solution.py:299
  19.6 0.0 all-to-all-done
  19.6 8.3 %shard_map.69 = (bf16[64,7168]{1,0:T(8,128)(2,1)}, bf16[64,7168]{1,0:T(8,128)(2,1)}, bf16[64,7168]{1,0:T(8,128)(2,1)}, bf16[64,7168]{1,0:T(8,128)(2,1)}, bf16[51...) custom-call(bf16[512,256]{1,0:T(8,128)(2,1)S(1)} %bitcast.41, bf16[2048,128]{1,0:T(8,128)(2,1)S(1)} %get-tuple-element.20.rot_ref, ...), custom_call_target="tpu_custom_call" | custom-call | tf_op jit(solution)/shard_map/pallas_call | solution.py:225
  27.9 0.0 copy-start
  27.9 0.1 collective-permute-start
  28.0 1.5 %collective-permute-done = bf16[512,256]{1,0:T(8,128)(2,1)S(1)} collective-permute-done((bf16[512,256]{1,0:T(8,128)(2,1)S(1)}, bf16[512,256]{1,0:T(8,128)(2,1)S(1)}, u32[]{:S(2)}, u32[]{:S(2)}) %collective-permute-start) | collective-permute-done | bytes 262176 | tf_op jit(solution)/shard_map/ppermute | solution.py:321
  29.5 0.1 add_convert_fusion.1
  29.6 1.6 %collective-permute-start.1 = (bf16[512,256]{1,0:T(8,128)(2,1)S(1)}, bf16[512,256]{1,0:T(8,128)(2,1)S(1)}, u32[]{:S(2)}, u32[]{:S(2)}) collective-permute-start(bf16[512,256]{1,0:T(8,128)(2,1)S(1)} %add_convert_fusion.1), channel_id=1, source_target_pairs={{0,2},{1,3},{2,0},{3,1},{4,6},{5,7},{6,4},{7,5},{8,10},{9,11},{10,... | collective-permute-start | bytes 786440 | tf_op jit(solution)/shard_map/ppermute | solution.py:321
  31.2 1.5 %collective-permute-start.3 = (bf16[64,7168]{1,0:T(8,128)(2,1)}, bf16[64,7168]{1,0:T(8,128)(2,1)S(1)}, u32[]{:S(2)}, u32[]{:S(2)}) collective-permute-start(bf16[64,7168]{1,0:T(8,128)(2,1)} %get-tuple-element.25), channel_id=1, source_target_pairs={{0,16},{1,5},{2,18},{3,7},{4,20},{5,9},{6,22},{7,11},{8,24},{9,13}... | collective-permute-start | bytes 2752520 | tf_op jit(solution)/shard_map/ppermute | solution.py:290
  32.7 1.8 %collective-permute-start.4 = (bf16[64,7168]{1,0:T(8,128)(2,1)}, bf16[64,7168]{1,0:T(8,128)(2,1)}, u32[]{:S(2)}, u32[]{:S(2)}) collective-permute-start(bf16[64,7168]{1,0:T(8,128)(2,1)} %get-tuple-element.26), channel_id=1, source_target_pairs={{0,48},{1,13},{2,50},{3,15},{4,52},{5,1},{6,54},{7,3},{8,56},{9,5}... | collective-permute-start | bytes 2752520 | tf_op jit(solution)/shard_map/ppermute | solution.py:290
  34.5 3.5 %collective-permute-done.1 = bf16[512,256]{1,0:T(8,128)(2,1)S(1)} collective-permute-done((bf16[512,256]{1,0:T(8,128)(2,1)S(1)}, bf16[512,256]{1,0:T(8,128)(2,1)S(1)}, u32[]{:S(2)}, u32[]{:S(2)}) %collective-permute-start.1) | collective-permute-done | bytes 262176 | tf_op jit(solution)/shard_map/ppermute | solution.py:321
  38.0 0.1 add_convert_fusion.up_ref
  38.1 2.3 %shard_map.70 = f32[2,4,2,32,128]{4,3,2,1,0:T(8,128)S(1)} custom-call(bf16[512,256]{1,0:T(8,128)(2,1)S(1)} %add_convert_fusion.up_ref, bf16[4,512,256]{2,1,0:T(8,128)(2,1)S(1)} %get-tuple-element.23.saved_ref, bf16[2048,128]{1,0:T(8,128)(2,1)S(1)} %get-tuple-element.20.rot_ref, s32[16,128]{1,0:T(8,128)S(1)} %get-tuple-element.24.idx_ref), custom_call_target="tpu_custom_call" | custom-call | tf_op jit(solution)/shard_map/pallas_call | solution.py:30
  40.4 3.3 %collective-permute-start.2 = (f32[4,2,32,128]{3,2,1,0:T(8,128)S(1)}, f32[4,2,32,128]{3,2,1,0:T(8,128)S(1)}, u32[]{:S(2)}, u32[]{:S(2)}) collective-permute-start(f32[4,2,32,128]{3,2,1,0:T(8,128)S(1)} %slice_bitcast_fusion), channel_id=1, source_target_pairs={{0,64},{64,0},{1,65},{65,1},{2,66},{66,2},{3,67},{67,3},{4,68},{68... | collective-permute-start | bytes 393224 | tf_op jit(solution)/shard_map/ppermute | solution.py:326
  43.7 3.0 %collective-permute-start.5 = (bf16[64,7168]{1,0:T(8,128)(2,1)}, bf16[64,7168]{1,0:T(8,128)(2,1)}, u32[]{:S(2)}, u32[]{:S(2)}) collective-permute-start(bf16[64,7168]{1,0:T(8,128)(2,1)} %get-tuple-element.29), channel_id=1, source_target_pairs={{0,32},{1,9},{2,34},{3,11},{4,36},{5,13},{6,38},{7,15},{8,40},{9,1... | collective-permute-start | bytes 2752520 | tf_op jit(solution)/shard_map/ppermute | solution.py:290
  46.7 0.3 collective-permute-done.2
  47.0 0.0 collective-permute-done.3
  47.0 0.0 collective-permute-done.4
  47.0 3.7 %collective-permute-start.6 = (f32[2,32,128]{2,1,0:T(8,128)S(1)}, f32[2,32,128]{2,1,0:T(8,128)S(1)}, u32[]{:S(2)}, u32[]{:S(2)}) collective-permute-start(f32[2,32,128]{2,1,0:T(8,128)S(1)} %get-tuple-element.47), channel_id=1, source_target_pairs={{0,0},{4,8},{8,16},{12,24},{16,32},{20,40},{24,48},{28,56},{32,64}... | collective-permute-start | bytes 98312 | tf_op jit(solution)/shard_map/ppermute | solution.py:330
  50.7 0.1 select_n.56
  50.8 0.1 select_n.60
  50.9 0.1 maximum_convert_fusion
  51.1 0.7 pad_maximum_fusion
  51.8 17.6 %all-to-all-start.1 = ((bf16[16,2,32,128]{3,2,1,0:T(8,128)(2,1)}), bf16[16,2,32,128]{3,2,1,0:T(8,128)(2,1)S(1)}, u32[]{:S(2)}, u32[]{:S(2)}) async-start(bf16[16,2,32,128]{3,2,1,0:T(8,128)(2,1)} %pad_maximum_fusion), calls=%async_computation.1 | async-start | bytes 524288 | tf_op jit(solution)/shard_map/all_to_all | solution.py:339
  69.4 0.0 collective-permute-done.5
  69.4 0.0 collective-permute-done.6
  69.4 0.0 copy-done
  69.4 2.5 %add_convert_fusion.3 = (bf16[16,7168]{1,0:T(8,128)(2,1)}, bf16[16,7168]{1,0:T(8,128)(2,1)}, bf16[16,7168]{1,0:T(8,128)(2,1)}) fusion(bf16[64,7168]{1,0:T(8,128)(2,1)} %collective-permute-done.5, bf16[64,7168]{1,0:T(8,128)(2,1)} %collective-permute-done.4, bf16[64,7168]{1,0:T(8,128)(2,1)S(1)} %collective-permute-done.3, bf16[64,7168]{1,0:T(8,128)(2,1)S(1)} %copy-done), kind=kLoop, calls=%fused_computation.3 | loop fusion | flops 2752512 | bytes 3440640 | tf_op jit(solution)/shard_map/convert_element_type | solution.py:343
  71.9 1.5 %collective-permute-start.7 = (bf16[16,7168]{1,0:T(8,128)(2,1)}, bf16[16,7168]{1,0:T(8,128)(2,1)S(1)}, u32[]{:S(2)}, u32[]{:S(2)}) collective-permute-start(bf16[16,7168]{1,0:T(8,128)(2,1)} %get-tuple-element.40), channel_id=1, source_target_pairs={{0,8},{1,33},{2,10},{3,35},{4,12},{5,37},{6,14},{7,39},{8,0},{9,41... | collective-permute-start | bytes 688136 | tf_op jit(solution)/shard_map/ppermute | solution.py:290
  73.4 2.1 %collective-permute-start.8 = (bf16[16,7168]{1,0:T(8,128)(2,1)}, bf16[16,7168]{1,0:T(8,128)(2,1)}, u32[]{:S(2)}, u32[]{:S(2)}) collective-permute-start(bf16[16,7168]{1,0:T(8,128)(2,1)} %get-tuple-element.39), channel_id=1, source_target_pairs={{0,4},{1,17},{2,6},{3,19},{4,8},{5,21},{6,10},{7,23},{8,12},{9,25}... | collective-permute-start | bytes 688136 | tf_op jit(solution)/shard_map/ppermute | solution.py:290
  75.5 0.0 collective-permute-start.9
  75.5 0.3 all-to-all-done.1
  75.9 2.1 %shard_map.71 = f32[8,32,128]{2,1,0:T(8,128)S(1)} custom-call(f32[8,32,128]{2,1,0:T(8,128)S(1)} %pad_maximum_fusion.1.g_ref, f32[1024,128]{1,0:T(8,128)S(1)} %get-tuple-element.33.ad_ref), custom_call_target="tpu_custom_call" | custom-call | tf_op jit(solution)/shard_map/pallas_call | solution.py:30
  78.0 0.3 reshape.39
  78.3 0.1 copy.17
  78.4 0.9 %reshape.40 = f32[4,8,1024]{2,1,0:T(8,128)} reshape(f32[4,2,4,32,32]{4,3,2,1,0:T(8,128)S(1)} %copy.17) | data formatting | bytes 262144 | tf_op jit(solution)/shard_map/reshape | solution.py:354
  79.3 0.4 collective-permute-done.7
  79.7 0.1 collective-permute-done.8
  79.7 3.3 %collective-permute-done.9 = bf16[16,7168]{1,0:T(8,128)(2,1)} collective-permute-done((bf16[16,7168]{1,0:T(8,128)(2,1)}, bf16[16,7168]{1,0:T(8,128)(2,1)}, u32[]{:S(2)}, u32[]{:S(2)}) %collective-permute-start.9) | collective-permute-done | bytes 229408 | tf_op jit(solution)/shard_map/ppermute | solution.py:290
  83.0 2.2 %add_convert_fusion.2 = bf16[16,7168]{1,0:T(8,128)(2,1)} fusion(bf16[16,7168]{1,0:T(8,128)(2,1)} %collective-permute-done.9, bf16[16,7168]{1,0:T(8,128)(2,1)} %collective-permute-done.8, bf16[16,7168]{1,0:T(8,128)(2,1)S(1)} %collective-permute-done.7, bf16[64,7168]{1,0:T(8,128)(2,1)} %collective-permute-done.5, bf16[64,7168]{1,0:T(8,128)(2,1)} %collective-permute-done.4, ...), kind=kLoop, calls=%fused_computation.2 | loop fusion | flops 1835008 | bytes 1835008 | tf_op jit(solution)/shard_map/convert_element_type | solution.py:357
  (13 shorter events, 0.2 us)
Async XLA Ops:
  2.4 17.2 %all-to-all-start = ((bf16[16,32,256]{2,1,0:T(8,128)(2,1)}), bf16[16,32,256]{2,1,0:T(8,128)(2,1)S(1)}, u32[]{:S(2)}, u32[]{:S(2)}) async-start(bf16[16,32,256]{2,1,0:T(8,128)(2,1)} %bitcast.1), calls=%async_computation | async-start | bytes 524288 | tf_op jit(solution)/shard_map/all_to_all | solution.py:295
  27.9 41.5 %copy-start = (bf16[64,7168]{1,0:T(8,128)(2,1)S(1)}, bf16[64,7168]{1,0:T(8,128)(2,1)}, u32[]{:S(2)}) copy-start(bf16[64,7168]{1,0:T(8,128)(2,1)} %get-tuple-element.21) | copy-start | bytes 2752516
  27.9 1.6 %collective-permute-start = (bf16[512,256]{1,0:T(8,128)(2,1)S(1)}, bf16[512,256]{1,0:T(8,128)(2,1)S(1)}, u32[]{:S(2)}, u32[]{:S(2)}) collective-permute-start(bf16[512,256]{1,0:T(8,128)(2,1)S(1)} %get-tuple-element.22), channel_id=1, source_target_pairs={{0,1},{1,0},{2,3},{3,2},{4,5},{5,4},{6,7},{7,6},{8,9},{9,8},{10,11... | collective-permute-start | bytes 786440 | tf_op jit(solution)/shard_map/ppermute | solution.py:321
  29.6 8.4 %collective-permute-start.1 = (bf16[512,256]{1,0:T(8,128)(2,1)S(1)}, bf16[512,256]{1,0:T(8,128)(2,1)S(1)}, u32[]{:S(2)}, u32[]{:S(2)}) collective-permute-start(bf16[512,256]{1,0:T(8,128)(2,1)S(1)} %add_convert_fusion.1), channel_id=1, source_target_pairs={{0,2},{1,3},{2,0},{3,1},{4,6},{5,7},{6,4},{7,5},{8,10},{9,11},{10,... | collective-permute-start | bytes 786440 | tf_op jit(solution)/shard_map/ppermute | solution.py:321
  31.2 15.7 %collective-permute-start.3 = (bf16[64,7168]{1,0:T(8,128)(2,1)}, bf16[64,7168]{1,0:T(8,128)(2,1)S(1)}, u32[]{:S(2)}, u32[]{:S(2)}) collective-permute-start(bf16[64,7168]{1,0:T(8,128)(2,1)} %get-tuple-element.25), channel_id=1, source_target_pairs={{0,16},{1,5},{2,18},{3,7},{4,20},{5,9},{6,22},{7,11},{8,24},{9,13}... | collective-permute-start | bytes 2752520 | tf_op jit(solution)/shard_map/ppermute | solution.py:290
  32.7 14.3 %collective-permute-start.4 = (bf16[64,7168]{1,0:T(8,128)(2,1)}, bf16[64,7168]{1,0:T(8,128)(2,1)}, u32[]{:S(2)}, u32[]{:S(2)}) collective-permute-start(bf16[64,7168]{1,0:T(8,128)(2,1)} %get-tuple-element.26), channel_id=1, source_target_pairs={{0,48},{1,13},{2,50},{3,15},{4,52},{5,1},{6,54},{7,3},{8,56},{9,5}... | collective-permute-start | bytes 2752520 | tf_op jit(solution)/shard_map/ppermute | solution.py:290
  40.4 6.6 %collective-permute-start.2 = (f32[4,2,32,128]{3,2,1,0:T(8,128)S(1)}, f32[4,2,32,128]{3,2,1,0:T(8,128)S(1)}, u32[]{:S(2)}, u32[]{:S(2)}) collective-permute-start(f32[4,2,32,128]{3,2,1,0:T(8,128)S(1)} %slice_bitcast_fusion), channel_id=1, source_target_pairs={{0,64},{64,0},{1,65},{65,1},{2,66},{66,2},{3,67},{67,3},{4,68},{68... | collective-permute-start | bytes 393224 | tf_op jit(solution)/shard_map/ppermute | solution.py:326
  43.7 25.7 %collective-permute-start.5 = (bf16[64,7168]{1,0:T(8,128)(2,1)}, bf16[64,7168]{1,0:T(8,128)(2,1)}, u32[]{:S(2)}, u32[]{:S(2)}) collective-permute-start(bf16[64,7168]{1,0:T(8,128)(2,1)} %get-tuple-element.29), channel_id=1, source_target_pairs={{0,32},{1,9},{2,34},{3,11},{4,36},{5,13},{6,38},{7,15},{8,40},{9,1... | collective-permute-start | bytes 2752520 | tf_op jit(solution)/shard_map/ppermute | solution.py:290
  47.0 22.4 %collective-permute-start.6 = (f32[2,32,128]{2,1,0:T(8,128)S(1)}, f32[2,32,128]{2,1,0:T(8,128)S(1)}, u32[]{:S(2)}, u32[]{:S(2)}) collective-permute-start(f32[2,32,128]{2,1,0:T(8,128)S(1)} %get-tuple-element.47), channel_id=1, source_target_pairs={{0,0},{4,8},{8,16},{12,24},{16,32},{20,40},{24,48},{28,56},{32,64}... | collective-permute-start | bytes 98312 | tf_op jit(solution)/shard_map/ppermute | solution.py:330
  51.8 24.0 %all-to-all-start.1 = ((bf16[16,2,32,128]{3,2,1,0:T(8,128)(2,1)}), bf16[16,2,32,128]{3,2,1,0:T(8,128)(2,1)S(1)}, u32[]{:S(2)}, u32[]{:S(2)}) async-start(bf16[16,2,32,128]{3,2,1,0:T(8,128)(2,1)} %pad_maximum_fusion), calls=%async_computation.1 | async-start | bytes 524288 | tf_op jit(solution)/shard_map/all_to_all | solution.py:339
  71.9 7.7 %collective-permute-start.7 = (bf16[16,7168]{1,0:T(8,128)(2,1)}, bf16[16,7168]{1,0:T(8,128)(2,1)S(1)}, u32[]{:S(2)}, u32[]{:S(2)}) collective-permute-start(bf16[16,7168]{1,0:T(8,128)(2,1)} %get-tuple-element.40), channel_id=1, source_target_pairs={{0,8},{1,33},{2,10},{3,35},{4,12},{5,37},{6,14},{7,39},{8,0},{9,41... | collective-permute-start | bytes 688136 | tf_op jit(solution)/shard_map/ppermute | solution.py:290
  73.4 6.3 %collective-permute-start.8 = (bf16[16,7168]{1,0:T(8,128)(2,1)}, bf16[16,7168]{1,0:T(8,128)(2,1)}, u32[]{:S(2)}, u32[]{:S(2)}) collective-permute-start(bf16[16,7168]{1,0:T(8,128)(2,1)} %get-tuple-element.39), channel_id=1, source_target_pairs={{0,4},{1,17},{2,6},{3,19},{4,8},{5,21},{6,10},{7,23},{8,12},{9,25}... | collective-permute-start | bytes 688136 | tf_op jit(solution)/shard_map/ppermute | solution.py:290
  75.5 7.5 %collective-permute-start.9 = (bf16[16,7168]{1,0:T(8,128)(2,1)}, bf16[16,7168]{1,0:T(8,128)(2,1)}, u32[]{:S(2)}, u32[]{:S(2)}) collective-permute-start(bf16[16,7168]{1,0:T(8,128)(2,1)} %get-tuple-element.38), channel_id=1, source_target_pairs={{0,12},{1,49},{2,14},{3,51},{4,0},{5,53},{6,2},{7,55},{8,4},{9,57}... | collective-permute-start | bytes 688136 | tf_op jit(solution)/shard_map/ppermute | solution.py:290

commit v3 on v2

--- a/solution.py
+++ b/solution.py
@@ -46,7 +46,26 @@
 
 
 def prepare_body(
-    params, perms, rot_ref, inv_ref, idx_ref, fetched, chosen, turned, mat, rows, perm_ref, sem, perm_sem
+    params,
+    perms,
+    weight,
+    cotan,
+    rot_ref,
+    inv_ref,
+    idx_ref,
+    up_ref,
+    w_ref,
+    c_ref,
+    fetched,
+    chosen,
+    turned,
+    mat,
+    rows,
+    perm_ref,
+    sem,
+    perm_sem,
+    w_sem,
+    c_sem,
 ):
     f = lax.axis_index("fsdp")
     d = lax.axis_index("dp")
@@ -69,6 +88,10 @@
         copy.start()
     perm_copy = pltpu.make_async_copy(perms, perm_ref, perm_sem)
     perm_copy.start()
+    w_copy = pltpu.make_async_copy(weight, w_ref, w_sem)
+    w_copy.start()
+    c_copy = pltpu.make_async_copy(cotan, c_ref, c_sem)
+    c_copy.start()
     perm_copy.wait()
 
     lane = iota((1, LANES), 1)
@@ -137,6 +160,9 @@
             rot_ref[g * LANES : (g + 1) * LANES, :] = dot(onehot(idx_ref, g), rotation, 1, 0).astype(BF)
         else:
             inv_ref[(g - 16) * LANES : (g - 15) * LANES, :] = wide
+    w_copy.wait()
+    c_copy.wait()
+    up_ref[...] = dot(w_ref[...], c_ref[...], 1, 1).astype(BF)
 
 
 def onehot(idx_ref, g):
@@ -168,16 +194,15 @@
 
 
 def forward_body(
-    x_ref, rot_ref, weight, cotan, *rest, tiles
+    x_ref, rot_ref, weight, *rest, tiles
 ):
-    parts, up_ref, saved_ref = rest[:4], rest[4], rest[5]
-    w_ref, c_ref, out_ref, staged, w_sems, c_sem, p_sem = rest[6:]
+    parts, saved_ref = rest[:4], rest[4]
+    w_ref, out_ref, staged, w_sems, p_sem = rest[5:]
     tile = weight.shape[1] // tiles
     fetches = []
     for i in range(tiles):
         span = pl.ds(i * tile, tile)
         fetches.append(pltpu.make_async_copy(weight.at[:, span], w_ref.at[:, span], w_sems.at[i]))
-    fetches.append(pltpu.make_async_copy(cotan, c_ref, c_sem))
     for fetch in fetches:
         fetch.start()
 
@@ -211,13 +236,11 @@
             copy = pltpu.make_async_copy(staged.at[i, pl.ds(s * 64, 64)], parts[s].at[:, span], p_sem)
             copy.start()
             copies.append(copy)
-    fetches[tiles].wait()
-    up_ref[...] = dot(w_ref[...], c_ref[...], 1, 1).astype(BF)
     for copy in copies:
         copy.wait()
 
 
-def forward(mixed, rot, weight, cotangent, tiles=7):
+def forward(mixed, rot, weight, tiles=7):
     depth, tokens = mixed.shape
     columns = weight.shape[1]
     vmem = pl.BlockSpec(memory_space=pltpu.VMEM)
@@ -225,20 +248,18 @@
     return pl.pallas_call(
         functools.partial(forward_body, tiles=tiles),
         out_shape=[pltpu.HBM((tokens // 4, columns), BF)] * 4
-        + [shape((depth, tokens), BF), shape((FACTORS, depth, tokens), BF)],
-        in_specs=[vmem, vmem, hbm, hbm],
-        out_specs=[hbm] * 4 + [vmem] * 2,
+        + [shape((FACTORS, depth, tokens), BF)],
+        in_specs=[vmem, vmem, hbm],
+        out_specs=[hbm] * 4 + [vmem],
         scratch_shapes=[
             pltpu.VMEM((depth, columns), BF),
-            pltpu.VMEM((tokens, columns), BF),
             pltpu.VMEM((tokens, depth), BF),
             pltpu.VMEM((tiles, tokens, columns // tiles), BF),
             pltpu.SemaphoreType.DMA((tiles,)),
             pltpu.SemaphoreType.DMA,
-            pltpu.SemaphoreType.DMA,
         ],
         compiler_params=pltpu.CompilerParams(vmem_limit_bytes=32 << 20),
-    )(mixed, rot, far(weight), far(cotangent))
+    )(mixed, rot, far(weight))
 
 
 def backward_body(up_ref, saved_ref, rot_ref, idx_ref, grad_ref):
@@ -296,12 +317,19 @@
         activations.T.reshape(16, BLOCK, tokens), "fsdp", 0, 0, tiled=True
     ).reshape(512, tokens)
 
-    rot, inv, idx = pl.pallas_call(
+    rot, inv, idx, up = pl.pallas_call(
         prepare_body,
-        out_shape=(shape((2048, LANES), BF), shape((1024, LANES), F32), shape((16, LANES), jnp.int32)),
-        in_specs=[pl.BlockSpec(memory_space=pl.ANY)] * 2,
-        out_specs=(pl.BlockSpec(memory_space=pltpu.VMEM),) * 3,
+        out_shape=(
+            shape((2048, LANES), BF),
+            shape((1024, LANES), F32),
+            shape((16, LANES), jnp.int32),
+            shape((512, tokens), BF),
+        ),
+        in_specs=[pl.BlockSpec(memory_space=pltpu.HBM)] * 4,
+        out_specs=(pl.BlockSpec(memory_space=pltpu.VMEM),) * 4,
         scratch_shapes=[
+            pltpu.VMEM(frozen_weight.shape, BF),
+            pltpu.VMEM(cotangent.shape, BF),
             pltpu.VMEM((160, BLOCK * BLOCK), F32),
             pltpu.VMEM((LANES, BLOCK * BLOCK), F32),
             pltpu.VMEM((BLOCK * BLOCK, LANES), F32),
@@ -310,11 +338,14 @@
             pltpu.VMEM((FACTORS, 8192), jnp.int32),
             pltpu.SemaphoreType.DMA,
             pltpu.SemaphoreType.DMA,
+            pltpu.SemaphoreType.DMA,
+            pltpu.SemaphoreType.DMA,
         ],
-        compiler_params=pltpu.CompilerParams(vmem_limit_bytes=12 << 20),
-    )(far(cayley_params), far(permutations))
-
-    *parts, up, saved = forward(mixed, rot, frozen_weight, cotangent)
+        compiler_params=pltpu.CompilerParams(vmem_limit_bytes=32 << 20),
+    )(far(cayley_params), far(permutations), far(frozen_weight), far(cotangent))
+
+    up, mixed = lax.optimization_barrier((up, mixed))
+    *parts, saved = forward(mixed, rot, frozen_weight)
     near, back, across = [ring(parts[s], 0, s) for s in (1, 3, 2)]
 
     for bit in (1, 2):
@@ -324,7 +355,7 @@
         backward_body, shape((2, FACTORS, 2, BLOCK, LANES), F32), (up, saved, rot, idx)
     )
     grads = grads[0] + lax.ppermute(grads[1], "dp", [(0, 1), (1, 0)])
-    grads, near, back = lax.optimization_barrier((grads, near, back))
+    grads, near = lax.optimization_barrier((grads, near))
 
     f = lax.axis_index("fsdp")
     level3 = lax.ppermute(

time: 85.6 us -> 81.9 us (0.957)
  starting transfers between devices: 44.3 us -> 33.6 us
  waiting for transfers between devices: 9.48 us -> 16.8 us
    ppermute x6, waiting for transfers between devices: 3.77 us -> 15.3 us  [ring(): return lax.ppermute(x, ('fsdp', 'tensor'), ring_pairs(stage, s))]
    all_to_all x1, starting transfers between devices: 17.6 us -> 8.98 us  [local(): slots = lax.all_to_all(slots.astype(BF), 'fsdp', 0, 0, tiled=True)]
    ppermute x2, waiting for transfers between devices: 5.07 us -> 1.52 us  [local(): other = lax.ppermute(up, 'tensor', [(t, t ^ bit) for t in range(4)])]
    pallas_call x1, Pallas kernels: 8.27 us -> 5.85 us  [forward(): pl.pallas_call(functools.partial(forward_body, tiles=tiles), out_shape=[p...]
    pallas_call x1, Pallas kernels: 8.92 us -> 11 us  [local(): pl.pallas_call(prepare_body, out_shape=(shape((2048, LANES), BF), shape((...]
    ppermute x1, starting transfers between devices: 3.67 us -> 2.44 us  [local(): lax.ppermute(grads[3], ('dp', 'fsdp'), [(e * 16 + s, s // 8 * 16 + s % 8...]
  transfers between devices with their start and end apart: 12 -> 12, of which waited for: 7 -> 6; matrix products, arithmetic and copies ran while one was open for 6% -> 6% of each run, Pallas kernels for 16% -> 26%
where the time goes in v3:
time: 81.9 us; the launch traced here: 81.5 us
  starting transfers between devices  33.6 us (41%)
  Pallas kernels  21.3 us (26%)
  waiting for transfers between devices  16.8 us (21%)
  other arithmetic  5.7 us (7%)
  local copies, waits for them, and re-layouts  3.27 us (4%)
  between operations  0.82 us (1%)
    ppermute x6, waiting for transfers between devices, ring(): return lax.ppermute(x, ('fsdp', 'tensor'), ring_pairs(stage, s))  15.3 us
    pallas_call x1, Pallas kernels, local(): pl.pallas_call(prepare_body, out_shape=(shape((2048, LANES), BF), shape((...  11 us
    ppermute x6, starting transfers between devices, ring(): return lax.ppermute(x, ('fsdp', 'tensor'), ring_pairs(stage, s))  9.21 us
    all_to_all x1, starting transfers between devices, local(): slots = lax.all_to_all(slots.astype(BF), 'fsdp', 0, 0, tiled=True)  8.98 us
    all_to_all x1, starting transfers between devices, local(): lax.all_to_all(activations.T.reshape(16, BLOCK, tokens), 'fsdp', 0, 0, ti...  8.26 us
    pallas_call x1, Pallas kernels, forward(): pl.pallas_call(functools.partial(forward_body, tiles=tiles), out_shape=[p...  5.85 us
    pallas_call x2, Pallas kernels, call(): pl.pallas_call(body, out_shape=out_shape, in_specs=[pl.BlockSpec(memory_s...  4.41 us
    ppermute x1, starting transfers between devices, local(): grads = grads[0] + lax.ppermute(grads[1], 'dp', [(0, 1), (1, 0)])  2.98 us
  transfers between devices with their start and end apart: 12, of which 6 were waited for; matrix products, arithmetic and copies ran while one was open for 6% of the time, Pallas kernels for 26%

profile of v3, /device:TPU:6, one launch (start us, length us, event | category | flops | bytes accessed | tf_op | source)
XLA Modules:
  0.0 81.5 jit_solution(12675359912571953344)
XLA Ops:
  0.6 1.8 %copy.13 = bf16[256,512]{0,1:T(8,128)(2,1)} copy(bf16[256,512]{1,0:T(8,128)(2,1)} %param.5) | data formatting | bytes 524288 | tf_op args[0]
  2.4 8.3 %all-to-all-start = ((bf16[16,32,256]{2,1,0:T(8,128)(2,1)}), bf16[16,32,256]{2,1,0:T(8,128)(2,1)S(1)}, u32[]{:S(2)}, u32[]{:S(2)}) async-start(bf16[16,32,256]{2,1,0:T(8,128)(2,1)} %bitcast.1), calls=%async_computation | async-start | bytes 524288 | tf_op jit(solution)/shard_map/all_to_all | solution.py:316
  10.7 11.0 %shard_map.68 = (bf16[2048,128]{1,0:T(8,128)(2,1)S(1)}, f32[1024,128]{1,0:T(8,128)S(1)}, s32[16,128]{1,0:T(8,128)S(1)}, bf16[512,256]{1,0:T(8,128)(2,1)S(1)}) custom-call(f32[4,256,1024]{2,1,0:T(8,128)} %params.1, s32[4,8192]{1,0:T(4,128)} %perms.1, bf16[512,7168]{1,0:T(8,128)(2,1)} %weight.3, bf16[256,7168]{1,0:T(8,128)(2,1)} %cotan.1), custom_call_target="tpu_custom_call" | custom-call | tf_op jit(solution)/shard_map/pallas_call | solution.py:320
  21.7 0.0 all-to-all-done
  21.7 0.1 collective-permute-start
  21.8 1.5 %collective-permute-done = bf16[512,256]{1,0:T(8,128)(2,1)S(1)} collective-permute-done((bf16[512,256]{1,0:T(8,128)(2,1)S(1)}, bf16[512,256]{1,0:T(8,128)(2,1)S(1)}, u32[]{:S(2)}, u32[]{:S(2)}) %collective-permute-start) | collective-permute-done | bytes 262176 | tf_op jit(solution)/shard_map/ppermute | solution.py:352
  23.4 0.1 add_convert_fusion.1
  23.4 1.7 %collective-permute-start.1 = (bf16[512,256]{1,0:T(8,128)(2,1)S(1)}, bf16[512,256]{1,0:T(8,128)(2,1)S(1)}, u32[]{:S(2)}, u32[]{:S(2)}) collective-permute-start(bf16[512,256]{1,0:T(8,128)(2,1)S(1)} %add_convert_fusion.1), channel_id=1, source_target_pairs={{0,2},{1,3},{2,0},{3,1},{4,6},{5,7},{6,4},{7,5},{8,10},{9,11},{10,... | collective-permute-start | bytes 786440 | tf_op jit(solution)/shard_map/ppermute | solution.py:352
  25.1 5.9 %shard_map.69 = (bf16[64,7168]{1,0:T(8,128)(2,1)}, bf16[64,7168]{1,0:T(8,128)(2,1)}, bf16[64,7168]{1,0:T(8,128)(2,1)}, bf16[64,7168]{1,0:T(8,128)(2,1)}, bf16[4,512,256]{2,1,0:T(8,128)(2,1)S(1)}) custom-call(bf16[512,256]{1,0:T(8,128)(2,1)S(1)} %bitcast.41, bf16[2048,128]{1,0:T(8,128)(2,1)S(1)} %get-tuple-element.23.rot_ref, bf16[512,7168]{1,0:T(8,128)(2,1)} %weight.3), custom_call_target="tpu_custom_call" | custom-call | tf_op jit(solution)/shard_map/pallas_call | solution.py:248
  30.9 0.0 copy-start
  30.9 1.5 %collective-permute-start.3 = (bf16[64,7168]{1,0:T(8,128)(2,1)}, bf16[64,7168]{1,0:T(8,128)(2,1)S(1)}, u32[]{:S(2)}, u32[]{:S(2)}) collective-permute-start(bf16[64,7168]{1,0:T(8,128)(2,1)} %get-tuple-element.28), channel_id=1, source_target_pairs={{0,16},{1,5},{2,18},{3,7},{4,20},{5,9},{6,22},{7,11},{8,24},{9,13}... | collective-permute-start | bytes 2752520 | tf_op jit(solution)/shard_map/ppermute | solution.py:311
  32.5 0.0 collective-permute-done.1
  32.5 0.1 add_convert_fusion.up_ref
  32.5 2.3 %shard_map.70 = f32[2,4,2,32,128]{4,3,2,1,0:T(8,128)S(1)} custom-call(bf16[512,256]{1,0:T(8,128)(2,1)S(1)} %add_convert_fusion.up_ref, bf16[4,512,256]{2,1,0:T(8,128)(2,1)S(1)} %get-tuple-element.26.saved_ref, bf16[2048,128]{1,0:T(8,128)(2,1)S(1)} %get-tuple-element.23.rot_ref, s32[16,128]{1,0:T(8,128)S(1)} %get-tuple-element.27.idx_ref), custom_call_target="tpu_custom_call" | custom-call | tf_op jit(solution)/shard_map/pallas_call | solution.py:30
  34.9 3.0 %collective-permute-start.2 = (f32[4,2,32,128]{3,2,1,0:T(8,128)S(1)}, f32[4,2,32,128]{3,2,1,0:T(8,128)S(1)}, u32[]{:S(2)}, u32[]{:S(2)}) collective-permute-start(f32[4,2,32,128]{3,2,1,0:T(8,128)S(1)} %slice_bitcast_fusion), channel_id=1, source_target_pairs={{0,64},{64,0},{1,65},{65,1},{2,66},{66,2},{3,67},{67,3},{4,68},{68... | collective-permute-start | bytes 393224 | tf_op jit(solution)/shard_map/ppermute | solution.py:357
  37.9 2.7 %collective-permute-start.5 = (bf16[64,7168]{1,0:T(8,128)(2,1)}, bf16[64,7168]{1,0:T(8,128)(2,1)}, u32[]{:S(2)}, u32[]{:S(2)}) collective-permute-start(bf16[64,7168]{1,0:T(8,128)(2,1)} %get-tuple-element.31), channel_id=1, source_target_pairs={{0,32},{1,9},{2,34},{3,11},{4,36},{5,13},{6,38},{7,15},{8,40},{9,1... | collective-permute-start | bytes 2752520 | tf_op jit(solution)/shard_map/ppermute | solution.py:311
  40.5 1.5 %collective-permute-start.4 = (bf16[64,7168]{1,0:T(8,128)(2,1)}, bf16[64,7168]{1,0:T(8,128)(2,1)}, u32[]{:S(2)}, u32[]{:S(2)}) collective-permute-start(bf16[64,7168]{1,0:T(8,128)(2,1)} %get-tuple-element.30), channel_id=1, source_target_pairs={{0,48},{1,13},{2,50},{3,15},{4,52},{5,1},{6,54},{7,3},{8,56},{9,5}... | collective-permute-start | bytes 2752520 | tf_op jit(solution)/shard_map/ppermute | solution.py:311
  42.0 0.0 collective-permute-done.2
  42.0 3.8 %collective-permute-done.3 = bf16[64,7168]{1,0:T(8,128)(2,1)S(1)} collective-permute-done((bf16[64,7168]{1,0:T(8,128)(2,1)}, bf16[64,7168]{1,0:T(8,128)(2,1)S(1)}, u32[]{:S(2)}, u32[]{:S(2)}) %collective-permute-start.3) | collective-permute-done | bytes 917536 | tf_op jit(solution)/shard_map/ppermute | solution.py:311
  45.8 2.4 %collective-permute-start.6 = (f32[2,32,128]{2,1,0:T(8,128)S(1)}, f32[2,32,128]{2,1,0:T(8,128)S(1)}, u32[]{:S(2)}, u32[]{:S(2)}) collective-permute-start(f32[2,32,128]{2,1,0:T(8,128)S(1)} %get-tuple-element.49), channel_id=1, source_target_pairs={{0,0},{4,8},{8,16},{12,24},{16,32},{20,40},{24,48},{28,56},{32,64}... | collective-permute-start | bytes 98312 | tf_op jit(solution)/shard_map/ppermute | solution.py:361
  48.3 0.1 select_n.56
  48.4 0.1 select_n.60
  48.5 0.1 maximum_convert_fusion
  48.6 0.7 pad_maximum_fusion
  49.4 9.0 %all-to-all-start.1 = ((bf16[16,2,32,128]{3,2,1,0:T(8,128)(2,1)}), bf16[16,2,32,128]{3,2,1,0:T(8,128)(2,1)S(1)}, u32[]{:S(2)}, u32[]{:S(2)}) async-start(bf16[16,2,32,128]{3,2,1,0:T(8,128)(2,1)} %pad_maximum_fusion), calls=%async_computation.1 | async-start | bytes 524288 | tf_op jit(solution)/shard_map/all_to_all | solution.py:370
  58.4 0.0 collective-permute-done.5
  58.4 0.0 collective-permute-done.6
  58.4 7.4 %collective-permute-done.4 = bf16[64,7168]{1,0:T(8,128)(2,1)} collective-permute-done((bf16[64,7168]{1,0:T(8,128)(2,1)}, bf16[64,7168]{1,0:T(8,128)(2,1)}, u32[]{:S(2)}, u32[]{:S(2)}) %collective-permute-start.4) | collective-permute-done | bytes 917536 | tf_op jit(solution)/shard_map/ppermute | solution.py:311
  65.8 0.0 copy-done
  65.8 2.5 %add_convert_fusion.3 = (bf16[16,7168]{1,0:T(8,128)(2,1)}, bf16[16,7168]{1,0:T(8,128)(2,1)}, bf16[16,7168]{1,0:T(8,128)(2,1)}) fusion(bf16[64,7168]{1,0:T(8,128)(2,1)} %collective-permute-done.4, bf16[64,7168]{1,0:T(8,128)(2,1)} %collective-permute-done.5, bf16[64,7168]{1,0:T(8,128)(2,1)S(1)} %collective-permute-done.3, bf16[64,7168]{1,0:T(8,128)(2,1)S(1)} %copy-done), kind=kLoop, calls=%fused_computation.3 | loop fusion | flops 2752512 | bytes 3440640 | tf_op jit(solution)/shard_map/convert_element_type | solution.py:374
  68.3 1.5 %collective-permute-start.7 = (bf16[16,7168]{1,0:T(8,128)(2,1)}, bf16[16,7168]{1,0:T(8,128)(2,1)S(1)}, u32[]{:S(2)}, u32[]{:S(2)}) collective-permute-start(bf16[16,7168]{1,0:T(8,128)(2,1)} %get-tuple-element.42), channel_id=1, source_target_pairs={{0,8},{1,33},{2,10},{3,35},{4,12},{5,37},{6,14},{7,39},{8,0},{9,41... | collective-permute-start | bytes 688136 | tf_op jit(solution)/shard_map/ppermute | solution.py:311
  69.8 2.1 %collective-permute-start.8 = (bf16[16,7168]{1,0:T(8,128)(2,1)}, bf16[16,7168]{1,0:T(8,128)(2,1)}, u32[]{:S(2)}, u32[]{:S(2)}) collective-permute-start(bf16[16,7168]{1,0:T(8,128)(2,1)} %get-tuple-element.41), channel_id=1, source_target_pairs={{0,4},{1,17},{2,6},{3,19},{4,8},{5,21},{6,10},{7,23},{8,12},{9,25}... | collective-permute-start | bytes 688136 | tf_op jit(solution)/shard_map/ppermute | solution.py:311
  71.8 0.0 collective-permute-start.9
  71.8 0.0 all-to-all-done.1
  71.9 2.1 %shard_map.71 = f32[8,32,128]{2,1,0:T(8,128)S(1)} custom-call(f32[8,32,128]{2,1,0:T(8,128)S(1)} %pad_maximum_fusion.1.g_ref, f32[1024,128]{1,0:T(8,128)S(1)} %get-tuple-element.35.ad_ref), custom_call_target="tpu_custom_call" | custom-call | tf_op jit(solution)/shard_map/pallas_call | solution.py:30
  74.0 0.3 reshape.39
  74.3 0.1 copy.17
  74.4 0.9 %reshape.40 = f32[4,8,1024]{2,1,0:T(8,128)} reshape(f32[4,2,4,32,32]{4,3,2,1,0:T(8,128)S(1)} %copy.17) | data formatting | bytes 262144 | tf_op jit(solution)/shard_map/reshape | solution.py:385
  75.3 0.8 collective-permute-done.7
  76.0 0.5 collective-permute-done.8
  76.5 2.9 %collective-permute-done.9 = bf16[16,7168]{1,0:T(8,128)(2,1)} collective-permute-done((bf16[16,7168]{1,0:T(8,128)(2,1)}, bf16[16,7168]{1,0:T(8,128)(2,1)}, u32[]{:S(2)}, u32[]{:S(2)}) %collective-permute-start.9) | collective-permute-done | bytes 229408 | tf_op jit(solution)/shard_map/ppermute | solution.py:311
  79.4 2.2 %add_convert_fusion.2 = bf16[16,7168]{1,0:T(8,128)(2,1)} fusion(bf16[16,7168]{1,0:T(8,128)(2,1)} %collective-permute-done.9, bf16[16,7168]{1,0:T(8,128)(2,1)} %collective-permute-done.8, bf16[16,7168]{1,0:T(8,128)(2,1)S(1)} %collective-permute-done.7, bf16[64,7168]{1,0:T(8,128)(2,1)} %collective-permute-done.4, bf16[64,7168]{1,0:T(8,128)(2,1)} %collective-permute-done.5, ...), kind=kLoop, calls=%fused_computation.2 | loop fusion | flops 1835008 | bytes 1835008 | tf_op jit(solution)/shard_map/convert_element_type | solution.py:388
  (13 shorter events, 0.2 us)
Async XLA Ops:
  2.4 19.3 %all-to-all-start = ((bf16[16,32,256]{2,1,0:T(8,128)(2,1)}), bf16[16,32,256]{2,1,0:T(8,128)(2,1)S(1)}, u32[]{:S(2)}, u32[]{:S(2)}) async-start(bf16[16,32,256]{2,1,0:T(8,128)(2,1)} %bitcast.1), calls=%async_computation | async-start | bytes 524288 | tf_op jit(solution)/shard_map/all_to_all | solution.py:316
  21.7 1.6 %collective-permute-start = (bf16[512,256]{1,0:T(8,128)(2,1)S(1)}, bf16[512,256]{1,0:T(8,128)(2,1)S(1)}, u32[]{:S(2)}, u32[]{:S(2)}) collective-permute-start(bf16[512,256]{1,0:T(8,128)(2,1)S(1)} %get-tuple-element.25), channel_id=1, source_target_pairs={{0,1},{1,0},{2,3},{3,2},{4,5},{5,4},{6,7},{7,6},{8,9},{9,8},{10,11... | collective-permute-start | bytes 786440 | tf_op jit(solution)/shard_map/ppermute | solution.py:352
  23.4 9.1 %collective-permute-start.1 = (bf16[512,256]{1,0:T(8,128)(2,1)S(1)}, bf16[512,256]{1,0:T(8,128)(2,1)S(1)}, u32[]{:S(2)}, u32[]{:S(2)}) collective-permute-start(bf16[512,256]{1,0:T(8,128)(2,1)S(1)} %add_convert_fusion.1), channel_id=1, source_target_pairs={{0,2},{1,3},{2,0},{3,1},{4,6},{5,7},{6,4},{7,5},{8,10},{9,11},{10,... | collective-permute-start | bytes 786440 | tf_op jit(solution)/shard_map/ppermute | solution.py:352
  30.9 34.8 %copy-start = (bf16[64,7168]{1,0:T(8,128)(2,1)S(1)}, bf16[64,7168]{1,0:T(8,128)(2,1)}, u32[]{:S(2)}) copy-start(bf16[64,7168]{1,0:T(8,128)(2,1)} %get-tuple-element.24) | copy-start | bytes 2752516
  30.9 14.9 %collective-permute-start.3 = (bf16[64,7168]{1,0:T(8,128)(2,1)}, bf16[64,7168]{1,0:T(8,128)(2,1)S(1)}, u32[]{:S(2)}, u32[]{:S(2)}) collective-permute-start(bf16[64,7168]{1,0:T(8,128)(2,1)} %get-tuple-element.28), channel_id=1, source_target_pairs={{0,16},{1,5},{2,18},{3,7},{4,20},{5,9},{6,22},{7,11},{8,24},{9,13}... | collective-permute-start | bytes 2752520 | tf_op jit(solution)/shard_map/ppermute | solution.py:311
  34.9 7.1 %collective-permute-start.2 = (f32[4,2,32,128]{3,2,1,0:T(8,128)S(1)}, f32[4,2,32,128]{3,2,1,0:T(8,128)S(1)}, u32[]{:S(2)}, u32[]{:S(2)}) collective-permute-start(f32[4,2,32,128]{3,2,1,0:T(8,128)S(1)} %slice_bitcast_fusion), channel_id=1, source_target_pairs={{0,64},{64,0},{1,65},{65,1},{2,66},{66,2},{3,67},{67,3},{4,68},{68... | collective-permute-start | bytes 393224 | tf_op jit(solution)/shard_map/ppermute | solution.py:357
  37.9 20.5 %collective-permute-start.5 = (bf16[64,7168]{1,0:T(8,128)(2,1)}, bf16[64,7168]{1,0:T(8,128)(2,1)}, u32[]{:S(2)}, u32[]{:S(2)}) collective-permute-start(bf16[64,7168]{1,0:T(8,128)(2,1)} %get-tuple-element.31), channel_id=1, source_target_pairs={{0,32},{1,9},{2,34},{3,11},{4,36},{5,13},{6,38},{7,15},{8,40},{9,1... | collective-permute-start | bytes 2752520 | tf_op jit(solution)/shard_map/ppermute | solution.py:311
  40.5 25.2 %collective-permute-start.4 = (bf16[64,7168]{1,0:T(8,128)(2,1)}, bf16[64,7168]{1,0:T(8,128)(2,1)}, u32[]{:S(2)}, u32[]{:S(2)}) collective-permute-start(bf16[64,7168]{1,0:T(8,128)(2,1)} %get-tuple-element.30), channel_id=1, source_target_pairs={{0,48},{1,13},{2,50},{3,15},{4,52},{5,1},{6,54},{7,3},{8,56},{9,5}... | collective-permute-start | bytes 2752520 | tf_op jit(solution)/shard_map/ppermute | solution.py:311
  45.8 12.5 %collective-permute-start.6 = (f32[2,32,128]{2,1,0:T(8,128)S(1)}, f32[2,32,128]{2,1,0:T(8,128)S(1)}, u32[]{:S(2)}, u32[]{:S(2)}) collective-permute-start(f32[2,32,128]{2,1,0:T(8,128)S(1)} %get-tuple-element.49), channel_id=1, source_target_pairs={{0,0},{4,8},{8,16},{12,24},{16,32},{20,40},{24,48},{28,56},{32,64}... | collective-permute-start | bytes 98312 | tf_op jit(solution)/shard_map/ppermute | solution.py:361
  49.4 22.5 %all-to-all-start.1 = ((bf16[16,2,32,128]{3,2,1,0:T(8,128)(2,1)}), bf16[16,2,32,128]{3,2,1,0:T(8,128)(2,1)S(1)}, u32[]{:S(2)}, u32[]{:S(2)}) async-start(bf16[16,2,32,128]{3,2,1,0:T(8,128)(2,1)} %pad_maximum_fusion), calls=%async_computation.1 | async-start | bytes 524288 | tf_op jit(solution)/shard_map/all_to_all | solution.py:370
  68.3 7.7 %collective-permute-start.7 = (bf16[16,7168]{1,0:T(8,128)(2,1)}, bf16[16,7168]{1,0:T(8,128)(2,1)S(1)}, u32[]{:S(2)}, u32[]{:S(2)}) collective-permute-start(bf16[16,7168]{1,0:T(8,128)(2,1)} %get-tuple-element.42), channel_id=1, source_target_pairs={{0,8},{1,33},{2,10},{3,35},{4,12},{5,37},{6,14},{7,39},{8,0},{9,41... | collective-permute-start | bytes 688136 | tf_op jit(solution)/shard_map/ppermute | solution.py:311
  69.8 6.7 %collective-permute-start.8 = (bf16[16,7168]{1,0:T(8,128)(2,1)}, bf16[16,7168]{1,0:T(8,128)(2,1)}, u32[]{:S(2)}, u32[]{:S(2)}) collective-permute-start(bf16[16,7168]{1,0:T(8,128)(2,1)} %get-tuple-element.41), channel_id=1, source_target_pairs={{0,4},{1,17},{2,6},{3,19},{4,8},{5,21},{6,10},{7,23},{8,12},{9,25}... | collective-permute-start | bytes 688136 | tf_op jit(solution)/shard_map/ppermute | solution.py:311
  71.8 7.5 %collective-permute-start.9 = (bf16[16,7168]{1,0:T(8,128)(2,1)}, bf16[16,7168]{1,0:T(8,128)(2,1)}, u32[]{:S(2)}, u32[]{:S(2)}) collective-permute-start(bf16[16,7168]{1,0:T(8,128)(2,1)} %get-tuple-element.40), channel_id=1, source_target_pairs={{0,12},{1,49},{2,14},{3,51},{4,0},{5,53},{6,2},{7,55},{8,4},{9,57}... | collective-permute-start | bytes 688136 | tf_op jit(solution)/shard_map/ppermute | solution.py:311

commit v4 on v3

--- a/solution.py
+++ b/solution.py
@@ -137,28 +137,40 @@
         skew = turned[i * BLOCK : (i + 1) * BLOCK, :] - turned[pl.ds(i, BLOCK, stride=BLOCK), :]
         mat[i] = jnp.where(sub == i, 1.0, 0.0) - skew
 
-    def step(k, carry):
-        here = sub == k
+    def step(pair, carry):
+        k = 2 * pair
+        here, next_here = sub == k, sub == k + 1
+        either = here | next_here
         pivot = 1.0 / mat[k, pl.ds(k, 1), :]
-        line = jnp.where(here, pivot, mat[k] * pivot)
+        first = jnp.where(here, pivot, mat[k] * pivot)
+        first_next = mat[k, pl.ds(k + 1, 1), :] * pivot
+        factor = mat[k + 1, pl.ds(k, 1), :]
+        second = jnp.where(here, 0.0, mat[k + 1]) - factor * first
+        pivot = 1.0 / (mat[k + 1, pl.ds(k + 1, 1), :] - factor * first_next)
+        second = jnp.where(next_here, pivot, second * pivot)
+        cut = jnp.where(next_here, 0.0, first)
         for i in range(BLOCK):
             factor = mat[i, pl.ds(k, 1), :]
-            mat[i] = jnp.where(here, 0.0, mat[i]) - factor * line
-        mat[k] = line
+            after = mat[i, pl.ds(k + 1, 1), :] - factor * first_next
+            mat[i] = jnp.where(either, 0.0, mat[i]) - factor * cut - after * second
+        mat[k] = cut - first_next * second
+        mat[k + 1] = second
         return carry
 
-    lax.fori_loop(0, BLOCK, step, 0)
+    lax.fori_loop(0, BLOCK // 2, step, 0)
     for i in range(BLOCK):
-        rows[pl.ds(i, LANES, stride=BLOCK), :] = mat[i].T
+        rows[pl.ds(i, 96, stride=BLOCK), :] = mat[i].T[:96]
     same = iota((LANES, LANES), 0) // BLOCK == iota((LANES, LANES), 1) // BLOCK
-    unit = jnp.where(iota((LANES, LANES), 0) == iota((LANES, LANES), 1), 1.0, 0.0)
+    spread = jnp.where(iota((BLOCK, LANES), 0) == iota((BLOCK, LANES), 1) % BLOCK, 1.0, 0.0).astype(BF)
+    unit = jnp.where(iota((LANES, BLOCK), 0) % BLOCK == iota((LANES, BLOCK), 1), 1.0, 0.0)
     for g in range(24):
         piece = rows[g * LANES : (g + 1) * LANES, :]
-        wide = jnp.where(same, jnp.concatenate([piece] * 4, axis=1), 0.0)
         if g < 16:
-            rotation = (2.0 * wide - unit).astype(BF)
+            rotation = dot((2.0 * piece - unit).astype(BF), spread, 1, 0)
+            rotation = jnp.where(same, rotation, 0.0).astype(BF)
             rot_ref[g * LANES : (g + 1) * LANES, :] = dot(onehot(idx_ref, g), rotation, 1, 0).astype(BF)
         else:
+            wide = jnp.where(same, jnp.concatenate([piece] * 4, axis=1), 0.0)
             inv_ref[(g - 16) * LANES : (g - 15) * LANES, :] = wide
     w_copy.wait()
     c_copy.wait()
@@ -334,7 +346,7 @@
             pltpu.VMEM((LANES, BLOCK * BLOCK), F32),
             pltpu.VMEM((BLOCK * BLOCK, LANES), F32),
             pltpu.VMEM((BLOCK, BLOCK, LANES), F32),
-            pltpu.VMEM((BLOCK * LANES, BLOCK), F32),
+            pltpu.VMEM((BLOCK * 96, BLOCK), F32),
             pltpu.VMEM((FACTORS, 8192), jnp.int32),
             pltpu.SemaphoreType.DMA,
             pltpu.SemaphoreType.DMA,

time: 81.9 us -> 80.4 us (0.982)
  Pallas kernels: 21.3 us -> 19.8 us
    pallas_call x1, Pallas kernels: 11 us -> 9.51 us  [local(): pl.pallas_call(prepare_body, out_shape=(shape((2048, LANES), BF), shape((...]
  transfers between devices with their start and end apart: 12 -> 12, of which waited for: 6 -> 6; matrix products, arithmetic and copies ran while one was open for 6% -> 6% of each run, Pallas kernels for 26% -> 25%
where the time goes in v4:
time: 80.4 us; the launch traced here: 80 us
  starting transfers between devices  33.6 us (42%)
  Pallas kernels  19.8 us (25%)
  waiting for transfers between devices  16.8 us (21%)
  other arithmetic  5.7 us (7%)
  local copies, waits for them, and re-layouts  3.27 us (4%)
  between operations  0.82 us (1%)
    ppermute x6, waiting for transfers between devices, ring(): return lax.ppermute(x, ('fsdp', 'tensor'), ring_pairs(stage, s))  15.3 us
    pallas_call x1, Pallas kernels, local(): pl.pallas_call(prepare_body, out_shape=(shape((2048, LANES), BF), shape((...  9.51 us
    ppermute x6, starting transfers between devices, ring(): return lax.ppermute(x, ('fsdp', 'tensor'), ring_pairs(stage, s))  9.21 us
    all_to_all x1, starting transfers between devices, local(): slots = lax.all_to_all(slots.astype(BF), 'fsdp', 0, 0, tiled=True)  8.98 us
    all_to_all x1, starting transfers between devices, local(): lax.all_to_all(activations.T.reshape(16, BLOCK, tokens), 'fsdp', 0, 0, ti...  8.26 us
    pallas_call x1, Pallas kernels, forward(): pl.pallas_call(functools.partial(forward_body, tiles=tiles), out_shape=[p...  5.85 us
    pallas_call x2, Pallas kernels, call(): pl.pallas_call(body, out_shape=out_shape, in_specs=[pl.BlockSpec(memory_s...  4.41 us
    ppermute x1, starting transfers between devices, local(): grads = grads[0] + lax.ppermute(grads[1], 'dp', [(0, 1), (1, 0)])  2.97 us
  transfers between devices with their start and end apart: 12, of which 6 were waited for; matrix products, arithmetic and copies ran while one was open for 6% of the time, Pallas kernels for 25%

profile of v4, /device:TPU:6, one launch (start us, length us, event | category | flops | bytes accessed | tf_op | source)
XLA Modules:
  0.0 80.0 jit_solution(117823819228227030)
XLA Ops:
  0.6 1.8 %copy.13 = bf16[256,512]{0,1:T(8,128)(2,1)} copy(bf16[256,512]{1,0:T(8,128)(2,1)} %param.5) | data formatting | bytes 524288 | tf_op args[0]
  2.4 8.3 %all-to-all-start = ((bf16[16,32,256]{2,1,0:T(8,128)(2,1)}), bf16[16,32,256]{2,1,0:T(8,128)(2,1)S(1)}, u32[]{:S(2)}, u32[]{:S(2)}) async-start(bf16[16,32,256]{2,1,0:T(8,128)(2,1)} %bitcast.1), calls=%async_computation | async-start | bytes 524288 | tf_op jit(solution)/shard_map/all_to_all | solution.py:328
  10.7 9.5 %shard_map.68 = (bf16[2048,128]{1,0:T(8,128)(2,1)S(1)}, f32[1024,128]{1,0:T(8,128)S(1)}, s32[16,128]{1,0:T(8,128)S(1)}, bf16[512,256]{1,0:T(8,128)(2,1)S(1)}) custom-call(f32[4,256,1024]{2,1,0:T(8,128)} %params.1, s32[4,8192]{1,0:T(4,128)} %perms.1, bf16[512,7168]{1,0:T(8,128)(2,1)} %weight.3, bf16[256,7168]{1,0:T(8,128)(2,1)} %cotan.1), custom_call_target="tpu_custom_call" | custom-call | tf_op jit(solution)/shard_map/pallas_call | solution.py:332
  20.2 0.0 all-to-all-done
  20.2 0.1 collective-permute-start
  20.3 1.5 %collective-permute-done = bf16[512,256]{1,0:T(8,128)(2,1)S(1)} collective-permute-done((bf16[512,256]{1,0:T(8,128)(2,1)S(1)}, bf16[512,256]{1,0:T(8,128)(2,1)S(1)}, u32[]{:S(2)}, u32[]{:S(2)}) %collective-permute-start) | collective-permute-done | bytes 262176 | tf_op jit(solution)/shard_map/ppermute | solution.py:364
  21.8 0.1 add_convert_fusion.1
  21.9 1.7 %collective-permute-start.1 = (bf16[512,256]{1,0:T(8,128)(2,1)S(1)}, bf16[512,256]{1,0:T(8,128)(2,1)S(1)}, u32[]{:S(2)}, u32[]{:S(2)}) collective-permute-start(bf16[512,256]{1,0:T(8,128)(2,1)S(1)} %add_convert_fusion.1), channel_id=1, source_target_pairs={{0,2},{1,3},{2,0},{3,1},{4,6},{5,7},{6,4},{7,5},{8,10},{9,11},{10,... | collective-permute-start | bytes 786440 | tf_op jit(solution)/shard_map/ppermute | solution.py:364
  23.6 5.9 %shard_map.69 = (bf16[64,7168]{1,0:T(8,128)(2,1)}, bf16[64,7168]{1,0:T(8,128)(2,1)}, bf16[64,7168]{1,0:T(8,128)(2,1)}, bf16[64,7168]{1,0:T(8,128)(2,1)}, bf16[4,512,256]{2,1,0:T(8,128)(2,1)S(1)}) custom-call(bf16[512,256]{1,0:T(8,128)(2,1)S(1)} %bitcast.41, bf16[2048,128]{1,0:T(8,128)(2,1)S(1)} %get-tuple-element.23.rot_ref, bf16[512,7168]{1,0:T(8,128)(2,1)} %weight.3), custom_call_target="tpu_custom_call" | custom-call | tf_op jit(solution)/shard_map/pallas_call | solution.py:260
  29.4 0.0 copy-start
  29.4 1.5 %collective-permute-start.3 = (bf16[64,7168]{1,0:T(8,128)(2,1)}, bf16[64,7168]{1,0:T(8,128)(2,1)S(1)}, u32[]{:S(2)}, u32[]{:S(2)}) collective-permute-start(bf16[64,7168]{1,0:T(8,128)(2,1)} %get-tuple-element.28), channel_id=1, source_target_pairs={{0,16},{1,5},{2,18},{3,7},{4,20},{5,9},{6,22},{7,11},{8,24},{9,13}... | collective-permute-start | bytes 2752520 | tf_op jit(solution)/shard_map/ppermute | solution.py:323
  31.0 0.0 collective-permute-done.1
  31.0 0.1 add_convert_fusion.up_ref
  31.0 2.3 %shard_map.70 = f32[2,4,2,32,128]{4,3,2,1,0:T(8,128)S(1)} custom-call(bf16[512,256]{1,0:T(8,128)(2,1)S(1)} %add_convert_fusion.up_ref, bf16[4,512,256]{2,1,0:T(8,128)(2,1)S(1)} %get-tuple-element.26.saved_ref, bf16[2048,128]{1,0:T(8,128)(2,1)S(1)} %get-tuple-element.23.rot_ref, s32[16,128]{1,0:T(8,128)S(1)} %get-tuple-element.27.idx_ref), custom_call_target="tpu_custom_call" | custom-call | tf_op jit(solution)/shard_map/pallas_call | solution.py:30
  33.4 3.0 %collective-permute-start.2 = (f32[4,2,32,128]{3,2,1,0:T(8,128)S(1)}, f32[4,2,32,128]{3,2,1,0:T(8,128)S(1)}, u32[]{:S(2)}, u32[]{:S(2)}) collective-permute-start(f32[4,2,32,128]{3,2,1,0:T(8,128)S(1)} %slice_bitcast_fusion), channel_id=1, source_target_pairs={{0,64},{64,0},{1,65},{65,1},{2,66},{66,2},{3,67},{67,3},{4,68},{68... | collective-permute-start | bytes 393224 | tf_op jit(solution)/shard_map/ppermute | solution.py:369
  36.3 2.7 %collective-permute-start.5 = (bf16[64,7168]{1,0:T(8,128)(2,1)}, bf16[64,7168]{1,0:T(8,128)(2,1)}, u32[]{:S(2)}, u32[]{:S(2)}) collective-permute-start(bf16[64,7168]{1,0:T(8,128)(2,1)} %get-tuple-element.31), channel_id=1, source_target_pairs={{0,32},{1,9},{2,34},{3,11},{4,36},{5,13},{6,38},{7,15},{8,40},{9,1... | collective-permute-start | bytes 2752520 | tf_op jit(solution)/shard_map/ppermute | solution.py:323
  39.0 1.5 %collective-permute-start.4 = (bf16[64,7168]{1,0:T(8,128)(2,1)}, bf16[64,7168]{1,0:T(8,128)(2,1)}, u32[]{:S(2)}, u32[]{:S(2)}) collective-permute-start(bf16[64,7168]{1,0:T(8,128)(2,1)} %get-tuple-element.30), channel_id=1, source_target_pairs={{0,48},{1,13},{2,50},{3,15},{4,52},{5,1},{6,54},{7,3},{8,56},{9,5}... | collective-permute-start | bytes 2752520 | tf_op jit(solution)/shard_map/ppermute | solution.py:323
  40.5 0.0 collective-permute-done.2
  40.5 3.8 %collective-permute-done.3 = bf16[64,7168]{1,0:T(8,128)(2,1)S(1)} collective-permute-done((bf16[64,7168]{1,0:T(8,128)(2,1)}, bf16[64,7168]{1,0:T(8,128)(2,1)S(1)}, u32[]{:S(2)}, u32[]{:S(2)}) %collective-permute-start.3) | collective-permute-done | bytes 917536 | tf_op jit(solution)/shard_map/ppermute | solution.py:323
  44.3 2.4 %collective-permute-start.6 = (f32[2,32,128]{2,1,0:T(8,128)S(1)}, f32[2,32,128]{2,1,0:T(8,128)S(1)}, u32[]{:S(2)}, u32[]{:S(2)}) collective-permute-start(f32[2,32,128]{2,1,0:T(8,128)S(1)} %get-tuple-element.49), channel_id=1, source_target_pairs={{0,0},{4,8},{8,16},{12,24},{16,32},{20,40},{24,48},{28,56},{32,64}... | collective-permute-start | bytes 98312 | tf_op jit(solution)/shard_map/ppermute | solution.py:373
  46.8 0.1 select_n.56
  46.9 0.1 select_n.60
  47.0 0.1 maximum_convert_fusion
  47.1 0.7 pad_maximum_fusion
  47.9 9.0 %all-to-all-start.1 = ((bf16[16,2,32,128]{3,2,1,0:T(8,128)(2,1)}), bf16[16,2,32,128]{3,2,1,0:T(8,128)(2,1)S(1)}, u32[]{:S(2)}, u32[]{:S(2)}) async-start(bf16[16,2,32,128]{3,2,1,0:T(8,128)(2,1)} %pad_maximum_fusion), calls=%async_computation.1 | async-start | bytes 524288 | tf_op jit(solution)/shard_map/all_to_all | solution.py:382
  56.8 0.0 collective-permute-done.5
  56.8 0.0 collective-permute-done.6
  56.8 7.4 %collective-permute-done.4 = bf16[64,7168]{1,0:T(8,128)(2,1)} collective-permute-done((bf16[64,7168]{1,0:T(8,128)(2,1)}, bf16[64,7168]{1,0:T(8,128)(2,1)}, u32[]{:S(2)}, u32[]{:S(2)}) %collective-permute-start.4) | collective-permute-done | bytes 917536 | tf_op jit(solution)/shard_map/ppermute | solution.py:323
  64.3 0.0 copy-done
  64.3 2.5 %add_convert_fusion.3 = (bf16[16,7168]{1,0:T(8,128)(2,1)}, bf16[16,7168]{1,0:T(8,128)(2,1)}, bf16[16,7168]{1,0:T(8,128)(2,1)}) fusion(bf16[64,7168]{1,0:T(8,128)(2,1)} %collective-permute-done.4, bf16[64,7168]{1,0:T(8,128)(2,1)} %collective-permute-done.5, bf16[64,7168]{1,0:T(8,128)(2,1)S(1)} %collective-permute-done.3, bf16[64,7168]{1,0:T(8,128)(2,1)S(1)} %copy-done), kind=kLoop, calls=%fused_computation.3 | loop fusion | flops 2752512 | bytes 3440640 | tf_op jit(solution)/shard_map/convert_element_type | solution.py:386
  66.8 1.5 %collective-permute-start.7 = (bf16[16,7168]{1,0:T(8,128)(2,1)}, bf16[16,7168]{1,0:T(8,128)(2,1)S(1)}, u32[]{:S(2)}, u32[]{:S(2)}) collective-permute-start(bf16[16,7168]{1,0:T(8,128)(2,1)} %get-tuple-element.42), channel_id=1, source_target_pairs={{0,8},{1,33},{2,10},{3,35},{4,12},{5,37},{6,14},{7,39},{8,0},{9,41... | collective-permute-start | bytes 688136 | tf_op jit(solution)/shard_map/ppermute | solution.py:323
  68.2 2.1 %collective-permute-start.8 = (bf16[16,7168]{1,0:T(8,128)(2,1)}, bf16[16,7168]{1,0:T(8,128)(2,1)}, u32[]{:S(2)}, u32[]{:S(2)}) collective-permute-start(bf16[16,7168]{1,0:T(8,128)(2,1)} %get-tuple-element.41), channel_id=1, source_target_pairs={{0,4},{1,17},{2,6},{3,19},{4,8},{5,21},{6,10},{7,23},{8,12},{9,25}... | collective-permute-start | bytes 688136 | tf_op jit(solution)/shard_map/ppermute | solution.py:323
  70.3 0.0 collective-permute-start.9
  70.3 0.0 all-to-all-done.1
  70.4 2.1 %shard_map.71 = f32[8,32,128]{2,1,0:T(8,128)S(1)} custom-call(f32[8,32,128]{2,1,0:T(8,128)S(1)} %pad_maximum_fusion.1.g_ref, f32[1024,128]{1,0:T(8,128)S(1)} %get-tuple-element.35.ad_ref), custom_call_target="tpu_custom_call" | custom-call | tf_op jit(solution)/shard_map/pallas_call | solution.py:30
  72.5 0.3 reshape.39
  72.8 0.1 copy.17
  72.9 0.9 %reshape.40 = f32[4,8,1024]{2,1,0:T(8,128)} reshape(f32[4,2,4,32,32]{4,3,2,1,0:T(8,128)S(1)} %copy.17) | data formatting | bytes 262144 | tf_op jit(solution)/shard_map/reshape | solution.py:397
  73.8 0.8 collective-permute-done.7
  74.5 0.4 collective-permute-done.8
  75.0 2.9 %collective-permute-done.9 = bf16[16,7168]{1,0:T(8,128)(2,1)} collective-permute-done((bf16[16,7168]{1,0:T(8,128)(2,1)}, bf16[16,7168]{1,0:T(8,128)(2,1)}, u32[]{:S(2)}, u32[]{:S(2)}) %collective-permute-start.9) | collective-permute-done | bytes 229408 | tf_op jit(solution)/shard_map/ppermute | solution.py:323
  77.8 2.2 %add_convert_fusion.2 = bf16[16,7168]{1,0:T(8,128)(2,1)} fusion(bf16[16,7168]{1,0:T(8,128)(2,1)} %collective-permute-done.9, bf16[16,7168]{1,0:T(8,128)(2,1)} %collective-permute-done.8, bf16[16,7168]{1,0:T(8,128)(2,1)S(1)} %collective-permute-done.7, bf16[64,7168]{1,0:T(8,128)(2,1)} %collective-permute-done.4, bf16[64,7168]{1,0:T(8,128)(2,1)} %collective-permute-done.5, ...), kind=kLoop, calls=%fused_computation.2 | loop fusion | flops 1835008 | bytes 1835008 | tf_op jit(solution)/shard_map/convert_element_type | solution.py:400
  (13 shorter events, 0.2 us)
Async XLA Ops:
  2.4 17.8 %all-to-all-start = ((bf16[16,32,256]{2,1,0:T(8,128)(2,1)}), bf16[16,32,256]{2,1,0:T(8,128)(2,1)S(1)}, u32[]{:S(2)}, u32[]{:S(2)}) async-start(bf16[16,32,256]{2,1,0:T(8,128)(2,1)} %bitcast.1), calls=%async_computation | async-start | bytes 524288 | tf_op jit(solution)/shard_map/all_to_all | solution.py:328
  20.2 1.6 %collective-permute-start = (bf16[512,256]{1,0:T(8,128)(2,1)S(1)}, bf16[512,256]{1,0:T(8,128)(2,1)S(1)}, u32[]{:S(2)}, u32[]{:S(2)}) collective-permute-start(bf16[512,256]{1,0:T(8,128)(2,1)S(1)} %get-tuple-element.25), channel_id=1, source_target_pairs={{0,1},{1,0},{2,3},{3,2},{4,5},{5,4},{6,7},{7,6},{8,9},{9,8},{10,11... | collective-permute-start | bytes 786440 | tf_op jit(solution)/shard_map/ppermute | solution.py:364
  21.9 9.1 %collective-permute-start.1 = (bf16[512,256]{1,0:T(8,128)(2,1)S(1)}, bf16[512,256]{1,0:T(8,128)(2,1)S(1)}, u32[]{:S(2)}, u32[]{:S(2)}) collective-permute-start(bf16[512,256]{1,0:T(8,128)(2,1)S(1)} %add_convert_fusion.1), channel_id=1, source_target_pairs={{0,2},{1,3},{2,0},{3,1},{4,6},{5,7},{6,4},{7,5},{8,10},{9,11},{10,... | collective-permute-start | bytes 786440 | tf_op jit(solution)/shard_map/ppermute | solution.py:364
  29.4 34.8 %copy-start = (bf16[64,7168]{1,0:T(8,128)(2,1)S(1)}, bf16[64,7168]{1,0:T(8,128)(2,1)}, u32[]{:S(2)}) copy-start(bf16[64,7168]{1,0:T(8,128)(2,1)} %get-tuple-element.24) | copy-start | bytes 2752516
  29.4 14.9 %collective-permute-start.3 = (bf16[64,7168]{1,0:T(8,128)(2,1)}, bf16[64,7168]{1,0:T(8,128)(2,1)S(1)}, u32[]{:S(2)}, u32[]{:S(2)}) collective-permute-start(bf16[64,7168]{1,0:T(8,128)(2,1)} %get-tuple-element.28), channel_id=1, source_target_pairs={{0,16},{1,5},{2,18},{3,7},{4,20},{5,9},{6,22},{7,11},{8,24},{9,13}... | collective-permute-start | bytes 2752520 | tf_op jit(solution)/shard_map/ppermute | solution.py:323
  33.4 7.1 %collective-permute-start.2 = (f32[4,2,32,128]{3,2,1,0:T(8,128)S(1)}, f32[4,2,32,128]{3,2,1,0:T(8,128)S(1)}, u32[]{:S(2)}, u32[]{:S(2)}) collective-permute-start(f32[4,2,32,128]{3,2,1,0:T(8,128)S(1)} %slice_bitcast_fusion), channel_id=1, source_target_pairs={{0,64},{64,0},{1,65},{65,1},{2,66},{66,2},{3,67},{67,3},{4,68},{68... | collective-permute-start | bytes 393224 | tf_op jit(solution)/shard_map/ppermute | solution.py:369
  36.3 20.5 %collective-permute-start.5 = (bf16[64,7168]{1,0:T(8,128)(2,1)}, bf16[64,7168]{1,0:T(8,128)(2,1)}, u32[]{:S(2)}, u32[]{:S(2)}) collective-permute-start(bf16[64,7168]{1,0:T(8,128)(2,1)} %get-tuple-element.31), channel_id=1, source_target_pairs={{0,32},{1,9},{2,34},{3,11},{4,36},{5,13},{6,38},{7,15},{8,40},{9,1... | collective-permute-start | bytes 2752520 | tf_op jit(solution)/shard_map/ppermute | solution.py:323
  39.0 25.2 %collective-permute-start.4 = (bf16[64,7168]{1,0:T(8,128)(2,1)}, bf16[64,7168]{1,0:T(8,128)(2,1)}, u32[]{:S(2)}, u32[]{:S(2)}) collective-permute-start(bf16[64,7168]{1,0:T(8,128)(2,1)} %get-tuple-element.30), channel_id=1, source_target_pairs={{0,48},{1,13},{2,50},{3,15},{4,52},{5,1},{6,54},{7,3},{8,56},{9,5}... | collective-permute-start | bytes 2752520 | tf_op jit(solution)/shard_map/ppermute | solution.py:323
  44.3 12.5 %collective-permute-start.6 = (f32[2,32,128]{2,1,0:T(8,128)S(1)}, f32[2,32,128]{2,1,0:T(8,128)S(1)}, u32[]{:S(2)}, u32[]{:S(2)}) collective-permute-start(f32[2,32,128]{2,1,0:T(8,128)S(1)} %get-tuple-element.49), channel_id=1, source_target_pairs={{0,0},{4,8},{8,16},{12,24},{16,32},{20,40},{24,48},{28,56},{32,64}... | collective-permute-start | bytes 98312 | tf_op jit(solution)/shard_map/ppermute | solution.py:373
  47.9 22.5 %all-to-all-start.1 = ((bf16[16,2,32,128]{3,2,1,0:T(8,128)(2,1)}), bf16[16,2,32,128]{3,2,1,0:T(8,128)(2,1)S(1)}, u32[]{:S(2)}, u32[]{:S(2)}) async-start(bf16[16,2,32,128]{3,2,1,0:T(8,128)(2,1)} %pad_maximum_fusion), calls=%async_computation.1 | async-start | bytes 524288 | tf_op jit(solution)/shard_map/all_to_all | solution.py:382
  66.8 7.7 %collective-permute-start.7 = (bf16[16,7168]{1,0:T(8,128)(2,1)}, bf16[16,7168]{1,0:T(8,128)(2,1)S(1)}, u32[]{:S(2)}, u32[]{:S(2)}) collective-permute-start(bf16[16,7168]{1,0:T(8,128)(2,1)} %get-tuple-element.42), channel_id=1, source_target_pairs={{0,8},{1,33},{2,10},{3,35},{4,12},{5,37},{6,14},{7,39},{8,0},{9,41... | collective-permute-start | bytes 688136 | tf_op jit(solution)/shard_map/ppermute | solution.py:323
  68.2 6.7 %collective-permute-start.8 = (bf16[16,7168]{1,0:T(8,128)(2,1)}, bf16[16,7168]{1,0:T(8,128)(2,1)}, u32[]{:S(2)}, u32[]{:S(2)}) collective-permute-start(bf16[16,7168]{1,0:T(8,128)(2,1)} %get-tuple-element.41), channel_id=1, source_target_pairs={{0,4},{1,17},{2,6},{3,19},{4,8},{5,21},{6,10},{7,23},{8,12},{9,25}... | collective-permute-start | bytes 688136 | tf_op jit(solution)/shard_map/ppermute | solution.py:323
  70.3 7.5 %collective-permute-start.9 = (bf16[16,7168]{1,0:T(8,128)(2,1)}, bf16[16,7168]{1,0:T(8,128)(2,1)}, u32[]{:S(2)}, u32[]{:S(2)}) collective-permute-start(bf16[16,7168]{1,0:T(8,128)(2,1)} %get-tuple-element.40), channel_id=1, source_target_pairs={{0,12},{1,49},{2,14},{3,51},{4,0},{5,53},{6,2},{7,55},{8,4},{9,57}... | collective-permute-start | bytes 688136 | tf_op jit(solution)/shard_map/ppermute | solution.py:323

commit v5 on v4

--- a/solution.py
+++ b/solution.py
@@ -367,7 +367,7 @@
         backward_body, shape((2, FACTORS, 2, BLOCK, LANES), F32), (up, saved, rot, idx)
     )
     grads = grads[0] + lax.ppermute(grads[1], "dp", [(0, 1), (1, 0)])
-    grads, near = lax.optimization_barrier((grads, near))
+    grads, across = lax.optimization_barrier((grads, across))
 
     f = lax.axis_index("fsdp")
     level3 = lax.ppermute(
@@ -381,7 +381,7 @@
     slots = jnp.stack([jnp.repeat(spots, 4, axis=0), jnp.repeat(grads[1], 8, axis=0)], axis=1)
     slots = lax.all_to_all(slots.astype(BF), "fsdp", 0, 0, tiled=True)
 
-    across, level3 = lax.optimization_barrier((across, level3))
+    near, level3 = lax.optimization_barrier((near, level3))
     parts = [parts[0], near, back, across]
     wide = [sum(p[k * RUN : (k + 1) * RUN].astype(F32) for p in parts).astype(BF) for k in range(4)]
     last = [ring(wide[s], 1, s) for s in (2, 1, 3)]

time: 80.4 us -> 74 us (0.920)
  waiting for transfers between devices: 16.8 us -> 9.24 us
  starting transfers between devices: 33.6 us -> 34.8 us
    ppermute x6, waiting for transfers between devices: 15.3 us -> 7.15 us  [ring(): return lax.ppermute(x, ('fsdp', 'tensor'), ring_pairs(stage, s))]
    ppermute x1, starting transfers between devices: 2.44 us -> 3.65 us  [local(): lax.ppermute(grads[3], ('dp', 'fsdp'), [(e * 16 + s, s // 8 * 16 + s % 8...]
  transfers between devices with their start and end apart: 12 -> 12, of which waited for: 6 -> 7; matrix products, arithmetic and copies ran while one was open for 6% -> 7% of each run, Pallas kernels for 25% -> 27%
where the time goes in v5:
time: 74 us; the launch traced here: 73.7 us
  starting transfers between devices  34.8 us (47%)
  Pallas kernels  19.8 us (27%)
  waiting for transfers between devices  9.24 us (12%)
  other arithmetic  5.7 us (8%)
  local copies, waits for them, and re-layouts  3.27 us (4%)
  between operations  0.84 us (1%)
    ppermute x6, starting transfers between devices, ring(): return lax.ppermute(x, ('fsdp', 'tensor'), ring_pairs(stage, s))  9.83 us
    pallas_call x1, Pallas kernels, local(): pl.pallas_call(prepare_body, out_shape=(shape((2048, LANES), BF), shape((...  9.51 us
    all_to_all x1, starting transfers between devices, local(): slots = lax.all_to_all(slots.astype(BF), 'fsdp', 0, 0, tiled=True)  8.37 us
    all_to_all x1, starting transfers between devices, local(): lax.all_to_all(activations.T.reshape(16, BLOCK, tokens), 'fsdp', 0, 0, ti...  8.26 us
    ppermute x6, waiting for transfers between devices, ring(): return lax.ppermute(x, ('fsdp', 'tensor'), ring_pairs(stage, s))  7.15 us
    pallas_call x1, Pallas kernels, forward(): pl.pallas_call(functools.partial(forward_body, tiles=tiles), out_shape=[p...  5.85 us
    pallas_call x2, Pallas kernels, call(): pl.pallas_call(body, out_shape=out_shape, in_specs=[pl.BlockSpec(memory_s...  4.41 us
    ppermute x1, starting transfers between devices, local(): lax.ppermute(grads[3], ('dp', 'fsdp'), [(e * 16 + s, s // 8 * 16 + s % 8...  3.65 us
  transfers between devices with their start and end apart: 12, of which 7 were waited for; matrix products, arithmetic and copies ran while one was open for 7% of the time, Pallas kernels for 27%

profile of v5, /device:TPU:6, one launch (start us, length us, event | category | flops | bytes accessed | tf_op | source)
XLA Modules:
  0.0 73.7 jit_solution(15272169140548152242)
XLA Ops:
  0.6 1.8 %copy.13 = bf16[256,512]{0,1:T(8,128)(2,1)} copy(bf16[256,512]{1,0:T(8,128)(2,1)} %param.5) | data formatting | bytes 524288 | tf_op args[0]
  2.4 8.3 %all-to-all-start = ((bf16[16,32,256]{2,1,0:T(8,128)(2,1)}), bf16[16,32,256]{2,1,0:T(8,128)(2,1)S(1)}, u32[]{:S(2)}, u32[]{:S(2)}) async-start(bf16[16,32,256]{2,1,0:T(8,128)(2,1)} %bitcast.1), calls=%async_computation | async-start | bytes 524288 | tf_op jit(solution)/shard_map/all_to_all | solution.py:328
  10.7 9.5 %shard_map.68 = (bf16[2048,128]{1,0:T(8,128)(2,1)S(1)}, f32[1024,128]{1,0:T(8,128)S(1)}, s32[16,128]{1,0:T(8,128)S(1)}, bf16[512,256]{1,0:T(8,128)(2,1)S(1)}) custom-call(f32[4,256,1024]{2,1,0:T(8,128)} %params.1, s32[4,8192]{1,0:T(4,128)} %perms.1, bf16[512,7168]{1,0:T(8,128)(2,1)} %weight.3, bf16[256,7168]{1,0:T(8,128)(2,1)} %cotan.1), custom_call_target="tpu_custom_call" | custom-call | tf_op jit(solution)/shard_map/pallas_call | solution.py:332
  20.2 0.0 all-to-all-done
  20.2 0.1 collective-permute-start.1
  20.3 1.5 %collective-permute-done.1 = bf16[512,256]{1,0:T(8,128)(2,1)S(1)} collective-permute-done((bf16[512,256]{1,0:T(8,128)(2,1)S(1)}, bf16[512,256]{1,0:T(8,128)(2,1)S(1)}, u32[]{:S(2)}, u32[]{:S(2)}) %collective-permute-start.1) | collective-permute-done | bytes 262176 | tf_op jit(solution)/shard_map/ppermute | solution.py:364
  21.8 0.1 add_convert_fusion.1
  21.9 1.7 %collective-permute-start.2 = (bf16[512,256]{1,0:T(8,128)(2,1)S(1)}, bf16[512,256]{1,0:T(8,128)(2,1)S(1)}, u32[]{:S(2)}, u32[]{:S(2)}) collective-permute-start(bf16[512,256]{1,0:T(8,128)(2,1)S(1)} %add_convert_fusion.1), channel_id=1, source_target_pairs={{0,2},{1,3},{2,0},{3,1},{4,6},{5,7},{6,4},{7,5},{8,10},{9,11},{10,... | collective-permute-start | bytes 786440 | tf_op jit(solution)/shard_map/ppermute | solution.py:364
  23.6 5.9 %shard_map.69 = (bf16[64,7168]{1,0:T(8,128)(2,1)}, bf16[64,7168]{1,0:T(8,128)(2,1)}, bf16[64,7168]{1,0:T(8,128)(2,1)}, bf16[64,7168]{1,0:T(8,128)(2,1)}, bf16[4,512,256]{2,1,0:T(8,128)(2,1)S(1)}) custom-call(bf16[512,256]{1,0:T(8,128)(2,1)S(1)} %bitcast.41, bf16[2048,128]{1,0:T(8,128)(2,1)S(1)} %get-tuple-element.23.rot_ref, bf16[512,7168]{1,0:T(8,128)(2,1)} %weight.3), custom_call_target="tpu_custom_call" | custom-call | tf_op jit(solution)/shard_map/pallas_call | solution.py:260
  29.4 0.0 copy-start
  29.4 3.1 %collective-permute-start.4 = (bf16[64,7168]{1,0:T(8,128)(2,1)}, bf16[64,7168]{1,0:T(8,128)(2,1)S(1)}, u32[]{:S(2)}, u32[]{:S(2)}) collective-permute-start(bf16[64,7168]{1,0:T(8,128)(2,1)} %get-tuple-element.29), channel_id=1, source_target_pairs={{0,32},{1,9},{2,34},{3,11},{4,36},{5,13},{6,38},{7,15},{8,40},{9,1... | collective-permute-start | bytes 2752520 | tf_op jit(solution)/shard_map/ppermute | solution.py:323
  32.5 0.0 collective-permute-done.2
  32.5 0.1 add_convert_fusion.up_ref
  32.5 2.3 %shard_map.70 = f32[2,4,2,32,128]{4,3,2,1,0:T(8,128)S(1)} custom-call(bf16[512,256]{1,0:T(8,128)(2,1)S(1)} %add_convert_fusion.up_ref, bf16[4,512,256]{2,1,0:T(8,128)(2,1)S(1)} %get-tuple-element.27.saved_ref, bf16[2048,128]{1,0:T(8,128)(2,1)S(1)} %get-tuple-element.23.rot_ref, s32[16,128]{1,0:T(8,128)S(1)} %get-tuple-element.28.idx_ref), custom_call_target="tpu_custom_call" | custom-call | tf_op jit(solution)/shard_map/pallas_call | solution.py:30
  34.9 3.0 %collective-permute-start.3 = (f32[4,2,32,128]{3,2,1,0:T(8,128)S(1)}, f32[4,2,32,128]{3,2,1,0:T(8,128)S(1)}, u32[]{:S(2)}, u32[]{:S(2)}) collective-permute-start(f32[4,2,32,128]{3,2,1,0:T(8,128)S(1)} %slice_bitcast_fusion), channel_id=1, source_target_pairs={{0,64},{64,0},{1,65},{65,1},{2,66},{66,2},{3,67},{67,3},{4,68},{68... | collective-permute-start | bytes 393224 | tf_op jit(solution)/shard_map/ppermute | solution.py:369
  37.9 0.6 collective-permute-start
  38.4 2.7 %collective-permute-start.6 = (bf16[64,7168]{1,0:T(8,128)(2,1)}, bf16[64,7168]{1,0:T(8,128)(2,1)}, u32[]{:S(2)}, u32[]{:S(2)}) collective-permute-start(bf16[64,7168]{1,0:T(8,128)(2,1)} %get-tuple-element.32), channel_id=1, source_target_pairs={{0,48},{1,13},{2,50},{3,15},{4,52},{5,1},{6,54},{7,3},{8,56},{9,5}... | collective-permute-start | bytes 2752520 | tf_op jit(solution)/shard_map/ppermute | solution.py:323
  41.1 0.3 collective-permute-done.3
  41.4 3.3 %collective-permute-done.4 = bf16[64,7168]{1,0:T(8,128)(2,1)S(1)} collective-permute-done((bf16[64,7168]{1,0:T(8,128)(2,1)}, bf16[64,7168]{1,0:T(8,128)(2,1)S(1)}, u32[]{:S(2)}, u32[]{:S(2)}) %collective-permute-start.4) | collective-permute-done | bytes 917536 | tf_op jit(solution)/shard_map/ppermute | solution.py:323
  44.7 3.7 %collective-permute-start.5 = (f32[2,32,128]{2,1,0:T(8,128)S(1)}, f32[2,32,128]{2,1,0:T(8,128)S(1)}, u32[]{:S(2)}, u32[]{:S(2)}) collective-permute-start(f32[2,32,128]{2,1,0:T(8,128)S(1)} %get-tuple-element.49), channel_id=1, source_target_pairs={{0,0},{4,8},{8,16},{12,24},{16,32},{20,40},{24,48},{28,56},{32,64}... | collective-permute-start | bytes 98312 | tf_op jit(solution)/shard_map/ppermute | solution.py:373
  48.4 0.1 select_n.56
  48.5 0.1 select_n.60
  48.6 0.1 maximum_convert_fusion
  48.7 0.7 %pad_maximum_fusion = bf16[16,2,32,128]{3,2,1,0:T(8,128)(2,1)} fusion(bf16[16,1,32,128]{3,2,1,0:T(8,128)(2,1)S(1)} %bitcast.44, bf16[16,1,32,128]{3,2,1,0:T(8,128)(2,1)S(1)} %bitcast.43), kind=kLoop, calls=%fused_computation.7 | loop fusion | flops 131072 | bytes 524288 | tf_op jit(solution)/shard_map/stack | solution.py:381
  49.5 8.4 %all-to-all-start.1 = ((bf16[16,2,32,128]{3,2,1,0:T(8,128)(2,1)}), bf16[16,2,32,128]{3,2,1,0:T(8,128)(2,1)S(1)}, u32[]{:S(2)}, u32[]{:S(2)}) async-start(bf16[16,2,32,128]{3,2,1,0:T(8,128)(2,1)} %pad_maximum_fusion), calls=%async_computation.1 | async-start | bytes 524288 | tf_op jit(solution)/shard_map/all_to_all | solution.py:382
  57.8 0.0 collective-permute-done
  57.8 0.0 collective-permute-done.5
  57.9 0.0 collective-permute-done.6
  57.9 0.0 copy-done
  57.9 2.5 %add_convert_fusion.3 = (bf16[16,7168]{1,0:T(8,128)(2,1)}, bf16[16,7168]{1,0:T(8,128)(2,1)}, bf16[16,7168]{1,0:T(8,128)(2,1)}) fusion(bf16[64,7168]{1,0:T(8,128)(2,1)} %collective-permute-done.6, bf16[64,7168]{1,0:T(8,128)(2,1)S(1)} %collective-permute-done.4, bf16[64,7168]{1,0:T(8,128)(2,1)} %collective-permute-done, bf16[64,7168]{1,0:T(8,128)(2,1)S(1)} %copy-done), kind=kLoop, calls=%fused_computation.3 | loop fusion | flops 2752512 | bytes 3440640 | tf_op jit(solution)/shard_map/convert_element_type | solution.py:386
  60.4 1.5 %collective-permute-start.7 = (bf16[16,7168]{1,0:T(8,128)(2,1)}, bf16[16,7168]{1,0:T(8,128)(2,1)S(1)}, u32[]{:S(2)}, u32[]{:S(2)}) collective-permute-start(bf16[16,7168]{1,0:T(8,128)(2,1)} %get-tuple-element.42), channel_id=1, source_target_pairs={{0,8},{1,33},{2,10},{3,35},{4,12},{5,37},{6,14},{7,39},{8,0},{9,41... | collective-permute-start | bytes 688136 | tf_op jit(solution)/shard_map/ppermute | solution.py:323
  61.9 2.1 %collective-permute-start.8 = (bf16[16,7168]{1,0:T(8,128)(2,1)}, bf16[16,7168]{1,0:T(8,128)(2,1)}, u32[]{:S(2)}, u32[]{:S(2)}) collective-permute-start(bf16[16,7168]{1,0:T(8,128)(2,1)} %get-tuple-element.41), channel_id=1, source_target_pairs={{0,4},{1,17},{2,6},{3,19},{4,8},{5,21},{6,10},{7,23},{8,12},{9,25}... | collective-permute-start | bytes 688136 | tf_op jit(solution)/shard_map/ppermute | solution.py:323
  63.9 0.0 collective-permute-start.9
  63.9 0.2 all-to-all-done.1
  64.3 2.1 %shard_map.71 = f32[8,32,128]{2,1,0:T(8,128)S(1)} custom-call(f32[8,32,128]{2,1,0:T(8,128)S(1)} %pad_maximum_fusion.1.g_ref, f32[1024,128]{1,0:T(8,128)S(1)} %get-tuple-element.35.ad_ref), custom_call_target="tpu_custom_call" | custom-call | tf_op jit(solution)/shard_map/pallas_call | solution.py:30
  66.4 0.3 reshape.39
  66.6 0.1 copy.17
  66.7 0.9 %reshape.40 = f32[4,8,1024]{2,1,0:T(8,128)} reshape(f32[4,2,4,32,32]{4,3,2,1,0:T(8,128)S(1)} %copy.17) | data formatting | bytes 262144 | tf_op jit(solution)/shard_map/reshape | solution.py:397
  67.6 0.5 collective-permute-done.7
  68.1 0.1 collective-permute-done.8
  68.2 3.3 %collective-permute-done.9 = bf16[16,7168]{1,0:T(8,128)(2,1)} collective-permute-done((bf16[16,7168]{1,0:T(8,128)(2,1)}, bf16[16,7168]{1,0:T(8,128)(2,1)}, u32[]{:S(2)}, u32[]{:S(2)}) %collective-permute-start.9) | collective-permute-done | bytes 229408 | tf_op jit(solution)/shard_map/ppermute | solution.py:323
  71.5 2.2 %add_convert_fusion.2 = bf16[16,7168]{1,0:T(8,128)(2,1)} fusion(bf16[16,7168]{1,0:T(8,128)(2,1)} %collective-permute-done.9, bf16[16,7168]{1,0:T(8,128)(2,1)} %collective-permute-done.8, bf16[16,7168]{1,0:T(8,128)(2,1)S(1)} %collective-permute-done.7, bf16[64,7168]{1,0:T(8,128)(2,1)} %collective-permute-done.6, ...), kind=kLoop, calls=%fused_computation.2 | loop fusion | flops 1835008 | bytes 1835008 | tf_op jit(solution)/shard_map/convert_element_type | solution.py:400
  (13 shorter events, 0.2 us)
Async XLA Ops:
  2.4 17.8 %all-to-all-start = ((bf16[16,32,256]{2,1,0:T(8,128)(2,1)}), bf16[16,32,256]{2,1,0:T(8,128)(2,1)S(1)}, u32[]{:S(2)}, u32[]{:S(2)}) async-start(bf16[16,32,256]{2,1,0:T(8,128)(2,1)} %bitcast.1), calls=%async_computation | async-start | bytes 524288 | tf_op jit(solution)/shard_map/all_to_all | solution.py:328
  20.2 1.6 %collective-permute-start.1 = (bf16[512,256]{1,0:T(8,128)(2,1)S(1)}, bf16[512,256]{1,0:T(8,128)(2,1)S(1)}, u32[]{:S(2)}, u32[]{:S(2)}) collective-permute-start(bf16[512,256]{1,0:T(8,128)(2,1)S(1)} %get-tuple-element.26), channel_id=1, source_target_pairs={{0,1},{1,0},{2,3},{3,2},{4,5},{5,4},{6,7},{7,6},{8,9},{9,8},{10,11... | collective-permute-start | bytes 786440 | tf_op jit(solution)/shard_map/ppermute | solution.py:364
  21.9 10.6 %collective-permute-start.2 = (bf16[512,256]{1,0:T(8,128)(2,1)S(1)}, bf16[512,256]{1,0:T(8,128)(2,1)S(1)}, u32[]{:S(2)}, u32[]{:S(2)}) collective-permute-start(bf16[512,256]{1,0:T(8,128)(2,1)S(1)} %add_convert_fusion.1), channel_id=1, source_target_pairs={{0,2},{1,3},{2,0},{3,1},{4,6},{5,7},{6,4},{7,5},{8,10},{9,11},{10,... | collective-permute-start | bytes 786440 | tf_op jit(solution)/shard_map/ppermute | solution.py:364
  29.4 28.5 %copy-start = (bf16[64,7168]{1,0:T(8,128)(2,1)S(1)}, bf16[64,7168]{1,0:T(8,128)(2,1)}, u32[]{:S(2)}) copy-start(bf16[64,7168]{1,0:T(8,128)(2,1)} %get-tuple-element.24) | copy-start | bytes 2752516
  29.4 15.3 %collective-permute-start.4 = (bf16[64,7168]{1,0:T(8,128)(2,1)}, bf16[64,7168]{1,0:T(8,128)(2,1)S(1)}, u32[]{:S(2)}, u32[]{:S(2)}) collective-permute-start(bf16[64,7168]{1,0:T(8,128)(2,1)} %get-tuple-element.29), channel_id=1, source_target_pairs={{0,32},{1,9},{2,34},{3,11},{4,36},{5,13},{6,38},{7,15},{8,40},{9,1... | collective-permute-start | bytes 2752520 | tf_op jit(solution)/shard_map/ppermute | solution.py:323
  34.9 6.6 %collective-permute-start.3 = (f32[4,2,32,128]{3,2,1,0:T(8,128)S(1)}, f32[4,2,32,128]{3,2,1,0:T(8,128)S(1)}, u32[]{:S(2)}, u32[]{:S(2)}) collective-permute-start(f32[4,2,32,128]{3,2,1,0:T(8,128)S(1)} %slice_bitcast_fusion), channel_id=1, source_target_pairs={{0,64},{64,0},{1,65},{65,1},{2,66},{66,2},{3,67},{67,3},{4,68},{68... | collective-permute-start | bytes 393224 | tf_op jit(solution)/shard_map/ppermute | solution.py:369
  37.9 20.0 %collective-permute-start = (bf16[64,7168]{1,0:T(8,128)(2,1)}, bf16[64,7168]{1,0:T(8,128)(2,1)}, u32[]{:S(2)}, u32[]{:S(2)}) collective-permute-start(bf16[64,7168]{1,0:T(8,128)(2,1)} %get-tuple-element.25), channel_id=1, source_target_pairs={{0,16},{1,5},{2,18},{3,7},{4,20},{5,9},{6,22},{7,11},{8,24},{9,13}... | collective-permute-start | bytes 2752520 | tf_op jit(solution)/shard_map/ppermute | solution.py:323
  38.4 19.4 %collective-permute-start.6 = (bf16[64,7168]{1,0:T(8,128)(2,1)}, bf16[64,7168]{1,0:T(8,128)(2,1)}, u32[]{:S(2)}, u32[]{:S(2)}) collective-permute-start(bf16[64,7168]{1,0:T(8,128)(2,1)} %get-tuple-element.32), channel_id=1, source_target_pairs={{0,48},{1,13},{2,50},{3,15},{4,52},{5,1},{6,54},{7,3},{8,56},{9,5}... | collective-permute-start | bytes 2752520 | tf_op jit(solution)/shard_map/ppermute | solution.py:323
  44.7 13.1 %collective-permute-start.5 = (f32[2,32,128]{2,1,0:T(8,128)S(1)}, f32[2,32,128]{2,1,0:T(8,128)S(1)}, u32[]{:S(2)}, u32[]{:S(2)}) collective-permute-start(f32[2,32,128]{2,1,0:T(8,128)S(1)} %get-tuple-element.49), channel_id=1, source_target_pairs={{0,0},{4,8},{8,16},{12,24},{16,32},{20,40},{24,48},{28,56},{32,64}... | collective-permute-start | bytes 98312 | tf_op jit(solution)/shard_map/ppermute | solution.py:373
  49.5 14.7 %all-to-all-start.1 = ((bf16[16,2,32,128]{3,2,1,0:T(8,128)(2,1)}), bf16[16,2,32,128]{3,2,1,0:T(8,128)(2,1)S(1)}, u32[]{:S(2)}, u32[]{:S(2)}) async-start(bf16[16,2,32,128]{3,2,1,0:T(8,128)(2,1)} %pad_maximum_fusion), calls=%async_computation.1 | async-start | bytes 524288 | tf_op jit(solution)/shard_map/all_to_all | solution.py:382
  60.4 7.7 %collective-permute-start.7 = (bf16[16,7168]{1,0:T(8,128)(2,1)}, bf16[16,7168]{1,0:T(8,128)(2,1)S(1)}, u32[]{:S(2)}, u32[]{:S(2)}) collective-permute-start(bf16[16,7168]{1,0:T(8,128)(2,1)} %get-tuple-element.42), channel_id=1, source_target_pairs={{0,8},{1,33},{2,10},{3,35},{4,12},{5,37},{6,14},{7,39},{8,0},{9,41... | collective-permute-start | bytes 688136 | tf_op jit(solution)/shard_map/ppermute | solution.py:323
  61.9 6.3 %collective-permute-start.8 = (bf16[16,7168]{1,0:T(8,128)(2,1)}, bf16[16,7168]{1,0:T(8,128)(2,1)}, u32[]{:S(2)}, u32[]{:S(2)}) collective-permute-start(bf16[16,7168]{1,0:T(8,128)(2,1)} %get-tuple-element.41), channel_id=1, source_target_pairs={{0,4},{1,17},{2,6},{3,19},{4,8},{5,21},{6,10},{7,23},{8,12},{9,25}... | collective-permute-start | bytes 688136 | tf_op jit(solution)/shard_map/ppermute | solution.py:323
  63.9 7.5 %collective-permute-start.9 = (bf16[16,7168]{1,0:T(8,128)(2,1)}, bf16[16,7168]{1,0:T(8,128)(2,1)}, u32[]{:S(2)}, u32[]{:S(2)}) collective-permute-start(bf16[16,7168]{1,0:T(8,128)(2,1)} %get-tuple-element.40), channel_id=1, source_target_pairs={{0,12},{1,49},{2,14},{3,51},{4,0},{5,53},{6,2},{7,55},{8,4},{9,57}... | collective-permute-start | bytes 688136 | tf_op jit(solution)/shard_map/ppermute | solution.py:323

commit v6 on v5

--- a/solution.py
+++ b/solution.py
@@ -252,7 +252,7 @@
         copy.wait()
 
 
-def forward(mixed, rot, weight, tiles=7):
+def forward(mixed, rot, weight, tiles=4):
     depth, tokens = mixed.shape
     columns = weight.shape[1]
     vmem = pl.BlockSpec(memory_space=pltpu.VMEM)

time: 74 us -> 74.2 us (level)
  no operation moved by 1% of the time
where the time goes in v6:
time: 74.2 us; the launch traced here: 73.9 us
  starting transfers between devices  34.8 us (47%)
  Pallas kernels  20 us (27%)
  waiting for transfers between devices  9.24 us (12%)
  other arithmetic  5.7 us (8%)
  local copies, waits for them, and re-layouts  3.27 us (4%)
  between operations  0.84 us (1%)
    ppermute x6, starting transfers between devices, ring(): return lax.ppermute(x, ('fsdp', 'tensor'), ring_pairs(stage, s))  9.83 us
    pallas_call x1, Pallas kernels, local(): pl.pallas_call(prepare_body, out_shape=(shape((2048, LANES), BF), shape((...  9.51 us
    all_to_all x1, starting transfers between devices, local(): slots = lax.all_to_all(slots.astype(BF), 'fsdp', 0, 0, tiled=True)  8.39 us
    all_to_all x1, starting transfers between devices, local(): lax.all_to_all(activations.T.reshape(16, BLOCK, tokens), 'fsdp', 0, 0, ti...  8.26 us
    ppermute x6, waiting for transfers between devices, ring(): return lax.ppermute(x, ('fsdp', 'tensor'), ring_pairs(stage, s))  7.15 us
    pallas_call x1, Pallas kernels, forward(): pl.pallas_call(functools.partial(forward_body, tiles=tiles), out_shape=[p...  6.06 us
    pallas_call x2, Pallas kernels, call(): pl.pallas_call(body, out_shape=out_shape, in_specs=[pl.BlockSpec(memory_s...  4.42 us
    ppermute x1, starting transfers between devices, local(): lax.ppermute(grads[3], ('dp', 'fsdp'), [(e * 16 + s, s // 8 * 16 + s % 8...  3.63 us
  transfers between devices with their start and end apart: 12, of which 7 were waited for; matrix products, arithmetic and copies ran while one was open for 7% of the time, Pallas kernels for 27%

profile of v6, /device:TPU:6, one launch (start us, length us, event | category | flops | bytes accessed | tf_op | source)
XLA Modules:
  0.0 73.9 jit_solution(6525922776368467135)
XLA Ops:
  0.6 1.8 %copy.13 = bf16[256,512]{0,1:T(8,128)(2,1)} copy(bf16[256,512]{1,0:T(8,128)(2,1)} %param.5) | data formatting | bytes 524288 | tf_op args[0]
  2.4 8.3 %all-to-all-start = ((bf16[16,32,256]{2,1,0:T(8,128)(2,1)}), bf16[16,32,256]{2,1,0:T(8,128)(2,1)S(1)}, u32[]{:S(2)}, u32[]{:S(2)}) async-start(bf16[16,32,256]{2,1,0:T(8,128)(2,1)} %bitcast.1), calls=%async_computation | async-start | bytes 524288 | tf_op jit(solution)/shard_map/all_to_all | solution.py:328
  10.7 9.5 %shard_map.68 = (bf16[2048,128]{1,0:T(8,128)(2,1)S(1)}, f32[1024,128]{1,0:T(8,128)S(1)}, s32[16,128]{1,0:T(8,128)S(1)}, bf16[512,256]{1,0:T(8,128)(2,1)S(1)}) custom-call(f32[4,256,1024]{2,1,0:T(8,128)} %params.1, s32[4,8192]{1,0:T(4,128)} %perms.1, bf16[512,7168]{1,0:T(8,128)(2,1)} %weight.3, bf16[256,7168]{1,0:T(8,128)(2,1)} %cotan.1), custom_call_target="tpu_custom_call" | custom-call | tf_op jit(solution)/shard_map/pallas_call | solution.py:332
  20.2 0.0 all-to-all-done
  20.2 0.1 collective-permute-start.1
  20.3 1.5 %collective-permute-done.1 = bf16[512,256]{1,0:T(8,128)(2,1)S(1)} collective-permute-done((bf16[512,256]{1,0:T(8,128)(2,1)S(1)}, bf16[512,256]{1,0:T(8,128)(2,1)S(1)}, u32[]{:S(2)}, u32[]{:S(2)}) %collective-permute-start.1) | collective-permute-done | bytes 262176 | tf_op jit(solution)/shard_map/ppermute | solution.py:364
  21.8 0.1 add_convert_fusion.1
  21.9 1.7 %collective-permute-start.2 = (bf16[512,256]{1,0:T(8,128)(2,1)S(1)}, bf16[512,256]{1,0:T(8,128)(2,1)S(1)}, u32[]{:S(2)}, u32[]{:S(2)}) collective-permute-start(bf16[512,256]{1,0:T(8,128)(2,1)S(1)} %add_convert_fusion.1), channel_id=1, source_target_pairs={{0,2},{1,3},{2,0},{3,1},{4,6},{5,7},{6,4},{7,5},{8,10},{9,11},{10,... | collective-permute-start | bytes 786440 | tf_op jit(solution)/shard_map/ppermute | solution.py:364
  23.6 6.1 %shard_map.69 = (bf16[64,7168]{1,0:T(8,128)(2,1)}, bf16[64,7168]{1,0:T(8,128)(2,1)}, bf16[64,7168]{1,0:T(8,128)(2,1)}, bf16[64,7168]{1,0:T(8,128)(2,1)}, bf16[4,512,256]{2,1,0:T(8,128)(2,1)S(1)}) custom-call(bf16[512,256]{1,0:T(8,128)(2,1)S(1)} %bitcast.41, bf16[2048,128]{1,0:T(8,128)(2,1)S(1)} %get-tuple-element.23.rot_ref, bf16[512,7168]{1,0:T(8,128)(2,1)} %weight.3), custom_call_target="tpu_custom_call" | custom-call | tf_op jit(solution)/shard_map/pallas_call | solution.py:260
  29.6 0.0 copy-start
  29.6 3.1 %collective-permute-start.4 = (bf16[64,7168]{1,0:T(8,128)(2,1)}, bf16[64,7168]{1,0:T(8,128)(2,1)S(1)}, u32[]{:S(2)}, u32[]{:S(2)}) collective-permute-start(bf16[64,7168]{1,0:T(8,128)(2,1)} %get-tuple-element.29), channel_id=1, source_target_pairs={{0,32},{1,9},{2,34},{3,11},{4,36},{5,13},{6,38},{7,15},{8,40},{9,1... | collective-permute-start | bytes 2752520 | tf_op jit(solution)/shard_map/ppermute | solution.py:323
  32.7 0.0 collective-permute-done.2
  32.7 0.1 add_convert_fusion.up_ref
  32.8 2.3 %shard_map.70 = f32[2,4,2,32,128]{4,3,2,1,0:T(8,128)S(1)} custom-call(bf16[512,256]{1,0:T(8,128)(2,1)S(1)} %add_convert_fusion.up_ref, bf16[4,512,256]{2,1,0:T(8,128)(2,1)S(1)} %get-tuple-element.27.saved_ref, bf16[2048,128]{1,0:T(8,128)(2,1)S(1)} %get-tuple-element.23.rot_ref, s32[16,128]{1,0:T(8,128)S(1)} %get-tuple-element.28.idx_ref), custom_call_target="tpu_custom_call" | custom-call | tf_op jit(solution)/shard_map/pallas_call | solution.py:30
  35.1 3.0 %collective-permute-start.3 = (f32[4,2,32,128]{3,2,1,0:T(8,128)S(1)}, f32[4,2,32,128]{3,2,1,0:T(8,128)S(1)}, u32[]{:S(2)}, u32[]{:S(2)}) collective-permute-start(f32[4,2,32,128]{3,2,1,0:T(8,128)S(1)} %slice_bitcast_fusion), channel_id=1, source_target_pairs={{0,64},{64,0},{1,65},{65,1},{2,66},{66,2},{3,67},{67,3},{4,68},{68... | collective-permute-start | bytes 393224 | tf_op jit(solution)/shard_map/ppermute | solution.py:369
  38.1 0.6 collective-permute-start
  38.6 2.7 %collective-permute-start.6 = (bf16[64,7168]{1,0:T(8,128)(2,1)}, bf16[64,7168]{1,0:T(8,128)(2,1)}, u32[]{:S(2)}, u32[]{:S(2)}) collective-permute-start(bf16[64,7168]{1,0:T(8,128)(2,1)} %get-tuple-element.32), channel_id=1, source_target_pairs={{0,48},{1,13},{2,50},{3,15},{4,52},{5,1},{6,54},{7,3},{8,56},{9,5}... | collective-permute-start | bytes 2752520 | tf_op jit(solution)/shard_map/ppermute | solution.py:323
  41.3 0.3 collective-permute-done.3
  41.7 3.3 %collective-permute-done.4 = bf16[64,7168]{1,0:T(8,128)(2,1)S(1)} collective-permute-done((bf16[64,7168]{1,0:T(8,128)(2,1)}, bf16[64,7168]{1,0:T(8,128)(2,1)S(1)}, u32[]{:S(2)}, u32[]{:S(2)}) %collective-permute-start.4) | collective-permute-done | bytes 917536 | tf_op jit(solution)/shard_map/ppermute | solution.py:323
  44.9 3.6 %collective-permute-start.5 = (f32[2,32,128]{2,1,0:T(8,128)S(1)}, f32[2,32,128]{2,1,0:T(8,128)S(1)}, u32[]{:S(2)}, u32[]{:S(2)}) collective-permute-start(f32[2,32,128]{2,1,0:T(8,128)S(1)} %get-tuple-element.49), channel_id=1, source_target_pairs={{0,0},{4,8},{8,16},{12,24},{16,32},{20,40},{24,48},{28,56},{32,64}... | collective-permute-start | bytes 98312 | tf_op jit(solution)/shard_map/ppermute | solution.py:373
  48.6 0.1 select_n.56
  48.7 0.1 select_n.60
  48.8 0.1 maximum_convert_fusion
  48.9 0.7 pad_maximum_fusion
  49.7 8.4 %all-to-all-start.1 = ((bf16[16,2,32,128]{3,2,1,0:T(8,128)(2,1)}), bf16[16,2,32,128]{3,2,1,0:T(8,128)(2,1)S(1)}, u32[]{:S(2)}, u32[]{:S(2)}) async-start(bf16[16,2,32,128]{3,2,1,0:T(8,128)(2,1)} %pad_maximum_fusion), calls=%async_computation.1 | async-start | bytes 524288 | tf_op jit(solution)/shard_map/all_to_all | solution.py:382
  58.0 0.0 collective-permute-done
  58.1 0.0 collective-permute-done.5
  58.1 0.0 collective-permute-done.6
  58.1 0.0 copy-done
  58.1 2.5 %add_convert_fusion.3 = (bf16[16,7168]{1,0:T(8,128)(2,1)}, bf16[16,7168]{1,0:T(8,128)(2,1)}, bf16[16,7168]{1,0:T(8,128)(2,1)}) fusion(bf16[64,7168]{1,0:T(8,128)(2,1)} %collective-permute-done.6, bf16[64,7168]{1,0:T(8,128)(2,1)S(1)} %collective-permute-done.4, bf16[64,7168]{1,0:T(8,128)(2,1)} %collective-permute-done, bf16[64,7168]{1,0:T(8,128)(2,1)S(1)} %copy-done), kind=kLoop, calls=%fused_computation.3 | loop fusion | flops 2752512 | bytes 3440640 | tf_op jit(solution)/shard_map/convert_element_type | solution.py:386
  60.6 1.5 %collective-permute-start.7 = (bf16[16,7168]{1,0:T(8,128)(2,1)}, bf16[16,7168]{1,0:T(8,128)(2,1)S(1)}, u32[]{:S(2)}, u32[]{:S(2)}) collective-permute-start(bf16[16,7168]{1,0:T(8,128)(2,1)} %get-tuple-element.42), channel_id=1, source_target_pairs={{0,8},{1,33},{2,10},{3,35},{4,12},{5,37},{6,14},{7,39},{8,0},{9,41... | collective-permute-start | bytes 688136 | tf_op jit(solution)/shard_map/ppermute | solution.py:323
  62.1 2.1 %collective-permute-start.8 = (bf16[16,7168]{1,0:T(8,128)(2,1)}, bf16[16,7168]{1,0:T(8,128)(2,1)}, u32[]{:S(2)}, u32[]{:S(2)}) collective-permute-start(bf16[16,7168]{1,0:T(8,128)(2,1)} %get-tuple-element.41), channel_id=1, source_target_pairs={{0,4},{1,17},{2,6},{3,19},{4,8},{5,21},{6,10},{7,23},{8,12},{9,25}... | collective-permute-start | bytes 688136 | tf_op jit(solution)/shard_map/ppermute | solution.py:323
  64.1 0.0 collective-permute-start.9
  64.1 0.2 all-to-all-done.1
  64.5 2.1 %shard_map.71 = f32[8,32,128]{2,1,0:T(8,128)S(1)} custom-call(f32[8,32,128]{2,1,0:T(8,128)S(1)} %pad_maximum_fusion.1.g_ref, f32[1024,128]{1,0:T(8,128)S(1)} %get-tuple-element.35.ad_ref), custom_call_target="tpu_custom_call" | custom-call | tf_op jit(solution)/shard_map/pallas_call | solution.py:30
  66.6 0.3 reshape.39
  66.9 0.1 copy.17
  66.9 0.9 %reshape.40 = f32[4,8,1024]{2,1,0:T(8,128)} reshape(f32[4,2,4,32,32]{4,3,2,1,0:T(8,128)S(1)} %copy.17) | data formatting | bytes 262144 | tf_op jit(solution)/shard_map/reshape | solution.py:397
  67.8 0.5 collective-permute-done.7
  68.3 0.1 collective-permute-done.8
  68.4 3.3 %collective-permute-done.9 = bf16[16,7168]{1,0:T(8,128)(2,1)} collective-permute-done((bf16[16,7168]{1,0:T(8,128)(2,1)}, bf16[16,7168]{1,0:T(8,128)(2,1)}, u32[]{:S(2)}, u32[]{:S(2)}) %collective-permute-start.9) | collective-permute-done | bytes 229408 | tf_op jit(solution)/shard_map/ppermute | solution.py:323
  71.7 2.2 %add_convert_fusion.2 = bf16[16,7168]{1,0:T(8,128)(2,1)} fusion(bf16[16,7168]{1,0:T(8,128)(2,1)} %collective-permute-done.9, bf16[16,7168]{1,0:T(8,128)(2,1)} %collective-permute-done.8, bf16[16,7168]{1,0:T(8,128)(2,1)S(1)} %collective-permute-done.7, bf16[64,7168]{1,0:T(8,128)(2,1)} %collective-permute-done.6, ...), kind=kLoop, calls=%fused_computation.2 | loop fusion | flops 1835008 | bytes 1835008 | tf_op jit(solution)/shard_map/convert_element_type | solution.py:400
  (13 shorter events, 0.2 us)
Async XLA Ops:
  2.4 17.8 %all-to-all-start = ((bf16[16,32,256]{2,1,0:T(8,128)(2,1)}), bf16[16,32,256]{2,1,0:T(8,128)(2,1)S(1)}, u32[]{:S(2)}, u32[]{:S(2)}) async-start(bf16[16,32,256]{2,1,0:T(8,128)(2,1)} %bitcast.1), calls=%async_computation | async-start | bytes 524288 | tf_op jit(solution)/shard_map/all_to_all | solution.py:328
  20.2 1.6 %collective-permute-start.1 = (bf16[512,256]{1,0:T(8,128)(2,1)S(1)}, bf16[512,256]{1,0:T(8,128)(2,1)S(1)}, u32[]{:S(2)}, u32[]{:S(2)}) collective-permute-start(bf16[512,256]{1,0:T(8,128)(2,1)S(1)} %get-tuple-element.26), channel_id=1, source_target_pairs={{0,1},{1,0},{2,3},{3,2},{4,5},{5,4},{6,7},{7,6},{8,9},{9,8},{10,11... | collective-permute-start | bytes 786440 | tf_op jit(solution)/shard_map/ppermute | solution.py:364
  21.9 10.8 %collective-permute-start.2 = (bf16[512,256]{1,0:T(8,128)(2,1)S(1)}, bf16[512,256]{1,0:T(8,128)(2,1)S(1)}, u32[]{:S(2)}, u32[]{:S(2)}) collective-permute-start(bf16[512,256]{1,0:T(8,128)(2,1)S(1)} %add_convert_fusion.1), channel_id=1, source_target_pairs={{0,2},{1,3},{2,0},{3,1},{4,6},{5,7},{6,4},{7,5},{8,10},{9,11},{10,... | collective-permute-start | bytes 786440 | tf_op jit(solution)/shard_map/ppermute | solution.py:364
  29.6 28.5 %copy-start = (bf16[64,7168]{1,0:T(8,128)(2,1)S(1)}, bf16[64,7168]{1,0:T(8,128)(2,1)}, u32[]{:S(2)}) copy-start(bf16[64,7168]{1,0:T(8,128)(2,1)} %get-tuple-element.24) | copy-start | bytes 2752516
  29.6 15.3 %collective-permute-start.4 = (bf16[64,7168]{1,0:T(8,128)(2,1)}, bf16[64,7168]{1,0:T(8,128)(2,1)S(1)}, u32[]{:S(2)}, u32[]{:S(2)}) collective-permute-start(bf16[64,7168]{1,0:T(8,128)(2,1)} %get-tuple-element.29), channel_id=1, source_target_pairs={{0,32},{1,9},{2,34},{3,11},{4,36},{5,13},{6,38},{7,15},{8,40},{9,1... | collective-permute-start | bytes 2752520 | tf_op jit(solution)/shard_map/ppermute | solution.py:323
  35.1 6.6 %collective-permute-start.3 = (f32[4,2,32,128]{3,2,1,0:T(8,128)S(1)}, f32[4,2,32,128]{3,2,1,0:T(8,128)S(1)}, u32[]{:S(2)}, u32[]{:S(2)}) collective-permute-start(f32[4,2,32,128]{3,2,1,0:T(8,128)S(1)} %slice_bitcast_fusion), channel_id=1, source_target_pairs={{0,64},{64,0},{1,65},{65,1},{2,66},{66,2},{3,67},{67,3},{4,68},{68... | collective-permute-start | bytes 393224 | tf_op jit(solution)/shard_map/ppermute | solution.py:369
  38.1 20.0 %collective-permute-start = (bf16[64,7168]{1,0:T(8,128)(2,1)}, bf16[64,7168]{1,0:T(8,128)(2,1)}, u32[]{:S(2)}, u32[]{:S(2)}) collective-permute-start(bf16[64,7168]{1,0:T(8,128)(2,1)} %get-tuple-element.25), channel_id=1, source_target_pairs={{0,16},{1,5},{2,18},{3,7},{4,20},{5,9},{6,22},{7,11},{8,24},{9,13}... | collective-permute-start | bytes 2752520 | tf_op jit(solution)/shard_map/ppermute | solution.py:323
  38.6 19.4 %collective-permute-start.6 = (bf16[64,7168]{1,0:T(8,128)(2,1)}, bf16[64,7168]{1,0:T(8,128)(2,1)}, u32[]{:S(2)}, u32[]{:S(2)}) collective-permute-start(bf16[64,7168]{1,0:T(8,128)(2,1)} %get-tuple-element.32), channel_id=1, source_target_pairs={{0,48},{1,13},{2,50},{3,15},{4,52},{5,1},{6,54},{7,3},{8,56},{9,5}... | collective-permute-start | bytes 2752520 | tf_op jit(solution)/shard_map/ppermute | solution.py:323
  44.9 13.1 %collective-permute-start.5 = (f32[2,32,128]{2,1,0:T(8,128)S(1)}, f32[2,32,128]{2,1,0:T(8,128)S(1)}, u32[]{:S(2)}, u32[]{:S(2)}) collective-permute-start(f32[2,32,128]{2,1,0:T(8,128)S(1)} %get-tuple-element.49), channel_id=1, source_target_pairs={{0,0},{4,8},{8,16},{12,24},{16,32},{20,40},{24,48},{28,56},{32,64}... | collective-permute-start | bytes 98312 | tf_op jit(solution)/shard_map/ppermute | solution.py:373
  49.7 14.7 %all-to-all-start.1 = ((bf16[16,2,32,128]{3,2,1,0:T(8,128)(2,1)}), bf16[16,2,32,128]{3,2,1,0:T(8,128)(2,1)S(1)}, u32[]{:S(2)}, u32[]{:S(2)}) async-start(bf16[16,2,32,128]{3,2,1,0:T(8,128)(2,1)} %pad_maximum_fusion), calls=%async_computation.1 | async-start | bytes 524288 | tf_op jit(solution)/shard_map/all_to_all | solution.py:382
  60.6 7.7 %collective-permute-start.7 = (bf16[16,7168]{1,0:T(8,128)(2,1)}, bf16[16,7168]{1,0:T(8,128)(2,1)S(1)}, u32[]{:S(2)}, u32[]{:S(2)}) collective-permute-start(bf16[16,7168]{1,0:T(8,128)(2,1)} %get-tuple-element.42), channel_id=1, source_target_pairs={{0,8},{1,33},{2,10},{3,35},{4,12},{5,37},{6,14},{7,39},{8,0},{9,41... | collective-permute-start | bytes 688136 | tf_op jit(solution)/shard_map/ppermute | solution.py:323
  62.1 6.3 %collective-permute-start.8 = (bf16[16,7168]{1,0:T(8,128)(2,1)}, bf16[16,7168]{1,0:T(8,128)(2,1)}, u32[]{:S(2)}, u32[]{:S(2)}) collective-permute-start(bf16[16,7168]{1,0:T(8,128)(2,1)} %get-tuple-element.41), channel_id=1, source_target_pairs={{0,4},{1,17},{2,6},{3,19},{4,8},{5,21},{6,10},{7,23},{8,12},{9,25}... | collective-permute-start | bytes 688136 | tf_op jit(solution)/shard_map/ppermute | solution.py:323
  64.1 7.5 %collective-permute-start.9 = (bf16[16,7168]{1,0:T(8,128)(2,1)}, bf16[16,7168]{1,0:T(8,128)(2,1)}, u32[]{:S(2)}, u32[]{:S(2)}) collective-permute-start(bf16[16,7168]{1,0:T(8,128)(2,1)} %get-tuple-element.40), channel_id=1, source_target_pairs={{0,12},{1,49},{2,14},{3,51},{4,0},{5,53},{6,2},{7,55},{8,4},{9,57}... | collective-permute-start | bytes 688136 | tf_op jit(solution)/shard_map/ppermute | solution.py:323
